TPU v7x, 512 devices: a whole 4x8x8 slice. The times are simulated.
512 devices in a mesh: segment: 4 (over x), dp: 8 (over y), mp: 16 (over z, core).
Axes of the slice: x: 4, y: 8, z: 8, core: 2. Of those that a mesh axis runs over, the one named last changes fastest.
Arguments:
- pending_inputs: bfloat16 [4, 8192, 4096], P('segment', ('dp', 'mp')), may hold values from -6 to 6
- arriving_samples: bfloat16 [8192, 4096], P(('dp', 'mp')), may hold values from -6 to 6
- layer_rms_gain: float32 [4, 4096], P('segment'), may hold values from 0.25 to 1.75
- scorer_vectors: float32 [4, 4096], P('segment'), may hold values from -0.09375 to 0.09375
- gating_matrix: bfloat16 [4, 4096, 14336], P('segment', 'dp', 'mp'), may hold values from -0.09375 to 0.09375
- expansion_matrix: bfloat16 [4, 4096, 14336], P('segment', 'dp', 'mp'), may hold values from -0.09375 to 0.09375
- contraction_matrix: bfloat16 [4, 14336, 4096], P('segment', 'mp', 'dp'), may hold values from -0.046875 to 0.046875
- dispatch_lists: int32 [2, 4, 128, 8], P(None, 'segment', ('dp', 'mp')), may hold values from -1 to 63, as said below
Outputs:
- first_out: bfloat16 [4, 8192, 4096], P('segment', ('dp', 'mp'))
- second_out: bfloat16 [4, 8192, 4096], P('segment', ('dp', 'mp'))
Inputs may be any that keep to these rules, and one draw needn't show every extreme that they name: `dispatch_lists`: in each list of 8 slots the used slots come first and name distinct rows of the block; the other slots hold -1. Some block of every group of 8 blocks that share an mp index uses all 8 slots, and every such group (same tick and section) uses exactly 32 slots together.
All inputs are finite; a program needn't handle non-finite values.
Results may differ from a plain program's by a relative error of at most 0.0065.
Values may be sent and summed in bfloat16 or wider, within the bound.
No kernel may reach another device: no remote copies, remote signals or barrier semaphores. Data moves between devices by JAX's collectives and lax.ppermute only.
A program may use at most 64 MiB of HBM per device.

v0:
```python
import jax
import jax.numpy as jnp
from jax import lax
from jax.sharding import PartitionSpec as P


def from_behind(value, axis, steps):
    count = lax.axis_size(axis)
    initial, last = (max(0, -steps), min(count, count - steps))
    return lax.ppermute(value, axis, [(source, source + steps) for source in range(initial, last)])


def selection(flags, dense_rows):
    used_slots = (flags[:, 0] > 0).astype(jnp.int32)
    dense_place = jnp.cumsum(used_slots) - 1
    targets = jnp.arange(dense_rows, dtype=jnp.int32)[:, None]
    return ((dense_place[None, :] == targets) & (used_slots[None, :] > 0)).astype(jnp.bfloat16)


def layer_tile(section_in, route_row, gain, router_vec, w_gate_local, w_up_local, w_down_local):
    width_parts = lax.axis_size("dp")
    slot_count = route_row.shape[0]
    is_live = route_row >= 0
    safe_rows = jnp.where(is_live, route_row, 0)
    picked = jnp.take(section_in, safe_rows, axis=0)
    values = picked.astype(jnp.float32)
    inv_rms = lax.rsqrt(jnp.mean(values * values, axis=-1, keepdims=True) + 1e-05)
    normed = jnp.where(is_live[:, None], values * inv_rms * gain, 0.0).astype(jnp.bfloat16)
    live_flags = jnp.broadcast_to(is_live[:, None], (slot_count, width_parts)).astype(jnp.bfloat16)
    slot_rows, flag_col = (
        lax.all_to_all(normed, "dp", split_axis=1, concat_axis=0, tiled=True),
        lax.all_to_all(live_flags, "dp", split_axis=1, concat_axis=0, tiled=True),
    )
    group_rows = width_parts * slot_count // 2
    selector = selection(flag_col, group_rows)
    all_rows, all_flags = (
        lax.all_gather(slot_rows, "mp", axis=0, tiled=True),
        lax.all_gather(flag_col, "mp", axis=0, tiled=True),
    )
    wide_selector = selection(all_flags, lax.axis_size("mp") * group_rows)
    gathered = jnp.dot(wide_selector, all_rows, preferred_element_type=jnp.float32).astype(
        jnp.bfloat16
    )
    joined = jnp.concatenate([w_gate_local, w_up_local], axis=1)
    hidden_cols = w_gate_local.shape[1]
    summed = lax.psum_scatter(
        jnp.dot(gathered, joined, preferred_element_type=jnp.float32).astype(jnp.bfloat16),
        "dp",
        scatter_dimension=0,
        tiled=True,
    ).astype(jnp.float32)
    hidden = (jax.nn.silu(summed[:, :hidden_cols]) * summed[:, hidden_cols:]).astype(jnp.bfloat16)
    all_hidden = lax.all_gather(hidden, "dp", axis=0, tiled=True)
    partial_block = jnp.dot(all_hidden, w_down_local, preferred_element_type=jnp.float32)
    full_sum = lax.psum(partial_block.astype(jnp.bfloat16), "mp").astype(jnp.float32)
    block_out = lax.dynamic_slice_in_dim(full_sum, lax.axis_index("mp") * group_rows, group_rows, 0)
    block_out = block_out.astype(jnp.bfloat16)
    spread_out = jnp.dot(selector.T, block_out, preferred_element_type=jnp.float32).astype(
        jnp.bfloat16
    )
    returned = lax.all_to_all(spread_out, "dp", split_axis=0, concat_axis=1, tiled=True)
    weight = jax.nn.sigmoid(jnp.dot(values, router_vec, precision=lax.Precision.HIGHEST))
    updated = (values + weight[:, None] * returned.astype(jnp.float32)).astype(jnp.bfloat16)
    target = jnp.where(is_live, route_row, section_in.shape[0])
    return section_in.at[target].set(updated, mode="drop")


def local(
    pending_inputs,
    arriving_samples,
    layer_rms_gain,
    scorer_vectors,
    gating_matrix,
    expansion_matrix,
    contraction_matrix,
    dispatch_lists,
):
    first_local = layer_tile(
        pending_inputs[0],
        dispatch_lists[0, 0, 0],
        layer_rms_gain[0],
        scorer_vectors[0],
        gating_matrix[0],
        expansion_matrix[0],
        contraction_matrix[0],
    )
    passed = from_behind(first_local, "segment", 1)
    second_in = jnp.where(lax.axis_index("segment") == 0, arriving_samples, passed)
    second_local = layer_tile(
        second_in,
        dispatch_lists[1, 0, 0],
        layer_rms_gain[0],
        scorer_vectors[0],
        gating_matrix[0],
        expansion_matrix[0],
        contraction_matrix[0],
    )
    return (first_local[None], second_local[None])


def solution(mesh):
    return jax.shard_map(
        local,
        mesh=mesh,
        in_specs=(
            P("segment", ("dp", "mp"), None),
            P(("dp", "mp"), None),
            P("segment", None),
            P("segment", None),
            P("segment", "dp", "mp"),
            P("segment", "dp", "mp"),
            P("segment", "mp", "dp"),
            P(None, "segment", ("dp", "mp"), None),
        ),
        out_specs=(P("segment", ("dp", "mp"), None), P("segment", ("dp", "mp"), None)),
        check_vma=False,
    )
```

profile of v0, /device:TPU:6, one launch (start us, length us, event | category | flops | bytes accessed | tf_op | source)
XLA Modules:
  0.0 563.6 jit_solution(5471080146650865949)
XLA Ops:
  10.7 15.4 %all_to_all.90 = bf16[8,8,512]{2,0,1:T(8,128)(2,1)} all-to-all(bf16[8,8,512]{2,0,1:T(8,128)(2,1)S(1)} %bitcast.119), channel_id=1, replica_groups=mesh['segment'=4,'dp'=8,'mp'=16] {'dp'}, dimensions={1} | all-to-all | bytes 131072 | tf_op jit(solution)/shard_map/all_to_all | solution.py:31
  26.7 3.3 all-to-all-start
  32.0 5.6 all-to-all-done
  38.2 3.3 all-to-all-start.3
  41.6 7.4 %all-to-all-done.3 = bf16[8,8,1]{0,2,1:T(2,128)(2,1)S(1)} async-done(((bf16[8,8,1]{0,2,1:T(2,128)(2,1)}), bf16[8,8,1]{0,2,1:T(2,128)(2,1)S(1)}, u32[]{:S(2)}, u32[]{:S(2)}) %all-to-all-start.3) | async-done | bytes 160 | tf_op jit(solution)/shard_map/all_to_all | solution.py:32
  49.6 29.4 %all-reduce.2 = (bf16[1024]{0:T(1024)(128)(2,1)S(1)}, bf16[1024]{0:T(1024)(128)(2,1)S(1)}) all-reduce(bf16[1024]{0:T(1024)(128)(2,1)S(1)} %dynamic-update-slice, bf16[1024]{0:T(1024)(128)(2,1)S(1)} %dynamic-update-slice.1), channel_id=1, replica_groups=mesh['segment'=4,'dp'=8,'mp'=16] {'mp'}, use_global_device_ids=true, to_apply=%add | all-reduce | flops 2048 | bytes 8192
  79.6 4.6 convolution_convert_fusion.1
  85.2 37.4 %reduce-scatter.3.cloned.1.call-done = bf16[64,1792]{1,0:T(8,128)(2,1)} async-done(((bf16[512,1792]{1,0:T(8,128)(2,1)}), bf16[64,1792]{1,0:T(8,128)(2,1)}) %reduce-scatter.3.cloned.1.call-update) | async-done | bytes 229392 | tf_op jit(solution)/shard_map/reduce_scatter | solution.py:46
  123.6 26.4 %all_gather.20 = bf16[512,896]{1,0:T(8,128)(2,1)S(1)} all-gather(bf16[64,896]{1,0:T(8,128)(2,1)S(1)} %fusion.33), channel_id=1, replica_groups=mesh['segment'=4,'dp'=8,'mp'=16] {'dp'}, dimensions={0}, use_global_device_ids=true | all-gather | bytes 1032192 | tf_op jit(solution)/shard_map/all_gather | solution.py:53
  150.0 1.5 convolution_convert_fusion.3
  152.0 114.8 %all-reduce.6.cloned.1.call-done = bf16[512,512]{1,0:T(8,128)(2,1)} async-done(((bf16[512,512]{1,0:T(8,128)(2,1)}), bf16[512,512]{1,0:T(8,128)(2,1)}) %all-reduce.6.cloned.1.call-update) | async-done | bytes 524304 | tf_op jit(solution)/shard_map/psum | solution.py:55
  266.8 1.6 fusion.12
  268.4 6.7 %all-to-all-start.2 = ((bf16[8,8,512]{2,1,0:T(8,128)(2,1)}), bf16[8,8,512]{2,1,0:T(8,128)(2,1)S(1)}, u32[]{:S(2)}, u32[]{:S(2)}) async-start(bf16[8,8,512]{2,1,0:T(8,128)(2,1)} %fusion.12), calls=%async_computation.3 | async-start | bytes 131072 | tf_op jit(solution)/shard_map/all_to_all | solution.py:61
  275.2 8.3 %all-to-all-done.2 = bf16[8,8,512]{2,1,0:T(8,128)(2,1)S(1)} async-done(((bf16[8,8,512]{2,1,0:T(8,128)(2,1)}), bf16[8,8,512]{2,1,0:T(8,128)(2,1)S(1)}, u32[]{:S(2)}, u32[]{:S(2)}) %all-to-all-start.2) | async-done | bytes 65568 | tf_op jit(solution)/shard_map/all_to_all | solution.py:61
  286.0 12.8 %collective-permute-done = bf16[64,4096]{1,0:T(8,128)(2,1)S(1)} collective-permute-done((bf16[64,4096]{1,0:T(8,128)(2,1)S(1)}, bf16[64,4096]{1,0:T(8,128)(2,1)S(1)}, u32[]{:S(2)}, u32[]{:S(2)}) %collective-permute-start) | collective-permute-done | bytes 524320 | tf_op jit(solution)/shard_map/ppermute | solution.py:10
  299.7 11.4 %all_to_all.91 = bf16[8,8,512]{2,0,1:T(8,128)(2,1)} all-to-all(bf16[8,8,512]{2,0,1:T(8,128)(2,1)S(1)} %bitcast.120), channel_id=1, replica_groups=mesh['segment'=4,'dp'=8,'mp'=16] {'dp'}, dimensions={1} | all-to-all | bytes 131072 | tf_op jit(solution)/shard_map/all_to_all | solution.py:31
  311.8 35.2 %all-gather.5.cloned.1.call-done = bf16[1024,512]{1,0:T(8,128)(2,1)} async-done(((bf16[64,512]{1,0:T(8,128)(2,1)}), bf16[1024,512]{1,0:T(8,128)(2,1)}) %all-gather.5.cloned.1.call-update) | async-done | bytes 1048592 | tf_op jit(solution)/shard_map/all_gather | solution.py:37
  347.0 4.9 convolution_convert_fusion
  351.9 42.1 %reduce-scatter.5.cloned.1.call-done = bf16[64,1792]{1,0:T(8,128)(2,1)} async-done(((bf16[512,1792]{1,0:T(8,128)(2,1)}), bf16[64,1792]{1,0:T(8,128)(2,1)}) %reduce-scatter.5.cloned.1.call-update) | async-done | bytes 229392 | tf_op jit(solution)/shard_map/reduce_scatter | solution.py:46
  395.1 26.2 %all_gather.23 = bf16[512,896]{1,0:T(8,128)(2,1)S(1)} all-gather(bf16[64,896]{1,0:T(8,128)(2,1)S(1)} %fusion.32), channel_id=1, replica_groups=mesh['segment'=4,'dp'=8,'mp'=16] {'dp'}, dimensions={0}, use_global_device_ids=true | all-gather | bytes 1032192 | tf_op jit(solution)/shard_map/all_gather | solution.py:53
  423.3 114.9 %all-reduce.8.cloned.1.call-done = bf16[512,512]{1,0:T(8,128)(2,1)} async-done(((bf16[512,512]{1,0:T(8,128)(2,1)}), bf16[512,512]{1,0:T(8,128)(2,1)}) %all-reduce.8.cloned.1.call-update) | async-done | bytes 524304 | tf_op jit(solution)/shard_map/psum | solution.py:55
  538.2 1.6 fusion.13
  539.8 6.7 %all-to-all-start.5 = ((bf16[8,8,512]{2,1,0:T(8,128)(2,1)}), bf16[8,8,512]{2,1,0:T(8,128)(2,1)S(1)}, u32[]{:S(2)}, u32[]{:S(2)}) async-start(bf16[8,8,512]{2,1,0:T(8,128)(2,1)} %fusion.13), calls=%async_computation.7 | async-start | bytes 131072 | tf_op jit(solution)/shard_map/all_to_all | solution.py:61
  546.8 8.1 %all-to-all-done.5 = bf16[8,8,512]{2,1,0:T(8,128)(2,1)S(1)} async-done(((bf16[8,8,512]{2,1,0:T(8,128)(2,1)}), bf16[8,8,512]{2,1,0:T(8,128)(2,1)S(1)}, u32[]{:S(2)}, u32[]{:S(2)}) %all-to-all-start.5) | async-done | bytes 65568 | tf_op jit(solution)/shard_map/all_to_all | solution.py:61
  (89 shorter events, 19.0 us)
Async XLA Ops:
  7.2 142.8 %copy-start = (bf16[1,896,512]{2,1,0:T(8,128)(2,1)S(1)}, bf16[1,896,512]{2,1,0:T(8,128)(2,1)}, u32[]{:S(2)}) copy-start(bf16[1,896,512]{2,1,0:T(8,128)(2,1)} %param.16) | copy-start | bytes 2752516
  7.2 72.4 %copy-start.6 = (bf16[1,512,896]{2,1,0:T(8,128)(2,1)S(1)}, bf16[1,512,896]{2,1,0:T(8,128)(2,1)}, u32[]{:S(2)}) copy-start(bf16[1,512,896]{2,1,0:T(8,128)(2,1)} %param.15) | copy-start | bytes 2752516
  7.2 72.4 %all-gather.3.cloned.1.call-start = ((), (), s32[]{:S(2)}) async-start(), calls=%async_computation.8 | async-start | bytes 1114112 | tf_op jit(solution)/shard_map/all_gather | solution.py:37
  26.7 10.8 %all-to-all-start = ((bf16[8,8,1]{0,2,1:T(2,128)(2,1)}), bf16[8,8,1]{0,2,1:T(2,128)(2,1)S(1)}, u32[]{:S(2)}, u32[]{:S(2)}) async-start(bf16[8,8,1]{0,2,1:T(2,128)(2,1)} %broadcast_in_dim.43), calls=%async_computation | async-start | bytes 8192 | tf_op jit(solution)/shard_map/all_to_all | solution.py:32
  38.2 10.8 %all-to-all-start.3 = ((bf16[8,8,1]{0,2,1:T(2,128)(2,1)}), bf16[8,8,1]{0,2,1:T(2,128)(2,1)S(1)}, u32[]{:S(2)}, u32[]{:S(2)}) async-start(bf16[8,8,1]{0,2,1:T(2,128)(2,1)} %broadcast_in_dim.77), calls=%async_computation.4 | async-start | bytes 8192 | tf_op jit(solution)/shard_map/all_to_all | solution.py:32
  41.5 81.1 %reduce-scatter.3.cloned.1.call-start = ((), (), s32[]{:S(2)}) async-start(), calls=%async_computation.9 | async-start | bytes 2064384 | tf_op jit(solution)/shard_map/reduce_scatter | solution.py:46
  84.2 0.7 copy-start.7
  84.2 182.6 %all-reduce.6.cloned.1.call-start = ((), (), s32[]{:S(2)}) async-start(), calls=%async_computation.10 | async-start | bytes 1048576 | tf_op jit(solution)/shard_map/psum | solution.py:55
  150.0 125.2 %copy-start.5 = (s32[2,1,1,8]{3,2,1,0:T(1,128)S(1)}, s32[2,1,1,8]{3,2,1,0:T(1,128)}, u32[]{:S(2)}) copy-start(s32[2,1,1,8]{3,2,1,0:T(1,128)} %param.17) | copy-start | bytes 196
  150.0 148.8 %copy-start.3 = (bf16[64,4096]{1,0:T(8,128)(2,1)S(1)}, bf16[64,4096]{1,0:T(8,128)(2,1)}, u32[]{:S(2)}) copy-start(bf16[64,4096]{1,0:T(8,128)(2,1)} %param.11) | copy-start | bytes 1572868
  151.5 148.1 %copy-start.4 = (f32[1,4096]{1,0:T(1,128)S(1)}, f32[1,4096]{1,0:T(1,128)}, u32[]{:S(2)}) copy-start(f32[1,4096]{1,0:T(1,128)} %param.12) | copy-start | bytes 49156
  268.4 15.1 %all-to-all-start.2 = ((bf16[8,8,512]{2,1,0:T(8,128)(2,1)}), bf16[8,8,512]{2,1,0:T(8,128)(2,1)S(1)}, u32[]{:S(2)}, u32[]{:S(2)}) async-start(bf16[8,8,512]{2,1,0:T(8,128)(2,1)} %fusion.12), calls=%async_computation.3 | async-start | bytes 131072 | tf_op jit(solution)/shard_map/all_to_all | solution.py:61
  275.1 71.9 %all-gather.5.cloned.1.call-start = ((), (), s32[]{:S(2)}) async-start(), calls=%async_computation.11 | async-start | bytes 1114112 | tf_op jit(solution)/shard_map/all_gather | solution.py:37
  284.6 67.2 %copy-start.1 = (bf16[64,4096]{1,0:T(8,128)(2,1)}, bf16[64,4096]{1,0:T(8,128)(2,1)S(1)}, u32[]{:S(2)}) copy-start(bf16[64,4096]{1,0:T(8,128)(2,1)S(1)} %scatter_custom_fusion) | copy-start | bytes 1572868
  284.7 14.1 %collective-permute-start = (bf16[64,4096]{1,0:T(8,128)(2,1)S(1)}, bf16[64,4096]{1,0:T(8,128)(2,1)S(1)}, u32[]{:S(2)}, u32[]{:S(2)}) collective-permute-start(bf16[64,4096]{1,0:T(8,128)(2,1)S(1)} %scatter_custom_fusion), channel_id=1, source_target_pairs={{0,128},{128,256},{256,384},{1,129},{129,257},{257,385},{2,130},{1... | collective-permute-start | bytes 1572872 | tf_op jit(solution)/shard_map/ppermute | solution.py:10
  311.2 82.9 %reduce-scatter.5.cloned.1.call-start = ((), (), s32[]{:S(2)}) async-start(), calls=%async_computation.12 | async-start | bytes 2064384 | tf_op jit(solution)/shard_map/reduce_scatter | solution.py:46
  351.9 186.3 %all-reduce.8.cloned.1.call-start = ((), (), s32[]{:S(2)}) async-start(), calls=%async_computation.13 | async-start | bytes 1048576 | tf_op jit(solution)/shard_map/psum | solution.py:55
  539.8 15.1 %all-to-all-start.5 = ((bf16[8,8,512]{2,1,0:T(8,128)(2,1)}), bf16[8,8,512]{2,1,0:T(8,128)(2,1)S(1)}, u32[]{:S(2)}, u32[]{:S(2)}) async-start(bf16[8,8,512]{2,1,0:T(8,128)(2,1)} %fusion.13), calls=%async_computation.7 | async-start | bytes 131072 | tf_op jit(solution)/shard_map/all_to_all | solution.py:61
  556.0 0.8 copy-start.2
Sparse Core Ops, SparseCore 0:
  26.3 41.3 all-gather.2
  84.3 38.1 reduce-scatter.2
  151.6 115.1 all-reduce.5
  311.3 35.6 all-gather.4
  352.0 42.0 reduce-scatter.4
  423.0 115.0 all-reduce.7
where the time goes:
time: 565 us; the launch traced here: 564 us
  waiting for transfers between devices  387 us (68%)
  blocking collectives  109 us (19%)
  starting transfers between devices  21.6 us (4%)
  matrix products  16.2 us (3%)
  between operations  15 us (3%)
  other arithmetic  7.69 us (1%)
  local copies, waits for them, and re-layouts  7.64 us (1%)
    psum x2, waiting for transfers between devices, layer_tile(): lax.psum(partial_block.astype(jnp.bfloat16), 'mp').astype(jnp.float32)  230 us
    reduce_scatter x2, waiting for transfers between devices, layer_tile(): lax.psum_scatter(jnp.dot(gathered, joined, preferred_element_type=jnp.flo...  79.5 us
    all_gather x2, blocking collectives, layer_tile(): all_hidden = lax.all_gather(hidden, 'dp', axis=0, tiled=True)  52.6 us
    all_gather x2, waiting for transfers between devices, layer_tile(): lax.all_gather(slot_rows, 'mp', axis=0, tiled=True)  35.2 us
    unnamed x1, blocking collectives  29.4 us
    all_to_all x2, blocking collectives, layer_tile(): lax.all_to_all(normed, 'dp', split_axis=1, concat_axis=0, tiled=True)  26.8 us
    all_to_all x2, waiting for transfers between devices, layer_tile(): lax.all_to_all(spread_out, 'dp', split_axis=0, concat_axis=1, tiled=True)  16.4 us
    all_to_all x2, starting transfers between devices, layer_tile(): lax.all_to_all(spread_out, 'dp', split_axis=0, concat_axis=1, tiled=True)  13.5 us
  transfers between devices with their start and end apart: 11, of which 10 were waited for; matrix products, arithmetic and copies ran while one was open for 1% of the time, Pallas kernels for 0%

commit v1 on v0

v1 whole, which is shorter than its diff:
```python
import jax
import jax.numpy as jnp
from jax import lax
from jax.sharding import Mesh, PartitionSpec as P

BF = jnp.bfloat16
F32 = jnp.float32
DP = ("q", "h")
PLANE = ("h", "z")


def parts3(x):
    hi = x.astype(BF)
    r = x - hi.astype(F32)
    mid = r.astype(BF)
    lo = (r - mid.astype(F32)).astype(BF)
    return [hi, mid, lo]


def lanes(cols, n):
    at = jnp.arange(128, dtype=jnp.int32)[None, :]
    out = jnp.zeros((n, 128), BF)
    for i, col in enumerate(cols):
        out = jnp.where(at == i, col[:, None], out)
    return out


def compaction(live, rows):
    n = live.shape[0]
    i = jnp.arange(n, dtype=jnp.int32)
    place = jnp.sum(jnp.where((i[None, :] < i[:, None]) & live[None, :], 1, 0), axis=1)
    return ((place[None, :] == jnp.arange(rows, dtype=jnp.int32)[:, None]) & live[None, :]).astype(BF)


def pick(onehot, x):
    return jnp.dot(onehot, x, preferred_element_type=F32).astype(BF)


def cross(w):
    w = lax.ppermute(w, ("h", "core"), [(0, 0), (3, 3), (1, 2), (2, 1)])
    return w, lax.ppermute(w, "core", [(0, 1), (1, 0)])


def tick(v, gains, scorers, wg, wu, wd, z, core):
    rows = v.shape[0]
    n_z = lax.axis_size("z")
    n_q = lax.axis_size("q")
    width = v.shape[1]
    g = lax.all_to_all(
        jnp.broadcast_to(v[None], (2 * n_z, rows, width)), PLANE, 0, 0, tiled=True
    ).reshape(2, n_z * rows, width)
    ss = 0.0
    dot = 0.0
    gate = 0.0
    up = 0.0
    for k in range(2):
        vk = lax.dynamic_index_in_dim(g, core ^ k, 0, keepdims=False).astype(F32)
        ss = ss + jnp.sum(vk * vk, axis=1)
        dot = dot + jnp.sum(vk * scorers[k], axis=1)
        x = (vk * gains[k]).astype(BF)
        gate = gate + jnp.dot(x, wg[k], preferred_element_type=F32)
        up = up + jnp.dot(x, wu[k], preferred_element_type=F32)
    everyone = n_z * rows
    extra = lanes(parts3(ss) + parts3(dot), everyone)
    part = jnp.concatenate([gate.astype(BF), up.astype(BF), extra], axis=1)
    units = gate.shape[1]
    part = lax.all_to_all(part.reshape(n_q, everyone // n_q, -1), "q", 0, 0, tiled=True)
    total = jnp.sum(part.astype(F32), axis=0)
    ext = total[:, 2 * units :]
    inv = lax.rsqrt((ext[:, 0] + ext[:, 1] + ext[:, 2]) / (8 * width) + 1e-05)[:, None]
    weight = jax.nn.sigmoid(ext[:, 3] + ext[:, 4] + ext[:, 5])
    hidden = (jax.nn.silu(total[:, :units] * inv) * (total[:, units : 2 * units] * inv)).astype(BF)
    hidden = jnp.concatenate([hidden, lanes(parts3(weight), everyone // n_q)], axis=1)
    hidden = lax.all_gather(hidden, "q", axis=0, tiled=True)
    own = lax.dynamic_slice_in_dim(hidden[:, units:], z * rows, rows, 0).astype(F32)
    weight = own[:, 0] + own[:, 1] + own[:, 2]
    hidden = hidden[:, :units]
    outs = [jnp.dot(hidden, wd[k], preferred_element_type=F32).astype(BF) for k in range(2)]
    out = jnp.stack([jnp.where(core == 0, outs[0], outs[1]), jnp.where(core == 0, outs[1], outs[0])])
    out = lax.all_to_all(out.reshape(2 * n_z, rows, width), PLANE, 0, 0, tiled=True)
    block_out = jnp.sum(out.astype(F32), axis=0).astype(BF).astype(F32)
    return (v.astype(F32) + weight[:, None] * block_out).astype(BF)


def local(pending, arriving, gain, scorer, w_gate, w_up, w_down, lists):
    pending = pending[0]
    n_seg = lax.axis_size("segment")
    n_dp = lax.axis_size("q") * 2
    s = lax.axis_index("segment")
    q = lax.axis_index("q")
    z = lax.axis_index("z")
    core = lax.axis_index("core")
    n_rows, width = pending.shape
    cut = width // n_dp
    cap = lists.shape[-1]
    compact = n_dp * cap // 2
    e1 = lists[0, 0, 0]
    e2 = lists[1, 0, 0]
    e2_next = lax.ppermute(e2, "segment", [(i, (i - 1) % n_seg) for i in range(n_seg)])
    v1 = jnp.take(pending, jnp.maximum(e1, 0), axis=0)
    safe = jnp.maximum(e2_next, 0)
    b2 = jnp.where(s == n_seg - 1, jnp.take(arriving, safe, axis=0), jnp.take(pending, safe, axis=0))
    both = jnp.concatenate([v1, b2], axis=0).reshape(2 * cap, n_dp, cut).transpose(1, 0, 2)
    codes = lanes([jnp.concatenate([e1, e2_next]).astype(BF)], 2 * cap)
    both = jnp.concatenate([both, jnp.broadcast_to(codes[None], (n_dp, 2 * cap, 128))], axis=2)
    got = lax.all_to_all(both, DP, 0, 0, tiled=True)
    slots1 = got[:, :cap].reshape(n_dp * cap, -1)
    slots2 = got[:, cap:].reshape(n_dp * cap, -1)
    c1 = slots1[:, cut].astype(jnp.int32)
    c2 = slots2[:, cut].astype(jnp.int32)
    block = jnp.arange(n_dp * cap, dtype=jnp.int32) // cap
    comp1 = compaction(c1 >= 0, compact)
    comp2 = compaction(c2 >= 0, compact)
    same = (c2[:, None] == c1[None, :]) & (c1[None, :] >= 0) & (block[:, None] == block[None, :])
    same = (same & (s < n_seg - 1)).astype(BF)
    hit = pick(pick(comp2, same), comp1.T)
    has = jnp.sum(hit.astype(F32), axis=1)[:, None] > 0
    v1c = pick(comp1, slots1[:, :cut])
    b2c = pick(comp2, slots2[:, :cut])

    wg = cross(w_gate[0])
    wu = cross(w_up[0])
    wd = cross(w_down[0])

    def slices(row):
        return [lax.dynamic_slice_in_dim(row[0], (2 * q + (core ^ k)) * cut, cut, 0) for k in range(2)]

    gains, scorers = slices(gain), slices(scorer)
    up1 = tick(v1c, gains, scorers, wg, wu, wd, z, core)
    v2n = jnp.where(has, pick(hit, up1), b2c)
    ahead = [(i, (i + 1) % n_seg) for i in range(n_seg)]
    v2c = lax.ppermute(v2n, "segment", ahead)
    up1_slots = jnp.concatenate([pick(comp1.T, up1), slots1[:, cut:]], axis=1)
    comp2_slots = comp2.T
    before = lax.ppermute(
        jnp.concatenate([up1_slots, jnp.concatenate([comp2_slots, jnp.zeros((n_dp * cap, cut + 128 - compact), BF)], axis=1)], axis=0),
        "segment",
        ahead,
    )
    base = lax.ppermute(pending, "segment", ahead[:-1])
    up2 = tick(v2c, gains, scorers, wg, wu, wd, z, core)
    own_comp2 = before[n_dp * cap :, :compact]
    before = before[: n_dp * cap]
    up2_slots = jnp.concatenate([pick(own_comp2, up2), slots1[:, cut:]], axis=1)
    back = jnp.stack([x.reshape(n_dp, cap, -1) for x in (up1_slots, before, up2_slots)], axis=1)
    back = lax.all_to_all(back, DP, 0, 0, tiled=True)
    e1_before = back[0, 1, :, cut].astype(jnp.int32)
    rows = back[..., :cut].transpose(1, 2, 0, 3).reshape(3, cap, width)

    def put(into, at, new):
        return into.at[jnp.where(at >= 0, at, n_rows)].set(new, mode="drop")

    first = put(pending, e1, rows[0])
    second = jnp.where(s == 0, arriving, base)
    second = put(second, jnp.where(s == 0, -1, e1_before), rows[1])
    second = put(second, e2, rows[2])
    return first[None], second[None]


def solution(mesh):
    fine = Mesh(mesh.devices.reshape(4, 4, 2, 8, 2), ("segment", "q", "h", "z", "core"))
    dp, mp = ("q", "h"), ("z", "core")
    return jax.shard_map(
        local,
        mesh=fine,
        in_specs=(
            P("segment", dp + mp, None),
            P(dp + mp, None),
            P("segment", None),
            P("segment", None),
            P("segment", dp, mp),
            P("segment", dp, mp),
            P("segment", mp, dp),
            P(None, "segment", dp + mp, None),
        ),
        out_specs=(P("segment", dp + mp, None), P("segment", dp + mp, None)),
        check_vma=False,
    )
```

time: 565 us -> 282 us (0.50)
  waiting for transfers between devices: 387 us -> 50.7 us
  starting transfers between devices: 21.6 us -> 113 us
  blocking collectives: 109 us -> 70.1 us
  between operations: 15 us -> 1.58 us
    psum x2 -> x0, waiting for transfers between devices: 230 us -> none  [layer_tile(): lax.psum(partial_block.astype(jnp.bfloat16), 'mp').astype(jnp.float32)]
    reduce_scatter x2 -> x0, waiting for transfers between devices: 79.5 us -> none  [layer_tile(): lax.psum_scatter(jnp.dot(gathered, joined, preferred_element_type=jnp.flo...]
    ppermute x1 -> x10, starting transfers between devices: 1.29 us -> 69.6 us  [the longest x3 48.2 us: cross(): return (w, lax.ppermute(w, 'core', [(0, 1), (1, 0)]))]
    all_gather x2 -> x0, waiting for transfers between devices: 35.2 us -> none  [layer_tile(): lax.all_gather(slot_rows, 'mp', axis=0, tiled=True)]
    unnamed x1 -> x0, blocking collectives: 29.4 us -> none
    all_to_all x4 -> x6, starting transfers between devices: 20.1 us -> 43.4 us  [the longest x2 20.4 us: tick(): lax.all_to_all(out.reshape(2 * n_z, rows, width), PLANE, 0, 0, tiled=True)]
    all_gather x2, blocking collectives: 52.6 us -> 37.3 us  [tick(): hidden = lax.all_gather(hidden, 'q', axis=0, tiled=True)]
    all_to_all x4 -> x6, waiting for transfers between devices: 29.3 us -> 37.3 us  [the longest x2 16.4 us: tick(): lax.all_to_all(part.reshape(n_q, everyone // n_q, -1), 'q', 0, 0, tiled=T...]
  transfers between devices with their start and end apart: 11 -> 16, of which waited for: 10 -> 7; matrix products, arithmetic and copies ran while one was open for 1% -> 8% of each run, Pallas kernels for 0% -> 0%
where the time goes in v1:
time: 282 us; the launch traced here: 279 us
  starting transfers between devices  113 us (40%)
  blocking collectives  70.1 us (25%)
  waiting for transfers between devices  50.7 us (18%)
  matrix products  20 us (7%)
  other arithmetic  13.2 us (5%)
  local copies, waits for them, and re-layouts  10.3 us (4%)
    ppermute x3, starting transfers between devices, cross(): return (w, lax.ppermute(w, 'core', [(0, 1), (1, 0)]))  48.2 us
    all_gather x2, blocking collectives, tick(): hidden = lax.all_gather(hidden, 'q', axis=0, tiled=True)  37.3 us
    all_to_all x2, starting transfers between devices, tick(): lax.all_to_all(out.reshape(2 * n_z, rows, width), PLANE, 0, 0, tiled=True)  20.4 us
    all_to_all x1, blocking collectives, tick(): lax.all_to_all(jnp.broadcast_to(v[None], (2 * n_z, rows, width)), PLANE,...  19.1 us
    all_to_all x2, waiting for transfers between devices, tick(): lax.all_to_all(part.reshape(n_q, everyone // n_q, -1), 'q', 0, 0, tiled=T...  16.4 us
    all_to_all x1, blocking collectives, local(): got = lax.all_to_all(both, DP, 0, 0, tiled=True)  13.7 us
    ppermute x3, starting transfers between devices, cross(): w = lax.ppermute(w, ('h', 'core'), [(0, 0), (3, 3), (1, 2), (2, 1)])  12 us
    all_to_all x2, waiting for transfers between devices, tick(): lax.all_to_all(out.reshape(2 * n_z, rows, width), PLANE, 0, 0, tiled=True)  10.7 us
  transfers between devices with their start and end apart: 16, of which 7 were waited for; matrix products, arithmetic and copies ran while one was open for 8% of the time, Pallas kernels for 0%

profile of v1, /device:TPU:6, one launch (start us, length us, event | category | flops | bytes accessed | tf_op | source)
XLA Modules:
  0.0 278.9 jit_solution(2179358096626361160)
XLA Ops:
  1.8 2.7 collective-permute-start
  5.2 5.8 %collective-permute-done = s32[8]{0:T(128)S(1)} collective-permute-done((s32[8]{0:T(128)S(1)}, s32[8]{0:T(128)S(1)}, u32[]{:S(2)}, u32[]{:S(2)}) %collective-permute-start) | collective-permute-done | bytes 64 | tf_op jit(solution)/shard_map/ppermute | solution.py:99
  12.6 13.7 %all_to_all.40 = bf16[8,16,640]{2,1,0:T(8,128)(2,1)S(1)} all-to-all(bf16[8,16,640]{2,1,0:T(8,128)(2,1)S(1)} %pad_maximum_fusion.5), channel_id=1, replica_groups=mesh['segment'=4,'q'=4,'h'=2,'z'=8,'core'=2] {'q','h'}, dimensions={0} | all-to-all | bytes 327680 | tf_op jit(solution)/shard_map/all_to_all | solution.py:106
  28.1 10.4 %all-to-all-start.1 = ((bf16[16,32,512]{2,1,0:T(8,128)(2,1)}), bf16[16,32,512]{2,1,0:T(8,128)(2,1)S(1)}, u32[]{:S(2)}, u32[]{:S(2)}) async-start(bf16[16,32,512]{2,1,0:T(8,128)(2,1)} %broadcast_in_dim.349), calls=%async_computation.1 | async-start | bytes 1048576 | tf_op jit(solution)/shard_map/all_to_all | solution.py:49
  43.0 13.6 %collective-permute-start.2 = (bf16[512,896]{1,0:T(8,128)(2,1)S(1)}, bf16[512,896]{1,0:T(8,128)(2,1)}, u32[]{:S(2)}, u32[]{:S(2)}) collective-permute-start(bf16[512,896]{1,0:T(8,128)(2,1)S(1)} %collective-permute-done.1), channel_id=1, source_target_pairs={{0,1},{1,0},{2,3},{3,2},{4,5},{5,4},{6,7},{7,6},{8,9},{9,8},{10,11... | collective-permute-start | bytes 2752520 | tf_op jit(solution)/shard_map/ppermute | solution.py:41
  56.7 9.8 %collective-permute-start.4 = (bf16[512,896]{1,0:T(8,128)(2,1)S(1)}, bf16[512,896]{1,0:T(8,128)(2,1)}, u32[]{:S(2)}, u32[]{:S(2)}) collective-permute-start(bf16[512,896]{1,0:T(8,128)(2,1)S(1)} %collective-permute-done.3), channel_id=1, source_target_pairs={{0,1},{1,0},{2,3},{3,2},{4,5},{5,4},{6,7},{7,6},{8,9},{9,8},{10,11... | collective-permute-start | bytes 2752520 | tf_op jit(solution)/shard_map/ppermute | solution.py:41
  72.3 3.5 %all-to-all-start.2 = ((bf16[4,64,1920]{2,1,0:T(8,128)(2,1)}), bf16[4,64,1920]{2,1,0:T(8,128)(2,1)S(1)}, u32[]{:S(2)}, u32[]{:S(2)}) async-start(bf16[4,64,1920]{2,1,0:T(8,128)(2,1)} %bitcast.19), calls=%async_computation.2 | async-start | bytes 1966080 | tf_op jit(solution)/shard_map/all_to_all | solution.py:67
  75.8 8.3 %collective-permute-start.5 = (bf16[896,512]{1,0:T(8,128)(2,1)}, bf16[896,512]{1,0:T(8,128)(2,1)}, u32[]{:S(2)}, u32[]{:S(2)}) collective-permute-start(bf16[896,512]{1,0:T(8,128)(2,1)} %bitcast.158), channel_id=1, source_target_pairs={{0,0},{17,17},{1,16},{16,1},{2,2},{19,19},{3,18},{18,3},{4,4},{21,... | collective-permute-start | bytes 2752520 | tf_op jit(solution)/shard_map/ppermute | solution.py:40
  86.0 24.7 %collective-permute-start.6 = (bf16[896,512]{1,0:T(8,128)(2,1)}, bf16[896,512]{1,0:T(8,128)(2,1)}, u32[]{:S(2)}, u32[]{:S(2)}) collective-permute-start(bf16[896,512]{1,0:T(8,128)(2,1)} %collective-permute-done.5), channel_id=1, source_target_pairs={{0,1},{1,0},{2,3},{3,2},{4,5},{5,4},{6,7},{7,6},{8,9},{9,8},{10,11... | collective-permute-start | bytes 2752520 | tf_op jit(solution)/shard_map/ppermute | solution.py:41
  114.2 16.9 %all_gather.6 = bf16[256,1024]{1,0:T(8,128)(2,1)S(1)} all-gather(bf16[64,1024]{1,0:T(8,128)(2,1)S(1)} %pad_maximum_fusion.8), channel_id=1, replica_groups=mesh['segment'=4,'q'=4,'h'=2,'z'=8,'core'=2] {'q'}, dimensions={0}, use_global_device_ids=true | all-gather | bytes 655360 | tf_op jit(solution)/shard_map/all_gather | solution.py:74
  135.2 9.2 %all-to-all-start.3 = ((bf16[16,32,512]{2,1,0:T(8,128)(2,1)}), bf16[16,32,512]{2,1,0:T(8,128)(2,1)S(1)}, u32[]{:S(2)}, u32[]{:S(2)}) async-start(bf16[16,32,512]{2,1,0:T(8,128)(2,1)} %bitcast.26), calls=%async_computation.3 | async-start | bytes 1048576 | tf_op jit(solution)/shard_map/all_to_all | solution.py:80
  144.5 2.2 convert_reduce_fusion.4
  149.7 8.1 %all-to-all-done.3 = bf16[16,32,512]{2,1,0:T(8,128)(2,1)S(1)} async-done(((bf16[16,32,512]{2,1,0:T(8,128)(2,1)}), bf16[16,32,512]{2,1,0:T(8,128)(2,1)S(1)}, u32[]{:S(2)}, u32[]{:S(2)}) %all-to-all-start.3) | async-done | bytes 524320 | tf_op jit(solution)/shard_map/all_to_all | solution.py:80
  160.8 3.9 %collective-permute-done.8 = bf16[32,512]{1,0:T(8,128)(2,1)S(1)} collective-permute-done((bf16[32,512]{1,0:T(8,128)(2,1)S(1)}, bf16[32,512]{1,0:T(8,128)(2,1)S(1)}, u32[]{:S(2)}, u32[]{:S(2)}) %collective-permute-start.8) | collective-permute-done | bytes 32800 | tf_op jit(solution)/shard_map/ppermute | solution.py:132
  164.7 19.1 %all_to_all.41 = bf16[16,32,512]{2,1,0:T(8,128)(2,1)S(1)} all-to-all(bf16[16,32,512]{2,1,0:T(8,128)(2,1)S(1)} %broadcast_in_dim.372), channel_id=1, replica_groups=mesh['segment'=4,'q'=4,'h'=2,'z'=8,'core'=2] {'h','z'}, dimensions={0} | all-to-all | bytes 1048576 | tf_op jit(solution)/shard_map/all_to_all | solution.py:49
  189.6 4.2 %all-to-all-start.5 = ((bf16[4,64,1920]{2,1,0:T(8,128)(2,1)}), bf16[4,64,1920]{2,1,0:T(8,128)(2,1)S(1)}, u32[]{:S(2)}, u32[]{:S(2)}) async-start(bf16[4,64,1920]{2,1,0:T(8,128)(2,1)} %bitcast.37), calls=%async_computation.5 | async-start | bytes 1966080 | tf_op jit(solution)/shard_map/all_to_all | solution.py:67
  195.2 16.4 %all-to-all-done.5 = bf16[4,64,1920]{2,1,0:T(8,128)(2,1)S(1)} async-done(((bf16[4,64,1920]{2,1,0:T(8,128)(2,1)}), bf16[4,64,1920]{2,1,0:T(8,128)(2,1)S(1)}, u32[]{:S(2)}, u32[]{:S(2)}) %all-to-all-start.5) | async-done | bytes 983072 | tf_op jit(solution)/shard_map/all_to_all | solution.py:67
  212.4 20.4 %all_gather.7 = bf16[256,1024]{1,0:T(8,128)(2,1)S(1)} all-gather(bf16[64,1024]{1,0:T(8,128)(2,1)S(1)} %pad_maximum_fusion.9), channel_id=1, replica_groups=mesh['segment'=4,'q'=4,'h'=2,'z'=8,'core'=2] {'q'}, dimensions={0}, use_global_device_ids=true | all-gather | bytes 655360 | tf_op jit(solution)/shard_map/all_gather | solution.py:74
  237.0 11.2 %all-to-all-start.6 = ((bf16[16,32,512]{2,1,0:T(8,128)(2,1)}), bf16[16,32,512]{2,1,0:T(8,128)(2,1)S(1)}, u32[]{:S(2)}, u32[]{:S(2)}) async-start(bf16[16,32,512]{2,1,0:T(8,128)(2,1)} %bitcast.43), calls=%async_computation.6 | async-start | bytes 1048576 | tf_op jit(solution)/shard_map/all_to_all | solution.py:80
  248.4 3.4 %collective-permute-start.7 = (bf16[128,640]{1,0:T(8,128)(2,1)S(1)}, bf16[128,640]{1,0:T(8,128)(2,1)S(1)}, u32[]{:S(2)}, u32[]{:S(2)}) collective-permute-start(bf16[128,640]{1,0:T(8,128)(2,1)S(1)} %pad_maximum_fusion.6), channel_id=1, source_target_pairs={{0,128},{128,256},{256,384},{384,0},{1,129},{129,257},{257,385},{3... | collective-permute-start | bytes 491528 | tf_op jit(solution)/shard_map/ppermute | solution.py:135
  251.9 3.7 %collective-permute-done.7 = bf16[128,640]{1,0:T(8,128)(2,1)S(1)} collective-permute-done((bf16[128,640]{1,0:T(8,128)(2,1)S(1)}, bf16[128,640]{1,0:T(8,128)(2,1)S(1)}, u32[]{:S(2)}, u32[]{:S(2)}) %collective-permute-start.7) | collective-permute-done | bytes 163872 | tf_op jit(solution)/shard_map/ppermute | solution.py:135
  255.9 2.7 all-to-all-done.6
  259.6 4.9 %all-to-all-start.7 = ((bf16[8,3,8,640]{3,2,1,0:T(8,128)(2,1)}), bf16[8,3,8,640]{3,2,1,0:T(8,128)(2,1)S(1)}, u32[]{:S(2)}, u32[]{:S(2)}) async-start(bf16[8,3,8,640]{3,2,1,0:T(8,128)(2,1)} %pad_maximum_fusion.4), calls=%async_computation.7 | async-start | bytes 491520 | tf_op jit(solution)/shard_map/all_to_all | solution.py:146
  264.6 10.2 %all-to-all-done.7 = bf16[8,3,8,640]{3,2,1,0:T(8,128)(2,1)S(1)} async-done(((bf16[8,3,8,640]{3,2,1,0:T(8,128)(2,1)}), bf16[8,3,8,640]{3,2,1,0:T(8,128)(2,1)S(1)}, u32[]{:S(2)}, u32[]{:S(2)}) %all-to-all-start.7) | async-done | bytes 245792 | tf_op jit(solution)/shard_map/all_to_all | solution.py:146
  (172 shorter events, 48.2 us)
Async XLA Ops:
  1.8 9.3 %collective-permute-start = (s32[8]{0:T(128)S(1)}, s32[8]{0:T(128)S(1)}, u32[]{:S(2)}, u32[]{:S(2)}) collective-permute-start(s32[8]{0:T(128)S(1)} %get-tuple-element.55), channel_id=1, source_target_pairs={{0,384},{128,0},{256,128},{384,256},{1,385},{129,1},{257,129},{385... | collective-permute-start | bytes 104 | tf_op jit(solution)/shard_map/ppermute | solution.py:99
  4.5 62.3 %copy-start.6 = (pred[128]{0:T(512)(128)(4,1)}, pred[128]{0:T(512)(128)(4,1)S(1)}, u32[]{:S(2)}) copy-start(pred[128]{0:T(512)(128)(4,1)S(1)} %iota_compare_fusion.9) | copy-start | bytes 388
  26.3 59.1 %copy-start.5 = (bf16[64,640]{1,0:T(8,128)(2,1)}, bf16[64,640]{1,0:T(8,128)(2,1)S(1)}, u32[]{:S(2)}) copy-start(bf16[64,640]{1,0:T(8,128)(2,1)S(1)} %get-tuple-element.32) | copy-start | bytes 245764
  28.1 38.4 %all-to-all-start.1 = ((bf16[16,32,512]{2,1,0:T(8,128)(2,1)}), bf16[16,32,512]{2,1,0:T(8,128)(2,1)S(1)}, u32[]{:S(2)}, u32[]{:S(2)}) async-start(bf16[16,32,512]{2,1,0:T(8,128)(2,1)} %broadcast_in_dim.349), calls=%async_computation.1 | async-start | bytes 1048576 | tf_op jit(solution)/shard_map/all_to_all | solution.py:49
  38.5 4.5 %collective-permute-start.1 = (bf16[512,896]{1,0:T(8,128)(2,1)}, bf16[512,896]{1,0:T(8,128)(2,1)S(1)}, u32[]{:S(2)}, u32[]{:S(2)}) collective-permute-start(bf16[512,896]{1,0:T(8,128)(2,1)} %bitcast.11), channel_id=1, source_target_pairs={{0,0},{17,17},{1,16},{16,1},{2,2},{19,19},{3,18},{18,3},{4,4},{21,... | collective-permute-start | bytes 2752520 | tf_op jit(solution)/shard_map/ppermute | solution.py:40
  40.4 16.3 %collective-permute-start.3 = (bf16[512,896]{1,0:T(8,128)(2,1)}, bf16[512,896]{1,0:T(8,128)(2,1)S(1)}, u32[]{:S(2)}, u32[]{:S(2)}) collective-permute-start(bf16[512,896]{1,0:T(8,128)(2,1)} %bitcast.157), channel_id=1, source_target_pairs={{0,0},{17,17},{1,16},{16,1},{2,2},{19,19},{3,18},{18,3},{4,4},{21,... | collective-permute-start | bytes 2752520 | tf_op jit(solution)/shard_map/ppermute | solution.py:40
  42.2 25.3 %copy-start.19 = (pred[128]{0:T(512)(128)(4,1)}, pred[128]{0:T(512)(128)(4,1)S(1)}, u32[]{:S(2)}) copy-start(pred[128]{0:T(512)(128)(4,1)S(1)} %iota_compare_fusion.8) | copy-start | bytes 388
  42.2 25.3 %copy-start.8 = (pred[128]{0:T(512)(128)(4,1)}, pred[128]{0:T(512)(128)(4,1)S(1)}, u32[]{:S(2)}) copy-start(pred[128]{0:T(512)(128)(4,1)S(1)} %get-tuple-element.66) | copy-start | bytes 388
  42.2 25.3 %copy-start.10 = (pred[128]{0:T(512)(128)(4,1)}, pred[128]{0:T(512)(128)(4,1)S(1)}, u32[]{:S(2)}) copy-start(pred[128]{0:T(512)(128)(4,1)S(1)} %get-tuple-element.67) | copy-start | bytes 388
  42.2 25.3 %copy-start.21 = (pred[128]{0:T(512)(128)(4,1)}, pred[128]{0:T(512)(128)(4,1)S(1)}, u32[]{:S(2)}) copy-start(pred[128]{0:T(512)(128)(4,1)S(1)} %get-tuple-element.68) | copy-start | bytes 388
  42.2 25.3 %copy-start.23 = (pred[128]{0:T(512)(128)(4,1)}, pred[128]{0:T(512)(128)(4,1)S(1)}, u32[]{:S(2)}) copy-start(pred[128]{0:T(512)(128)(4,1)S(1)} %get-tuple-element.69) | copy-start | bytes 388
  43.0 25.0 %collective-permute-start.2 = (bf16[512,896]{1,0:T(8,128)(2,1)S(1)}, bf16[512,896]{1,0:T(8,128)(2,1)}, u32[]{:S(2)}, u32[]{:S(2)}) collective-permute-start(bf16[512,896]{1,0:T(8,128)(2,1)S(1)} %collective-permute-done.1), channel_id=1, source_target_pairs={{0,1},{1,0},{2,3},{3,2},{4,5},{5,4},{6,7},{7,6},{8,9},{9,8},{10,11... | collective-permute-start | bytes 2752520 | tf_op jit(solution)/shard_map/ppermute | solution.py:41
  56.7 13.0 %collective-permute-start.4 = (bf16[512,896]{1,0:T(8,128)(2,1)S(1)}, bf16[512,896]{1,0:T(8,128)(2,1)}, u32[]{:S(2)}, u32[]{:S(2)}) collective-permute-start(bf16[512,896]{1,0:T(8,128)(2,1)S(1)} %collective-permute-done.3), channel_id=1, source_target_pairs={{0,1},{1,0},{2,3},{3,2},{4,5},{5,4},{6,7},{7,6},{8,9},{9,8},{10,11... | collective-permute-start | bytes 2752520 | tf_op jit(solution)/shard_map/ppermute | solution.py:41
  72.3 38.5 %all-to-all-start.2 = ((bf16[4,64,1920]{2,1,0:T(8,128)(2,1)}), bf16[4,64,1920]{2,1,0:T(8,128)(2,1)S(1)}, u32[]{:S(2)}, u32[]{:S(2)}) async-start(bf16[4,64,1920]{2,1,0:T(8,128)(2,1)} %bitcast.19), calls=%async_computation.2 | async-start | bytes 1966080 | tf_op jit(solution)/shard_map/all_to_all | solution.py:67
  75.8 10.2 %collective-permute-start.5 = (bf16[896,512]{1,0:T(8,128)(2,1)}, bf16[896,512]{1,0:T(8,128)(2,1)}, u32[]{:S(2)}, u32[]{:S(2)}) collective-permute-start(bf16[896,512]{1,0:T(8,128)(2,1)} %bitcast.158), channel_id=1, source_target_pairs={{0,0},{17,17},{1,16},{16,1},{2,2},{19,19},{3,18},{18,3},{4,4},{21,... | collective-permute-start | bytes 2752520 | tf_op jit(solution)/shard_map/ppermute | solution.py:40
  86.0 46.6 %collective-permute-start.6 = (bf16[896,512]{1,0:T(8,128)(2,1)}, bf16[896,512]{1,0:T(8,128)(2,1)}, u32[]{:S(2)}, u32[]{:S(2)}) collective-permute-start(bf16[896,512]{1,0:T(8,128)(2,1)} %collective-permute-done.5), channel_id=1, source_target_pairs={{0,1},{1,0},{2,3},{3,2},{4,5},{5,4},{6,7},{7,6},{8,9},{9,8},{10,11... | collective-permute-start | bytes 2752520 | tf_op jit(solution)/shard_map/ppermute | solution.py:41
  135.2 22.6 %all-to-all-start.3 = ((bf16[16,32,512]{2,1,0:T(8,128)(2,1)}), bf16[16,32,512]{2,1,0:T(8,128)(2,1)S(1)}, u32[]{:S(2)}, u32[]{:S(2)}) async-start(bf16[16,32,512]{2,1,0:T(8,128)(2,1)} %bitcast.26), calls=%async_computation.3 | async-start | bytes 1048576 | tf_op jit(solution)/shard_map/all_to_all | solution.py:80
  158.8 25.3 %copy-start.7 = (pred[128]{0:T(512)(128)(4,1)S(1)}, pred[128]{0:T(512)(128)(4,1)}, u32[]{:S(2)}) copy-start(pred[128]{0:T(512)(128)(4,1)} %copy-done.6) | copy-start | bytes 388
  158.9 5.8 %collective-permute-start.8 = (bf16[32,512]{1,0:T(8,128)(2,1)S(1)}, bf16[32,512]{1,0:T(8,128)(2,1)S(1)}, u32[]{:S(2)}, u32[]{:S(2)}) collective-permute-start(bf16[32,512]{1,0:T(8,128)(2,1)S(1)} %fusion.4), channel_id=1, source_target_pairs={{0,128},{128,256},{256,384},{384,0},{1,129},{129,257},{257,385},{3... | collective-permute-start | bytes 98312 | tf_op jit(solution)/shard_map/ppermute | solution.py:132
  189.6 21.9 %all-to-all-start.5 = ((bf16[4,64,1920]{2,1,0:T(8,128)(2,1)}), bf16[4,64,1920]{2,1,0:T(8,128)(2,1)S(1)}, u32[]{:S(2)}, u32[]{:S(2)}) async-start(bf16[4,64,1920]{2,1,0:T(8,128)(2,1)} %bitcast.37), calls=%async_computation.5 | async-start | bytes 1966080 | tf_op jit(solution)/shard_map/all_to_all | solution.py:67
  193.8 70.7 %collective-permute-start.9 = (bf16[64,4096]{1,0:T(8,128)(2,1)S(1)}, bf16[64,4096]{1,0:T(8,128)(2,1)S(1)}, u32[]{:S(2)}, u32[]{:S(2)}) collective-permute-start(bf16[64,4096]{1,0:T(8,128)(2,1)S(1)} %bitcast.126), channel_id=1, source_target_pairs={{0,128},{128,256},{256,384},{1,129},{129,257},{257,385},{2,130},{1... | collective-permute-start | bytes 1572872 | tf_op jit(solution)/shard_map/ppermute | solution.py:140
  237.0 21.6 %all-to-all-start.6 = ((bf16[16,32,512]{2,1,0:T(8,128)(2,1)}), bf16[16,32,512]{2,1,0:T(8,128)(2,1)S(1)}, u32[]{:S(2)}, u32[]{:S(2)}) async-start(bf16[16,32,512]{2,1,0:T(8,128)(2,1)} %bitcast.43), calls=%async_computation.6 | async-start | bytes 1048576 | tf_op jit(solution)/shard_map/all_to_all | solution.py:80
  248.4 7.2 %collective-permute-start.7 = (bf16[128,640]{1,0:T(8,128)(2,1)S(1)}, bf16[128,640]{1,0:T(8,128)(2,1)S(1)}, u32[]{:S(2)}, u32[]{:S(2)}) collective-permute-start(bf16[128,640]{1,0:T(8,128)(2,1)S(1)} %pad_maximum_fusion.6), channel_id=1, source_target_pairs={{0,128},{128,256},{256,384},{384,0},{1,129},{129,257},{257,385},{3... | collective-permute-start | bytes 491528 | tf_op jit(solution)/shard_map/ppermute | solution.py:135
  259.6 15.2 %all-to-all-start.7 = ((bf16[8,3,8,640]{3,2,1,0:T(8,128)(2,1)}), bf16[8,3,8,640]{3,2,1,0:T(8,128)(2,1)S(1)}, u32[]{:S(2)}, u32[]{:S(2)}) async-start(bf16[8,3,8,640]{3,2,1,0:T(8,128)(2,1)} %pad_maximum_fusion.4), calls=%async_computation.7 | async-start | bytes 491520 | tf_op jit(solution)/shard_map/all_to_all | solution.py:146
  (18 other events, 198.7 us)

commit v2 on v1

--- a/solution.py
+++ b/solution.py
@@ -37,11 +37,18 @@
 
 
 def cross(w):
-    w = lax.ppermute(w, ("h", "core"), [(0, 0), (3, 3), (1, 2), (2, 1)])
-    return w, lax.ppermute(w, "core", [(0, 1), (1, 0)])
+    return lax.ppermute(w, ("h", "core"), [(0, 0), (3, 3), (1, 2), (2, 1)])
 
 
-def tick(v, gains, scorers, wg, wu, wd, z, core):
+def sibling(w):
+    return lax.ppermute(w, "core", [(0, 1), (1, 0)])
+
+
+def after(x, *others):
+    return lax.optimization_barrier((x, *others))
+
+
+def tick(v, gains, scorers, w1, w2, base, z, core):
     rows = v.shape[0]
     n_z = lax.axis_size("z")
     n_q = lax.axis_size("q")
@@ -49,6 +56,8 @@
     g = lax.all_to_all(
         jnp.broadcast_to(v[None], (2 * n_z, rows, width)), PLANE, 0, 0, tiled=True
     ).reshape(2, n_z * rows, width)
+    g, *w1 = after(g, *w1)
+    wg, wu = [w[0] for w in w1], [w[1] for w in w1]
     ss = 0.0
     dot = 0.0
     gate = 0.0
@@ -64,6 +73,7 @@
     extra = lanes(parts3(ss) + parts3(dot), everyone)
     part = jnp.concatenate([gate.astype(BF), up.astype(BF), extra], axis=1)
     units = gate.shape[1]
+    part, w2_own = after(part, w2[0])
     part = lax.all_to_all(part.reshape(n_q, everyone // n_q, -1), "q", 0, 0, tiled=True)
     total = jnp.sum(part.astype(F32), axis=0)
     ext = total[:, 2 * units :]
@@ -71,15 +81,18 @@
     weight = jax.nn.sigmoid(ext[:, 3] + ext[:, 4] + ext[:, 5])
     hidden = (jax.nn.silu(total[:, :units] * inv) * (total[:, units : 2 * units] * inv)).astype(BF)
     hidden = jnp.concatenate([hidden, lanes(parts3(weight), everyone // n_q)], axis=1)
+    hidden, w2_other = after(hidden, sibling(w2_own) if len(w2) == 1 else w2[1])
+    wd = (w2_own, w2_other)
     hidden = lax.all_gather(hidden, "q", axis=0, tiled=True)
     own = lax.dynamic_slice_in_dim(hidden[:, units:], z * rows, rows, 0).astype(F32)
     weight = own[:, 0] + own[:, 1] + own[:, 2]
     hidden = hidden[:, :units]
     outs = [jnp.dot(hidden, wd[k], preferred_element_type=F32).astype(BF) for k in range(2)]
     out = jnp.stack([jnp.where(core == 0, outs[0], outs[1]), jnp.where(core == 0, outs[1], outs[0])])
+    out, base = after(out, base)
     out = lax.all_to_all(out.reshape(2 * n_z, rows, width), PLANE, 0, 0, tiled=True)
     block_out = jnp.sum(out.astype(F32), axis=0).astype(BF).astype(F32)
-    return (v.astype(F32) + weight[:, None] * block_out).astype(BF)
+    return (v.astype(F32) + weight[:, None] * block_out).astype(BF), wd, base
 
 
 def local(pending, arriving, gain, scorer, w_gate, w_up, w_down, lists):
@@ -118,17 +131,19 @@
     v1c = pick(comp1, slots1[:, :cut])
     b2c = pick(comp2, slots2[:, :cut])
 
-    wg = cross(w_gate[0])
-    wu = cross(w_up[0])
-    wd = cross(w_down[0])
+    w1 = cross(jnp.stack([w_gate[0], w_up[0]]))
+    v1c, w1 = after(v1c, w1)
+    w1 = (w1, sibling(w1))
+    w2 = cross(w_down[0])
+    ahead = [(i, (i + 1) % n_seg) for i in range(n_seg)]
+    base = lax.ppermute(pending, "segment", ahead[:-1])
 
     def slices(row):
         return [lax.dynamic_slice_in_dim(row[0], (2 * q + (core ^ k)) * cut, cut, 0) for k in range(2)]
 
     gains, scorers = slices(gain), slices(scorer)
-    up1 = tick(v1c, gains, scorers, wg, wu, wd, z, core)
+    up1, w2, base = tick(v1c, gains, scorers, w1, (w2,), base, z, core)
     v2n = jnp.where(has, pick(hit, up1), b2c)
-    ahead = [(i, (i + 1) % n_seg) for i in range(n_seg)]
     v2c = lax.ppermute(v2n, "segment", ahead)
     up1_slots = jnp.concatenate([pick(comp1.T, up1), slots1[:, cut:]], axis=1)
     comp2_slots = comp2.T
@@ -137,8 +152,7 @@
         "segment",
         ahead,
     )
-    base = lax.ppermute(pending, "segment", ahead[:-1])
-    up2 = tick(v2c, gains, scorers, wg, wu, wd, z, core)
+    up2, _, base = tick(v2c, gains, scorers, w1, w2, base, z, core)
     own_comp2 = before[n_dp * cap :, :compact]
     before = before[: n_dp * cap]
     up2_slots = jnp.concatenate([pick(own_comp2, up2), slots1[:, cut:]], axis=1)
@@ -148,12 +162,14 @@
     rows = back[..., :cut].transpose(1, 2, 0, 3).reshape(3, cap, width)
 
     def put(into, at, new):
-        return into.at[jnp.where(at >= 0, at, n_rows)].set(new, mode="drop")
+        onehot = jnp.arange(n_rows, dtype=jnp.int32)[:, None] == at[None, :]
+        return jnp.where(jnp.any(onehot, axis=1)[:, None], pick(onehot.astype(BF), new), into)
 
     first = put(pending, e1, rows[0])
     second = jnp.where(s == 0, arriving, base)
-    second = put(second, jnp.where(s == 0, -1, e1_before), rows[1])
-    second = put(second, e2, rows[2])
+    replaced = jnp.any(e1_before[:, None] == jnp.where(e2 >= 0, e2, -2)[None, :], axis=1)
+    e1_before = jnp.where((s == 0) | replaced, -1, e1_before)
+    second = put(second, jnp.concatenate([e1_before, e2]), jnp.concatenate([rows[1], rows[2]], axis=0))
     return first[None], second[None]
 
 

time: 282 us -> 271 us (0.961)
  starting transfers between devices: 113 us -> 75.9 us
  blocking collectives: 70.1 us -> 83.5 us
  waiting for transfers between devices: 50.7 us -> 60.7 us
  local copies, waits for them, and re-layouts: 10.3 us -> 5.4 us
  other arithmetic: 13.2 us -> 17.7 us
  matrix products: 20 us -> 23.4 us
    ppermute x6 -> x4, starting transfers between devices: 60.2 us -> 16.6 us  [the longest x2 10.5 us: cross(): return lax.ppermute(w, ('h', 'core'), [(0, 0), (3, 3), (1, 2), (2, 1)])]
    all_to_all x2, waiting for transfers between devices: 16.4 us -> 30.4 us  [tick(): lax.all_to_all(part.reshape(n_q, everyone // n_q, -1), 'q', 0, 0, tiled=T...]
    all_to_all x1, blocking collectives: 13.7 us -> 24.6 us  [local(): got = lax.all_to_all(both, DP, 0, 0, tiled=True)]
    all_to_all x1, waiting for transfers between devices: 0.01 us -> 6.93 us  [tick(): lax.all_to_all(jnp.broadcast_to(v[None], (2 * n_z, rows, width)), PLANE,...]
    ppermute x1, waiting for transfers between devices: 5.79 us -> 0.19 us  [local(): lax.ppermute(e2, 'segment', [(i, (i - 1) % n_seg) for i in range(n_seg)])]
    all_gather x2, blocking collectives: 37.3 us -> 41 us  [tick(): hidden = lax.all_gather(hidden, 'q', axis=0, tiled=True)]
    dot_general x6 -> x8, matrix products: 5.29 us -> 8.69 us  [pick(): return jnp.dot(onehot, x, preferred_element_type=F32).astype(BF)]
    scatter x3 -> x0, local copies, waits for them, and re-layouts: 3.07 us -> none  [put(): return into.at[jnp.where(at >= 0, at, n_rows)].set(new, mode='drop')]
  transfers between devices with their start and end apart: 16 -> 14, of which waited for: 7 -> 9; matrix products, arithmetic and copies ran while one was open for 8% -> 10% of each run, Pallas kernels for 0% -> 0%
where the time goes in v2:
time: 271 us; the launch traced here: 268 us
  blocking collectives  83.5 us (31%)
  starting transfers between devices  75.9 us (28%)
  waiting for transfers between devices  60.7 us (22%)
  matrix products  23.4 us (9%)
  other arithmetic  17.7 us (7%)
  local copies, waits for them, and re-layouts  5.4 us (2%)
    all_gather x2, blocking collectives, tick(): hidden = lax.all_gather(hidden, 'q', axis=0, tiled=True)  41 us
    all_to_all x2, waiting for transfers between devices, tick(): lax.all_to_all(part.reshape(n_q, everyone // n_q, -1), 'q', 0, 0, tiled=T...  30.4 us
    all_to_all x1, blocking collectives, local(): got = lax.all_to_all(both, DP, 0, 0, tiled=True)  24.6 us
    all_to_all x2, starting transfers between devices, tick(): lax.all_to_all(out.reshape(2 * n_z, rows, width), PLANE, 0, 0, tiled=True)  20.7 us
    all_to_all x1, blocking collectives, tick(): lax.all_to_all(jnp.broadcast_to(v[None], (2 * n_z, rows, width)), PLANE,...  17.8 us
    all_to_all x1, starting transfers between devices, tick(): lax.all_to_all(jnp.broadcast_to(v[None], (2 * n_z, rows, width)), PLANE,...  11.1 us
    ppermute x2, starting transfers between devices, cross(): return lax.ppermute(w, ('h', 'core'), [(0, 0), (3, 3), (1, 2), (2, 1)])  10.5 us
    all_to_all x1, waiting for transfers between devices, local(): back = lax.all_to_all(back, DP, 0, 0, tiled=True)  10.2 us
  transfers between devices with their start and end apart: 14, of which 9 were waited for; matrix products, arithmetic and copies ran while one was open for 10% of the time, Pallas kernels for 0%

profile of v2, /device:TPU:6, one launch (start us, length us, event | category | flops | bytes accessed | tf_op | source)
XLA Modules:
  0.0 268.1 jit_solution(16451851775352579373)
XLA Ops:
  1.9 2.9 %collective-permute-start = (s32[8]{0:T(128)S(1)}, s32[8]{0:T(128)S(1)}, u32[]{:S(2)}, u32[]{:S(2)}) collective-permute-start(s32[8]{0:T(128)S(1)} %get-tuple-element.94), channel_id=1, source_target_pairs={{0,384},{128,0},{256,128},{384,256},{1,385},{129,1},{257,129},{385... | collective-permute-start | bytes 104 | tf_op jit(solution)/shard_map/ppermute | solution.py:112
  4.8 2.9 %pad_maximum_fusion = bf16[2,512,896]{2,1,0:T(8,128)(2,1)} fusion(bf16[1,512,896]{2,1,0:T(8,128)(2,1)} %param.15, bf16[1,512,896]{2,1,0:T(8,128)(2,1)} %param.14), kind=kLoop, calls=%fused_computation.11 | loop fusion | flops 917504 | bytes 3670016 | tf_op jit(solution)/shard_map/stack | solution.py:134
  7.7 2.1 collective-permute-start.1
  12.8 24.6 %all_to_all.40 = bf16[8,16,640]{2,1,0:T(8,128)(2,1)S(1)} all-to-all(bf16[8,16,640]{2,1,0:T(8,128)(2,1)S(1)} %pad_maximum_fusion.6), channel_id=1, replica_groups=mesh['segment'=4,'q'=4,'h'=2,'z'=8,'core'=2] {'q','h'}, dimensions={0} | all-to-all | bytes 327680 | tf_op jit(solution)/shard_map/all_to_all | solution.py:119
  38.4 4.3 %collective-permute-start.2 = (bf16[2,512,896]{2,1,0:T(8,128)(2,1)S(1)}, bf16[2,512,896]{2,1,0:T(8,128)(2,1)}, u32[]{:S(2)}, u32[]{:S(2)}) collective-permute-start(bf16[2,512,896]{2,1,0:T(8,128)(2,1)S(1)} %collective-permute-done.1), channel_id=1, source_target_pairs={{0,1},{1,0},{2,3},{3,2},{4,5},{5,4},{6,7},{7,6},{8,9},{9,8},{10,11... | collective-permute-start | bytes 5505032 | tf_op jit(solution)/shard_map/ppermute | solution.py:44
  43.6 11.1 %all-to-all-start.1 = ((bf16[16,32,512]{2,1,0:T(8,128)(2,1)}), bf16[16,32,512]{2,1,0:T(8,128)(2,1)S(1)}, u32[]{:S(2)}, u32[]{:S(2)}) async-start(bf16[16,32,512]{2,1,0:T(8,128)(2,1)} %broadcast_in_dim.364), calls=%async_computation.1 | async-start | bytes 1048576 | tf_op jit(solution)/shard_map/all_to_all | solution.py:56
  54.7 8.3 %collective-permute-start.3 = (bf16[896,512]{1,0:T(8,128)(2,1)}, bf16[896,512]{1,0:T(8,128)(2,1)}, u32[]{:S(2)}, u32[]{:S(2)}) collective-permute-start(bf16[896,512]{1,0:T(8,128)(2,1)} %bitcast.193), channel_id=1, source_target_pairs={{0,0},{17,17},{1,16},{16,1},{2,2},{19,19},{3,18},{18,3},{4,4},{21,... | collective-permute-start | bytes 2752520 | tf_op jit(solution)/shard_map/ppermute | solution.py:40
  63.8 6.9 %all-to-all-done.1 = bf16[16,32,512]{2,1,0:T(8,128)(2,1)S(1)} async-done(((bf16[16,32,512]{2,1,0:T(8,128)(2,1)}), bf16[16,32,512]{2,1,0:T(8,128)(2,1)S(1)}, u32[]{:S(2)}, u32[]{:S(2)}) %all-to-all-start.1) | async-done | bytes 524320 | tf_op jit(solution)/shard_map/all_to_all | solution.py:56
  76.6 3.5 %all-to-all-start.2 = ((bf16[4,64,1920]{2,1,0:T(8,128)(2,1)}), bf16[4,64,1920]{2,1,0:T(8,128)(2,1)S(1)}, u32[]{:S(2)}, u32[]{:S(2)}) async-start(bf16[4,64,1920]{2,1,0:T(8,128)(2,1)} %bitcast.19), calls=%async_computation.2 | async-start | bytes 1966080 | tf_op jit(solution)/shard_map/all_to_all | solution.py:77
  85.2 12.8 %all-to-all-done.2 = bf16[4,64,1920]{2,1,0:T(8,128)(2,1)S(1)} async-done(((bf16[4,64,1920]{2,1,0:T(8,128)(2,1)}), bf16[4,64,1920]{2,1,0:T(8,128)(2,1)S(1)}, u32[]{:S(2)}, u32[]{:S(2)}) %all-to-all-start.2) | async-done | bytes 983072 | tf_op jit(solution)/shard_map/all_to_all | solution.py:77
  101.4 20.8 %all_gather.6 = bf16[256,1024]{1,0:T(8,128)(2,1)S(1)} all-gather(bf16[64,1024]{1,0:T(8,128)(2,1)S(1)} %pad_maximum_fusion.9), channel_id=1, replica_groups=mesh['segment'=4,'q'=4,'h'=2,'z'=8,'core'=2] {'q'}, dimensions={0}, use_global_device_ids=true | all-gather | bytes 655360 | tf_op jit(solution)/shard_map/all_gather | solution.py:86
  126.3 9.3 %all-to-all-start.3 = ((bf16[16,32,512]{2,1,0:T(8,128)(2,1)}), bf16[16,32,512]{2,1,0:T(8,128)(2,1)S(1)}, u32[]{:S(2)}, u32[]{:S(2)}) async-start(bf16[16,32,512]{2,1,0:T(8,128)(2,1)} %bitcast.25), calls=%async_computation.3 | async-start | bytes 1048576 | tf_op jit(solution)/shard_map/all_to_all | solution.py:93
  140.3 6.8 %all-to-all-done.3 = bf16[16,32,512]{2,1,0:T(8,128)(2,1)S(1)} async-done(((bf16[16,32,512]{2,1,0:T(8,128)(2,1)}), bf16[16,32,512]{2,1,0:T(8,128)(2,1)S(1)}, u32[]{:S(2)}, u32[]{:S(2)}) %all-to-all-start.3) | async-done | bytes 524320 | tf_op jit(solution)/shard_map/all_to_all | solution.py:93
  148.1 4.3 %collective-permute-start.7 = (bf16[32,512]{1,0:T(8,128)(2,1)S(1)}, bf16[32,512]{1,0:T(8,128)(2,1)S(1)}, u32[]{:S(2)}, u32[]{:S(2)}) collective-permute-start(bf16[32,512]{1,0:T(8,128)(2,1)S(1)} %fusion.8), channel_id=1, source_target_pairs={{0,128},{128,256},{256,384},{384,0},{1,129},{129,257},{257,385},{3... | collective-permute-start | bytes 98312 | tf_op jit(solution)/shard_map/ppermute | solution.py:147
  154.1 17.8 %all_to_all.41 = bf16[16,32,512]{2,1,0:T(8,128)(2,1)S(1)} all-to-all(bf16[16,32,512]{2,1,0:T(8,128)(2,1)S(1)} %broadcast_in_dim.387), channel_id=1, replica_groups=mesh['segment'=4,'q'=4,'h'=2,'z'=8,'core'=2] {'h','z'}, dimensions={0} | all-to-all | bytes 1048576 | tf_op jit(solution)/shard_map/all_to_all | solution.py:56
  177.8 4.8 %all-to-all-start.5 = ((bf16[4,64,1920]{2,1,0:T(8,128)(2,1)}), bf16[4,64,1920]{2,1,0:T(8,128)(2,1)S(1)}, u32[]{:S(2)}, u32[]{:S(2)}) async-start(bf16[4,64,1920]{2,1,0:T(8,128)(2,1)} %bitcast.40), calls=%async_computation.5 | async-start | bytes 1966080 | tf_op jit(solution)/shard_map/all_to_all | solution.py:77
  182.7 17.7 %all-to-all-done.5 = bf16[4,64,1920]{2,1,0:T(8,128)(2,1)S(1)} async-done(((bf16[4,64,1920]{2,1,0:T(8,128)(2,1)}), bf16[4,64,1920]{2,1,0:T(8,128)(2,1)S(1)}, u32[]{:S(2)}, u32[]{:S(2)}) %all-to-all-start.5) | async-done | bytes 983072 | tf_op jit(solution)/shard_map/all_to_all | solution.py:77
  201.2 20.3 %all_gather.7 = bf16[256,1024]{1,0:T(8,128)(2,1)S(1)} all-gather(bf16[64,1024]{1,0:T(8,128)(2,1)S(1)} %pad_maximum_fusion.10), channel_id=1, replica_groups=mesh['segment'=4,'q'=4,'h'=2,'z'=8,'core'=2] {'q'}, dimensions={0}, use_global_device_ids=true | all-gather | bytes 655360 | tf_op jit(solution)/shard_map/all_gather | solution.py:86
  225.6 11.4 %all-to-all-start.6 = ((bf16[16,32,512]{2,1,0:T(8,128)(2,1)}), bf16[16,32,512]{2,1,0:T(8,128)(2,1)S(1)}, u32[]{:S(2)}, u32[]{:S(2)}) async-start(bf16[16,32,512]{2,1,0:T(8,128)(2,1)} %bitcast.46), calls=%async_computation.6 | async-start | bytes 1048576 | tf_op jit(solution)/shard_map/all_to_all | solution.py:93
  237.3 5.2 %collective-permute-start.6 = (bf16[128,640]{1,0:T(8,128)(2,1)S(1)}, bf16[128,640]{1,0:T(8,128)(2,1)S(1)}, u32[]{:S(2)}, u32[]{:S(2)}) collective-permute-start(bf16[128,640]{1,0:T(8,128)(2,1)S(1)} %pad_maximum_fusion.7), channel_id=1, source_target_pairs={{0,128},{128,256},{256,384},{384,0},{1,129},{129,257},{257,385},{3... | collective-permute-start | bytes 491528 | tf_op jit(solution)/shard_map/ppermute | solution.py:150
  242.5 2.8 %collective-permute-done.6 = bf16[128,640]{1,0:T(8,128)(2,1)S(1)} collective-permute-done((bf16[128,640]{1,0:T(8,128)(2,1)S(1)}, bf16[128,640]{1,0:T(8,128)(2,1)S(1)}, u32[]{:S(2)}, u32[]{:S(2)}) %collective-permute-start.6) | collective-permute-done | bytes 163872 | tf_op jit(solution)/shard_map/ppermute | solution.py:150
  248.4 5.4 %all-to-all-start.7 = ((bf16[8,3,8,640]{3,2,1,0:T(8,128)(2,1)}), bf16[8,3,8,640]{3,2,1,0:T(8,128)(2,1)S(1)}, u32[]{:S(2)}, u32[]{:S(2)}) async-start(bf16[8,3,8,640]{3,2,1,0:T(8,128)(2,1)} %pad_maximum_fusion.5), calls=%async_computation.7 | async-start | bytes 491520 | tf_op jit(solution)/shard_map/all_to_all | solution.py:160
  253.9 10.2 %all-to-all-done.7 = bf16[8,3,8,640]{3,2,1,0:T(8,128)(2,1)S(1)} async-done(((bf16[8,3,8,640]{3,2,1,0:T(8,128)(2,1)}), bf16[8,3,8,640]{3,2,1,0:T(8,128)(2,1)S(1)}, u32[]{:S(2)}, u32[]{:S(2)}) %all-to-all-start.7) | async-done | bytes 245792 | tf_op jit(solution)/shard_map/all_to_all | solution.py:160
  265.8 2.2 fusion.1
  (181 shorter events, 48.2 us)
Async XLA Ops:
  1.9 9.4 %collective-permute-start = (s32[8]{0:T(128)S(1)}, s32[8]{0:T(128)S(1)}, u32[]{:S(2)}, u32[]{:S(2)}) collective-permute-start(s32[8]{0:T(128)S(1)} %get-tuple-element.94), channel_id=1, source_target_pairs={{0,384},{128,0},{256,128},{384,256},{1,385},{129,1},{257,129},{385... | collective-permute-start | bytes 104 | tf_op jit(solution)/shard_map/ppermute | solution.py:112
  7.7 30.8 %collective-permute-start.1 = (bf16[2,512,896]{2,1,0:T(8,128)(2,1)}, bf16[2,512,896]{2,1,0:T(8,128)(2,1)S(1)}, u32[]{:S(2)}, u32[]{:S(2)}) collective-permute-start(bf16[2,512,896]{2,1,0:T(8,128)(2,1)} %pad_maximum_fusion), channel_id=1, source_target_pairs={{0,0},{17,17},{1,16},{16,1},{2,2},{19,19},{3,18},{18,3},{4,4},{21,... | collective-permute-start | bytes 5505032 | tf_op jit(solution)/shard_map/ppermute | solution.py:40
  9.8 62.1 %copy-start.5 = (pred[128]{0:T(512)(128)(4,1)}, pred[128]{0:T(512)(128)(4,1)S(1)}, u32[]{:S(2)}) copy-start(pred[128]{0:T(512)(128)(4,1)S(1)} %get-tuple-element.110) | copy-start | bytes 388
  9.8 62.1 %copy-start.20 = (pred[128]{0:T(512)(128)(4,1)}, pred[128]{0:T(512)(128)(4,1)S(1)}, u32[]{:S(2)}) copy-start(pred[128]{0:T(512)(128)(4,1)S(1)} %get-tuple-element.109) | copy-start | bytes 388
  37.4 45.2 %copy-start.4 = (bf16[64,640]{1,0:T(8,128)(2,1)}, bf16[64,640]{1,0:T(8,128)(2,1)S(1)}, u32[]{:S(2)}) copy-start(bf16[64,640]{1,0:T(8,128)(2,1)S(1)} %get-tuple-element.70) | copy-start | bytes 245764
  38.4 32.3 %collective-permute-start.2 = (bf16[2,512,896]{2,1,0:T(8,128)(2,1)S(1)}, bf16[2,512,896]{2,1,0:T(8,128)(2,1)}, u32[]{:S(2)}, u32[]{:S(2)}) collective-permute-start(bf16[2,512,896]{2,1,0:T(8,128)(2,1)S(1)} %collective-permute-done.1), channel_id=1, source_target_pairs={{0,1},{1,0},{2,3},{3,2},{4,5},{5,4},{6,7},{7,6},{8,9},{9,8},{10,11... | collective-permute-start | bytes 5505032 | tf_op jit(solution)/shard_map/ppermute | solution.py:44
  43.6 27.2 %all-to-all-start.1 = ((bf16[16,32,512]{2,1,0:T(8,128)(2,1)}), bf16[16,32,512]{2,1,0:T(8,128)(2,1)S(1)}, u32[]{:S(2)}, u32[]{:S(2)}) async-start(bf16[16,32,512]{2,1,0:T(8,128)(2,1)} %broadcast_in_dim.364), calls=%async_computation.1 | async-start | bytes 1048576 | tf_op jit(solution)/shard_map/all_to_all | solution.py:56
  54.7 21.9 %collective-permute-start.3 = (bf16[896,512]{1,0:T(8,128)(2,1)}, bf16[896,512]{1,0:T(8,128)(2,1)}, u32[]{:S(2)}, u32[]{:S(2)}) collective-permute-start(bf16[896,512]{1,0:T(8,128)(2,1)} %bitcast.193), channel_id=1, source_target_pairs={{0,0},{17,17},{1,16},{16,1},{2,2},{19,19},{3,18},{18,3},{4,4},{21,... | collective-permute-start | bytes 2752520 | tf_op jit(solution)/shard_map/ppermute | solution.py:40
  76.6 21.4 %all-to-all-start.2 = ((bf16[4,64,1920]{2,1,0:T(8,128)(2,1)}), bf16[4,64,1920]{2,1,0:T(8,128)(2,1)S(1)}, u32[]{:S(2)}, u32[]{:S(2)}) async-start(bf16[4,64,1920]{2,1,0:T(8,128)(2,1)} %bitcast.19), calls=%async_computation.2 | async-start | bytes 1966080 | tf_op jit(solution)/shard_map/all_to_all | solution.py:77
  80.1 46.2 %collective-permute-start.5 = (bf16[64,4096]{1,0:T(8,128)(2,1)S(1)}, bf16[64,4096]{1,0:T(8,128)(2,1)}, u32[]{:S(2)}, u32[]{:S(2)}) collective-permute-start(bf16[64,4096]{1,0:T(8,128)(2,1)S(1)} %bitcast.175), channel_id=1, source_target_pairs={{0,128},{128,256},{256,384},{1,129},{129,257},{257,385},{2,130},{1... | collective-permute-start | bytes 1572872 | tf_op jit(solution)/shard_map/ppermute | solution.py:139
  83.3 18.1 %collective-permute-start.4 = (bf16[896,512]{1,0:T(8,128)(2,1)}, bf16[896,512]{1,0:T(8,128)(2,1)}, u32[]{:S(2)}, u32[]{:S(2)}) collective-permute-start(bf16[896,512]{1,0:T(8,128)(2,1)} %collective-permute-done.3), channel_id=1, source_target_pairs={{0,1},{1,0},{2,3},{3,2},{4,5},{5,4},{6,7},{7,6},{8,9},{9,8},{10,11... | collective-permute-start | bytes 2752520 | tf_op jit(solution)/shard_map/ppermute | solution.py:44
  126.3 20.8 %all-to-all-start.3 = ((bf16[16,32,512]{2,1,0:T(8,128)(2,1)}), bf16[16,32,512]{2,1,0:T(8,128)(2,1)S(1)}, u32[]{:S(2)}, u32[]{:S(2)}) async-start(bf16[16,32,512]{2,1,0:T(8,128)(2,1)} %bitcast.25), calls=%async_computation.3 | async-start | bytes 1048576 | tf_op jit(solution)/shard_map/all_to_all | solution.py:93
  135.7 36.2 %copy-start.26 = (s32[64]{0:T(128)}, s32[64]{0:T(128)S(1)}, u32[]{:S(2)}) copy-start(s32[64]{0:T(128)S(1)} %select_reduce_fusion) | copy-start | bytes 772
  148.1 5.9 %collective-permute-start.7 = (bf16[32,512]{1,0:T(8,128)(2,1)S(1)}, bf16[32,512]{1,0:T(8,128)(2,1)S(1)}, u32[]{:S(2)}, u32[]{:S(2)}) collective-permute-start(bf16[32,512]{1,0:T(8,128)(2,1)S(1)} %fusion.8), channel_id=1, source_target_pairs={{0,128},{128,256},{256,384},{384,0},{1,129},{129,257},{257,385},{3... | collective-permute-start | bytes 98312 | tf_op jit(solution)/shard_map/ppermute | solution.py:147
  177.8 22.6 %all-to-all-start.5 = ((bf16[4,64,1920]{2,1,0:T(8,128)(2,1)}), bf16[4,64,1920]{2,1,0:T(8,128)(2,1)S(1)}, u32[]{:S(2)}, u32[]{:S(2)}) async-start(bf16[4,64,1920]{2,1,0:T(8,128)(2,1)} %bitcast.40), calls=%async_computation.5 | async-start | bytes 1966080 | tf_op jit(solution)/shard_map/all_to_all | solution.py:77
  223.1 13.9 %copy-start.16 = (pred[64]{0:T(512)(128)(4,1)S(1)}, pred[64]{0:T(512)(128)(4,1)}, u32[]{:S(2)}) copy-start(pred[64]{0:T(512)(128)(4,1)} %copy-done.14) | copy-start | bytes 196
  223.1 13.9 %copy-start.19 = (s32[64]{0:T(128)S(1)}, s32[64]{0:T(128)}, u32[]{:S(2)}) copy-start(s32[64]{0:T(128)} %copy-done.17) | copy-start | bytes 772
  225.6 28.2 %copy-start.13 = (s32[8]{0:T(128)S(1)}, s32[8]{0:T(128)}, u32[]{:S(2)}) copy-start(s32[8]{0:T(128)} %get-tuple-element.92) | copy-start | bytes 100
  225.6 21.8 %all-to-all-start.6 = ((bf16[16,32,512]{2,1,0:T(8,128)(2,1)}), bf16[16,32,512]{2,1,0:T(8,128)(2,1)S(1)}, u32[]{:S(2)}, u32[]{:S(2)}) async-start(bf16[16,32,512]{2,1,0:T(8,128)(2,1)} %bitcast.46), calls=%async_computation.6 | async-start | bytes 1048576 | tf_op jit(solution)/shard_map/all_to_all | solution.py:93
  237.0 27.3 %copy-start.31 = (s32[8]{0:T(128)S(1)}, s32[8]{0:T(128)}, u32[]{:S(2)}) copy-start(s32[8]{0:T(128)} %get-tuple-element.90) | copy-start | bytes 100
  237.0 27.4 %copy-start.29 = (s32[8]{0:T(128)S(1)}, s32[8]{0:T(128)}, u32[]{:S(2)}) copy-start(s32[8]{0:T(128)} %copy-done.28) | copy-start | bytes 100
  237.3 8.0 %collective-permute-start.6 = (bf16[128,640]{1,0:T(8,128)(2,1)S(1)}, bf16[128,640]{1,0:T(8,128)(2,1)S(1)}, u32[]{:S(2)}, u32[]{:S(2)}) collective-permute-start(bf16[128,640]{1,0:T(8,128)(2,1)S(1)} %pad_maximum_fusion.7), channel_id=1, source_target_pairs={{0,128},{128,256},{256,384},{384,0},{1,129},{129,257},{257,385},{3... | collective-permute-start | bytes 491528 | tf_op jit(solution)/shard_map/ppermute | solution.py:150
  245.5 20.3 %copy-start.3 = (bf16[64,4096]{1,0:T(8,128)(2,1)S(1)}, bf16[64,4096]{1,0:T(8,128)(2,1)}, u32[]{:S(2)}) copy-start(bf16[64,4096]{1,0:T(8,128)(2,1)} %param.11) | copy-start | bytes 1572868
  248.4 15.7 %all-to-all-start.7 = ((bf16[8,3,8,640]{3,2,1,0:T(8,128)(2,1)}), bf16[8,3,8,640]{3,2,1,0:T(8,128)(2,1)S(1)}, u32[]{:S(2)}, u32[]{:S(2)}) async-start(bf16[8,3,8,640]{3,2,1,0:T(8,128)(2,1)} %pad_maximum_fusion.5), calls=%async_computation.7 | async-start | bytes 491520 | tf_op jit(solution)/shard_map/all_to_all | solution.py:160
  (22 other events, 132.0 us)

commit v3 on v2

--- a/solution.py
+++ b/solution.py
@@ -48,16 +48,15 @@
     return lax.optimization_barrier((x, *others))
 
 
-def tick(v, gains, scorers, w1, w2, base, z, core):
-    rows = v.shape[0]
+def tick(v, gains, scorers, wg, wu, wd, late, z, core):
+    rows, width = v.shape
     n_z = lax.axis_size("z")
     n_q = lax.axis_size("q")
-    width = v.shape[1]
+    everyone = n_z * rows
+    chunk = everyone // n_q
     g = lax.all_to_all(
         jnp.broadcast_to(v[None], (2 * n_z, rows, width)), PLANE, 0, 0, tiled=True
-    ).reshape(2, n_z * rows, width)
-    g, *w1 = after(g, *w1)
-    wg, wu = [w[0] for w in w1], [w[1] for w in w1]
+    ).reshape(2, everyone, width)
     ss = 0.0
     dot = 0.0
     gate = 0.0
@@ -69,30 +68,28 @@
         x = (vk * gains[k]).astype(BF)
         gate = gate + jnp.dot(x, wg[k], preferred_element_type=F32)
         up = up + jnp.dot(x, wu[k], preferred_element_type=F32)
-    everyone = n_z * rows
     extra = lanes(parts3(ss) + parts3(dot), everyone)
     part = jnp.concatenate([gate.astype(BF), up.astype(BF), extra], axis=1)
     units = gate.shape[1]
-    part, w2_own = after(part, w2[0])
-    part = lax.all_to_all(part.reshape(n_q, everyone // n_q, -1), "q", 0, 0, tiled=True)
+    part, *late = after(part, *late)
+    part = lax.all_to_all(part.reshape(n_q, chunk, -1), "q", 0, 0, tiled=True)
     total = jnp.sum(part.astype(F32), axis=0)
     ext = total[:, 2 * units :]
     inv = lax.rsqrt((ext[:, 0] + ext[:, 1] + ext[:, 2]) / (8 * width) + 1e-05)[:, None]
     weight = jax.nn.sigmoid(ext[:, 3] + ext[:, 4] + ext[:, 5])
     hidden = (jax.nn.silu(total[:, :units] * inv) * (total[:, units : 2 * units] * inv)).astype(BF)
-    hidden = jnp.concatenate([hidden, lanes(parts3(weight), everyone // n_q)], axis=1)
-    hidden, w2_other = after(hidden, sibling(w2_own) if len(w2) == 1 else w2[1])
-    wd = (w2_own, w2_other)
-    hidden = lax.all_gather(hidden, "q", axis=0, tiled=True)
-    own = lax.dynamic_slice_in_dim(hidden[:, units:], z * rows, rows, 0).astype(F32)
+    hidden = jnp.concatenate([hidden, lanes(parts3(weight), chunk)[:, :64]], axis=1)
+    hidden = lax.all_gather(hidden, DP, axis=0, tiled=True).reshape(n_q, 2, chunk, -1)
+    own = lax.dynamic_slice(hidden[:, 0, :, units:], (z * rows // chunk, z * rows % chunk, 0), (1, rows, 64))
+    own = own[0].astype(F32)
     weight = own[:, 0] + own[:, 1] + own[:, 2]
-    hidden = hidden[:, :units]
-    outs = [jnp.dot(hidden, wd[k], preferred_element_type=F32).astype(BF) for k in range(2)]
-    out = jnp.stack([jnp.where(core == 0, outs[0], outs[1]), jnp.where(core == 0, outs[1], outs[0])])
-    out, base = after(out, base)
-    out = lax.all_to_all(out.reshape(2 * n_z, rows, width), PLANE, 0, 0, tiled=True)
+    out = 0.0
+    for k in range(2):
+        hk = lax.dynamic_index_in_dim(hidden[..., :units], core ^ k, 1, keepdims=False)
+        out = out + jnp.dot(hk.reshape(everyone, units), wd[k], preferred_element_type=F32)
+    out = lax.all_to_all(out.astype(BF).reshape(n_z, rows, width), "z", 0, 0, tiled=True)
     block_out = jnp.sum(out.astype(F32), axis=0).astype(BF).astype(F32)
-    return (v.astype(F32) + weight[:, None] * block_out).astype(BF), wd, base
+    return (v.astype(F32) + weight[:, None] * block_out).astype(BF), late
 
 
 def local(pending, arriving, gain, scorer, w_gate, w_up, w_down, lists):
@@ -116,6 +113,7 @@
     both = jnp.concatenate([v1, b2], axis=0).reshape(2 * cap, n_dp, cut).transpose(1, 0, 2)
     codes = lanes([jnp.concatenate([e1, e2_next]).astype(BF)], 2 * cap)
     both = jnp.concatenate([both, jnp.broadcast_to(codes[None], (n_dp, 2 * cap, 128))], axis=2)
+    both, wg = after(both, cross(w_gate[0]))
     got = lax.all_to_all(both, DP, 0, 0, tiled=True)
     slots1 = got[:, :cap].reshape(n_dp * cap, -1)
     slots2 = got[:, cap:].reshape(n_dp * cap, -1)
@@ -131,10 +129,10 @@
     v1c = pick(comp1, slots1[:, :cut])
     b2c = pick(comp2, slots2[:, :cut])
 
-    w1 = cross(jnp.stack([w_gate[0], w_up[0]]))
-    v1c, w1 = after(v1c, w1)
-    w1 = (w1, sibling(w1))
-    w2 = cross(w_down[0])
+    v1c, wu = after(v1c, cross(w_up[0]))
+    wg = (wg, sibling(wg))
+    wu = (wu, sibling(wu))
+    wd = (w_down[0], sibling(w_down[0]))
     ahead = [(i, (i + 1) % n_seg) for i in range(n_seg)]
     base = lax.ppermute(pending, "segment", ahead[:-1])
 
@@ -142,7 +140,7 @@
         return [lax.dynamic_slice_in_dim(row[0], (2 * q + (core ^ k)) * cut, cut, 0) for k in range(2)]
 
     gains, scorers = slices(gain), slices(scorer)
-    up1, w2, base = tick(v1c, gains, scorers, w1, (w2,), base, z, core)
+    up1, _ = tick(v1c, gains, scorers, wg, wu, wd, [], z, core)
     v2n = jnp.where(has, pick(hit, up1), b2c)
     v2c = lax.ppermute(v2n, "segment", ahead)
     up1_slots = jnp.concatenate([pick(comp1.T, up1), slots1[:, cut:]], axis=1)
@@ -152,7 +150,7 @@
         "segment",
         ahead,
     )
-    up2, _, base = tick(v2c, gains, scorers, w1, w2, base, z, core)
+    up2, (before, base) = tick(v2c, gains, scorers, wg, wu, wd, [before, base], z, core)
     own_comp2 = before[n_dp * cap :, :compact]
     before = before[: n_dp * cap]
     up2_slots = jnp.concatenate([pick(own_comp2, up2), slots1[:, cut:]], axis=1)

time: 271 us -> 270 us (level)
  local copies, waits for them, and re-layouts: 5.4 us -> 9.84 us
  matrix products: 23.4 us -> 19.3 us
  other arithmetic: 17.7 us -> 14.5 us
  starting transfers between devices: 75.9 us -> 78.8 us
    all_to_all x2 -> x1, blocking collectives: 42.4 us -> 23.4 us  [tick(): part = lax.all_to_all(part.reshape(n_q, chunk, -1), 'q', 0, 0, tiled=True)]
    all_gather x2, blocking collectives: 41 us -> 58.4 us  [tick(): lax.all_gather(hidden, DP, axis=0, tiled=True).reshape(n_q, 2, chunk, -1)]
    all_to_all x1 -> x2, starting transfers between devices: 11.1 us -> 19.8 us  [tick(): lax.all_to_all(jnp.broadcast_to(v[None], (2 * n_z, rows, width)), PLANE,...]
    ppermute x2, starting transfers between devices: 10.5 us -> 3.67 us  [cross(): return lax.ppermute(w, ('h', 'core'), [(0, 0), (3, 3), (1, 2), (2, 1)])]
    another operation x3 -> x0, other arithmetic: 4.58 us -> none  [the longest x1 2.9 us: local(): w1 = cross(jnp.stack([w_gate[0], w_up[0]]))]
    all_to_all x1 -> x2, waiting for transfers between devices: 6.93 us -> 10 us  [tick(): lax.all_to_all(jnp.broadcast_to(v[None], (2 * n_z, rows, width)), PLANE,...]
    ppermute x1, waiting for transfers between devices: 2.82 us -> 0.01 us  [local(): lax.ppermute(jnp.concatenate([up1_slots, jnp.concatenate([comp2_slots, jn...]
    ppermute x2 -> x3, starting transfers between devices: 6.17 us -> 6.24 us  [sibling(): return lax.ppermute(w, 'core', [(0, 1), (1, 0)])]
  transfers between devices with their start and end apart: 14 -> 16, of which waited for: 9 -> 9; matrix products, arithmetic and copies ran while one was open for 10% -> 8% of each run, Pallas kernels for 0% -> 0%
where the time goes in v3:
time: 270 us; the launch traced here: 268 us
  blocking collectives  81.8 us (30%)
  starting transfers between devices  78.8 us (29%)
  waiting for transfers between devices  62.2 us (23%)
  matrix products  19.3 us (7%)
  other arithmetic  14.5 us (5%)
  local copies, waits for them, and re-layouts  9.84 us (4%)
    all_gather x2, blocking collectives, tick(): lax.all_gather(hidden, DP, axis=0, tiled=True).reshape(n_q, 2, chunk, -1)  58.4 us
    all_to_all x1, blocking collectives, tick(): part = lax.all_to_all(part.reshape(n_q, chunk, -1), 'q', 0, 0, tiled=True)  23.4 us
    all_to_all x2, starting transfers between devices, tick(): lax.all_to_all(jnp.broadcast_to(v[None], (2 * n_z, rows, width)), PLANE,...  19.8 us
    all_to_all x2, waiting for transfers between devices, tick(): lax.all_to_all(out.astype(BF).reshape(n_z, rows, width), 'z', 0, 0, tiled...  18.1 us
    all_to_all x2, starting transfers between devices, tick(): lax.all_to_all(out.astype(BF).reshape(n_z, rows, width), 'z', 0, 0, tiled...  13.1 us
    all_to_all x1, waiting for transfers between devices, tick(): part = lax.all_to_all(part.reshape(n_q, chunk, -1), 'q', 0, 0, tiled=True)  12.7 us
    all_to_all x1, starting transfers between devices, local(): got = lax.all_to_all(both, DP, 0, 0, tiled=True)  12.5 us
    all_to_all x1, waiting for transfers between devices, local(): back = lax.all_to_all(back, DP, 0, 0, tiled=True)  10.2 us
  transfers between devices with their start and end apart: 16, of which 9 were waited for; matrix products, arithmetic and copies ran while one was open for 8% of the time, Pallas kernels for 0%

profile of v3, /device:TPU:6, one launch (start us, length us, event | category | flops | bytes accessed | tf_op | source)
XLA Modules:
  0.0 268.2 jit_solution(4505337831535126493)
XLA Ops:
  2.0 2.7 %collective-permute-start = (s32[8]{0:T(128)S(1)}, s32[8]{0:T(128)S(1)}, u32[]{:S(2)}, u32[]{:S(2)}) collective-permute-start(s32[8]{0:T(128)S(1)} %get-tuple-element.68), channel_id=1, source_target_pairs={{0,384},{128,0},{256,128},{384,256},{1,385},{129,1},{257,129},{385... | collective-permute-start | bytes 104 | tf_op jit(solution)/shard_map/ppermute | solution.py:109
  13.4 12.5 %all-to-all-start = ((bf16[8,16,640]{2,1,0:T(8,128)(2,1)}), bf16[8,16,640]{2,1,0:T(8,128)(2,1)S(1)}, u32[]{:S(2)}, u32[]{:S(2)}) async-start(bf16[8,16,640]{2,1,0:T(8,128)(2,1)} %pad_maximum_fusion.3), calls=%async_computation | async-start | bytes 327680 | tf_op jit(solution)/shard_map/all_to_all | solution.py:117
  27.8 8.7 %all-to-all-done = bf16[8,16,640]{2,1,0:T(8,128)(2,1)S(1)} async-done(((bf16[8,16,640]{2,1,0:T(8,128)(2,1)}), bf16[8,16,640]{2,1,0:T(8,128)(2,1)S(1)}, u32[]{:S(2)}, u32[]{:S(2)}) %all-to-all-start) | async-done | bytes 163872 | tf_op jit(solution)/shard_map/all_to_all | solution.py:117
  38.5 16.2 %all-to-all-start.1 = ((bf16[16,32,512]{2,1,0:T(8,128)(2,1)}), bf16[16,32,512]{2,1,0:T(8,128)(2,1)S(1)}, u32[]{:S(2)}, u32[]{:S(2)}) async-start(bf16[16,32,512]{2,1,0:T(8,128)(2,1)} %broadcast_in_dim.364), calls=%async_computation.1 | async-start | bytes 1048576 | tf_op jit(solution)/shard_map/all_to_all | solution.py:57
  54.7 1.9 collective-permute-start.3
  56.6 2.4 collective-permute-start.4
  60.0 8.2 %all-to-all-done.1 = bf16[16,32,512]{2,1,0:T(8,128)(2,1)S(1)} async-done(((bf16[16,32,512]{2,1,0:T(8,128)(2,1)}), bf16[16,32,512]{2,1,0:T(8,128)(2,1)S(1)}, u32[]{:S(2)}, u32[]{:S(2)}) %all-to-all-start.1) | async-done | bytes 524320 | tf_op jit(solution)/shard_map/all_to_all | solution.py:57
  73.0 5.9 %all-to-all-start.2 = ((bf16[4,64,1920]{2,1,0:T(8,128)(2,1)}), bf16[4,64,1920]{2,1,0:T(8,128)(2,1)S(1)}, u32[]{:S(2)}, u32[]{:S(2)}) async-start(bf16[4,64,1920]{2,1,0:T(8,128)(2,1)} %bitcast.16), calls=%async_computation.2 | async-start | bytes 1966080 | tf_op jit(solution)/shard_map/all_to_all | solution.py:75
  78.9 1.9 collective-permute-start.5
  84.0 12.7 %all-to-all-done.2 = bf16[4,64,1920]{2,1,0:T(8,128)(2,1)S(1)} async-done(((bf16[4,64,1920]{2,1,0:T(8,128)(2,1)}), bf16[4,64,1920]{2,1,0:T(8,128)(2,1)S(1)}, u32[]{:S(2)}, u32[]{:S(2)}) %all-to-all-start.2) | async-done | bytes 983072 | tf_op jit(solution)/shard_map/all_to_all | solution.py:75
  97.6 31.9 %all_gather.6 = bf16[512,960]{1,0:T(8,128)(2,1)S(1)} all-gather(bf16[64,960]{1,0:T(8,128)(2,1)S(1)} %pad_maximum_fusion.6), channel_id=1, replica_groups=mesh['segment'=4,'q'=4,'h'=2,'z'=8,'core'=2] {'q','h'}, dimensions={0}, use_global_device_ids=true | all-gather | bytes 1105920 | tf_op jit(solution)/shard_map/all_gather | solution.py:82
  130.1 2.3 fusion.6
  132.4 7.6 %all-to-all-start.3 = ((bf16[8,32,512]{2,1,0:T(8,128)(2,1)}), bf16[8,32,512]{2,1,0:T(8,128)(2,1)}, u32[]{:S(2)}, u32[]{:S(2)}) async-start(bf16[8,32,512]{2,1,0:T(8,128)(2,1)} %bitcast.157), calls=%async_computation.3 | async-start | bytes 524288 | tf_op jit(solution)/shard_map/all_to_all | solution.py:90
  141.9 8.7 %all-to-all-done.3 = bf16[8,32,512]{2,1,0:T(8,128)(2,1)} async-done(((bf16[8,32,512]{2,1,0:T(8,128)(2,1)}), bf16[8,32,512]{2,1,0:T(8,128)(2,1)}, u32[]{:S(2)}, u32[]{:S(2)}) %all-to-all-start.3) | async-done | bytes 262176 | tf_op jit(solution)/shard_map/all_to_all | solution.py:90
  153.2 4.3 %collective-permute-start.6 = (bf16[32,512]{1,0:T(8,128)(2,1)S(1)}, bf16[32,512]{1,0:T(8,128)(2,1)S(1)}, u32[]{:S(2)}, u32[]{:S(2)}) collective-permute-start(bf16[32,512]{1,0:T(8,128)(2,1)S(1)} %fusion.8), channel_id=1, source_target_pairs={{0,128},{128,256},{256,384},{384,0},{1,129},{129,257},{257,385},{3... | collective-permute-start | bytes 98312 | tf_op jit(solution)/shard_map/ppermute | solution.py:145
  160.0 3.6 %all-to-all-start.4 = ((bf16[16,32,512]{2,1,0:T(8,128)(2,1)}), bf16[16,32,512]{2,1,0:T(8,128)(2,1)S(1)}, u32[]{:S(2)}, u32[]{:S(2)}) async-start(bf16[16,32,512]{2,1,0:T(8,128)(2,1)} %broadcast_in_dim.387), calls=%async_computation.4 | async-start | bytes 1048576 | tf_op jit(solution)/shard_map/all_to_all | solution.py:57
  166.7 5.5 %collective-permute-start.7 = (bf16[128,640]{1,0:T(8,128)(2,1)}, bf16[128,640]{1,0:T(8,128)(2,1)}, u32[]{:S(2)}, u32[]{:S(2)}) collective-permute-start(bf16[128,640]{1,0:T(8,128)(2,1)} %pad_maximum_fusion.4), channel_id=1, source_target_pairs={{0,128},{128,256},{256,384},{384,0},{1,129},{129,257},{257,385},{3... | collective-permute-start | bytes 491528 | tf_op jit(solution)/shard_map/ppermute | solution.py:148
  179.5 23.4 %all_to_all.40 = bf16[4,64,1920]{2,1,0:T(8,128)(2,1)S(1)} all-to-all(bf16[4,64,1920]{2,1,0:T(8,128)(2,1)S(1)} %bitcast.151), channel_id=1, replica_groups=mesh['segment'=4,'q'=4,'h'=2,'z'=8,'core'=2] {'q'}, dimensions={0} | all-to-all | bytes 1966080 | tf_op jit(solution)/shard_map/all_to_all | solution.py:75
  203.8 26.5 %all_gather.7 = bf16[512,960]{1,0:T(8,128)(2,1)S(1)} all-gather(bf16[64,960]{1,0:T(8,128)(2,1)S(1)} %pad_maximum_fusion.7), channel_id=1, replica_groups=mesh['segment'=4,'q'=4,'h'=2,'z'=8,'core'=2] {'q','h'}, dimensions={0}, use_global_device_ids=true | all-gather | bytes 1105920 | tf_op jit(solution)/shard_map/all_gather | solution.py:82
  230.9 2.3 fusion.7
  233.2 5.5 %all-to-all-start.6 = ((bf16[8,32,512]{2,1,0:T(8,128)(2,1)}), bf16[8,32,512]{2,1,0:T(8,128)(2,1)S(1)}, u32[]{:S(2)}, u32[]{:S(2)}) async-start(bf16[8,32,512]{2,1,0:T(8,128)(2,1)} %bitcast.46), calls=%async_computation.6 | async-start | bytes 524288 | tf_op jit(solution)/shard_map/all_to_all | solution.py:90
  239.9 9.3 %all-to-all-done.6 = bf16[8,32,512]{2,1,0:T(8,128)(2,1)S(1)} async-done(((bf16[8,32,512]{2,1,0:T(8,128)(2,1)}), bf16[8,32,512]{2,1,0:T(8,128)(2,1)S(1)}, u32[]{:S(2)}, u32[]{:S(2)}) %all-to-all-start.6) | async-done | bytes 262176 | tf_op jit(solution)/shard_map/all_to_all | solution.py:90
  251.0 3.8 %all-to-all-start.7 = ((bf16[8,3,8,640]{3,2,1,0:T(8,128)(2,1)}), bf16[8,3,8,640]{3,2,1,0:T(8,128)(2,1)S(1)}, u32[]{:S(2)}, u32[]{:S(2)}) async-start(bf16[8,3,8,640]{3,2,1,0:T(8,128)(2,1)} %pad_maximum_fusion.2), calls=%async_computation.7 | async-start | bytes 491520 | tf_op jit(solution)/shard_map/all_to_all | solution.py:158
  254.9 10.2 %all-to-all-done.7 = bf16[8,3,8,640]{3,2,1,0:T(8,128)(2,1)S(1)} async-done(((bf16[8,3,8,640]{3,2,1,0:T(8,128)(2,1)}), bf16[8,3,8,640]{3,2,1,0:T(8,128)(2,1)S(1)}, u32[]{:S(2)}, u32[]{:S(2)}) %all-to-all-start.7) | async-done | bytes 245792 | tf_op jit(solution)/shard_map/all_to_all | solution.py:158
  (231 shorter events, 48.3 us)
Async XLA Ops:
  2.0 9.3 %collective-permute-start = (s32[8]{0:T(128)S(1)}, s32[8]{0:T(128)S(1)}, u32[]{:S(2)}, u32[]{:S(2)}) collective-permute-start(s32[8]{0:T(128)S(1)} %get-tuple-element.68), channel_id=1, source_target_pairs={{0,384},{128,0},{256,128},{384,256},{1,385},{129,1},{257,129},{385... | collective-permute-start | bytes 104 | tf_op jit(solution)/shard_map/ppermute | solution.py:109
  4.7 8.7 %collective-permute-start.1 = (bf16[512,896]{1,0:T(8,128)(2,1)}, bf16[512,896]{1,0:T(8,128)(2,1)S(1)}, u32[]{:S(2)}, u32[]{:S(2)}) collective-permute-start(bf16[512,896]{1,0:T(8,128)(2,1)} %bitcast.181), channel_id=1, source_target_pairs={{0,0},{17,17},{1,16},{16,1},{2,2},{19,19},{3,18},{18,3},{4,4},{21,... | collective-permute-start | bytes 2752520 | tf_op jit(solution)/shard_map/ppermute | solution.py:40
  6.5 65.1 %copy-start.23 = (pred[128]{0:T(512)(128)(4,1)}, pred[128]{0:T(512)(128)(4,1)S(1)}, u32[]{:S(2)}) copy-start(pred[128]{0:T(512)(128)(4,1)S(1)} %iota_compare_fusion.13) | copy-start | bytes 388
  13.4 55.2 %copy-start.2 = (bf16[512,896]{1,0:T(8,128)(2,1)}, bf16[512,896]{1,0:T(8,128)(2,1)S(1)}, u32[]{:S(2)}) copy-start(bf16[512,896]{1,0:T(8,128)(2,1)S(1)} %collective-permute-done.1) | copy-start | bytes 2752516
  13.4 23.0 %all-to-all-start = ((bf16[8,16,640]{2,1,0:T(8,128)(2,1)}), bf16[8,16,640]{2,1,0:T(8,128)(2,1)S(1)}, u32[]{:S(2)}, u32[]{:S(2)}) async-start(bf16[8,16,640]{2,1,0:T(8,128)(2,1)} %pad_maximum_fusion.3), calls=%async_computation | async-start | bytes 327680 | tf_op jit(solution)/shard_map/all_to_all | solution.py:117
  25.9 11.4 %collective-permute-start.2 = (bf16[512,896]{1,0:T(8,128)(2,1)}, bf16[512,896]{1,0:T(8,128)(2,1)S(1)}, u32[]{:S(2)}, u32[]{:S(2)}) collective-permute-start(bf16[512,896]{1,0:T(8,128)(2,1)} %bitcast.182), channel_id=1, source_target_pairs={{0,0},{17,17},{1,16},{16,1},{2,2},{19,19},{3,18},{18,3},{4,4},{21,... | collective-permute-start | bytes 2752520 | tf_op jit(solution)/shard_map/ppermute | solution.py:40
  36.5 45.1 %copy-start.10 = (bf16[64,640]{1,0:T(8,128)(2,1)}, bf16[64,640]{1,0:T(8,128)(2,1)S(1)}, u32[]{:S(2)}) copy-start(bf16[64,640]{1,0:T(8,128)(2,1)S(1)} %get-tuple-element.44) | copy-start | bytes 245764
  37.4 114.3 %copy-start.11 = (bf16[32,512]{1,0:T(8,128)(2,1)}, bf16[32,512]{1,0:T(8,128)(2,1)S(1)}, u32[]{:S(2)}) copy-start(bf16[32,512]{1,0:T(8,128)(2,1)S(1)} %convolution_convert_fusion.6) | copy-start | bytes 98308
  38.5 29.7 %all-to-all-start.1 = ((bf16[16,32,512]{2,1,0:T(8,128)(2,1)}), bf16[16,32,512]{2,1,0:T(8,128)(2,1)S(1)}, u32[]{:S(2)}, u32[]{:S(2)}) async-start(bf16[16,32,512]{2,1,0:T(8,128)(2,1)} %broadcast_in_dim.364), calls=%async_computation.1 | async-start | bytes 1048576 | tf_op jit(solution)/shard_map/all_to_all | solution.py:57
  54.7 5.2 %collective-permute-start.3 = (bf16[512,896]{1,0:T(8,128)(2,1)S(1)}, bf16[512,896]{1,0:T(8,128)(2,1)S(1)}, u32[]{:S(2)}, u32[]{:S(2)}) collective-permute-start(bf16[512,896]{1,0:T(8,128)(2,1)S(1)} %collective-permute-done.1), channel_id=1, source_target_pairs={{0,1},{1,0},{2,3},{3,2},{4,5},{5,4},{6,7},{7,6},{8,9},{9,8},{10,11... | collective-permute-start | bytes 2752520 | tf_op jit(solution)/shard_map/ppermute | solution.py:44
  56.6 12.5 %collective-permute-start.4 = (bf16[512,896]{1,0:T(8,128)(2,1)}, bf16[512,896]{1,0:T(8,128)(2,1)}, u32[]{:S(2)}, u32[]{:S(2)}) collective-permute-start(bf16[512,896]{1,0:T(8,128)(2,1)} %copy-done.6), channel_id=1, source_target_pairs={{0,1},{1,0},{2,3},{3,2},{4,5},{5,4},{6,7},{7,6},{8,9},{9,8},{10,11... | collective-permute-start | bytes 2752520 | tf_op jit(solution)/shard_map/ppermute | solution.py:44
  73.0 23.7 %all-to-all-start.2 = ((bf16[4,64,1920]{2,1,0:T(8,128)(2,1)}), bf16[4,64,1920]{2,1,0:T(8,128)(2,1)S(1)}, u32[]{:S(2)}, u32[]{:S(2)}) async-start(bf16[4,64,1920]{2,1,0:T(8,128)(2,1)} %bitcast.16), calls=%async_computation.2 | async-start | bytes 1966080 | tf_op jit(solution)/shard_map/all_to_all | solution.py:75
  78.9 51.2 %collective-permute-start.5 = (bf16[896,512]{1,0:T(8,128)(2,1)S(1)}, bf16[896,512]{1,0:T(8,128)(2,1)}, u32[]{:S(2)}, u32[]{:S(2)}) collective-permute-start(bf16[896,512]{1,0:T(8,128)(2,1)S(1)} %bitcast.152), channel_id=1, source_target_pairs={{0,1},{1,0},{2,3},{3,2},{4,5},{5,4},{6,7},{7,6},{8,9},{9,8},{10,11... | collective-permute-start | bytes 2752520 | tf_op jit(solution)/shard_map/ppermute | solution.py:44
  132.4 18.2 %all-to-all-start.3 = ((bf16[8,32,512]{2,1,0:T(8,128)(2,1)}), bf16[8,32,512]{2,1,0:T(8,128)(2,1)}, u32[]{:S(2)}, u32[]{:S(2)}) async-start(bf16[8,32,512]{2,1,0:T(8,128)(2,1)} %bitcast.157), calls=%async_computation.3 | async-start | bytes 524288 | tf_op jit(solution)/shard_map/all_to_all | solution.py:90
  141.9 23.0 %copy-start.34 = (pred[64]{0:T(512)(128)(4,1)S(1)}, pred[64]{0:T(512)(128)(4,1)}, u32[]{:S(2)}) copy-start(pred[64]{0:T(512)(128)(4,1)} %copy-done.32) | copy-start | bytes 196
  141.9 23.0 %copy-start.49 = (s32[64]{0:T(128)S(1)}, s32[64]{0:T(128)}, u32[]{:S(2)}) copy-start(s32[64]{0:T(128)} %copy-done.47) | copy-start | bytes 772
  153.2 5.9 %collective-permute-start.6 = (bf16[32,512]{1,0:T(8,128)(2,1)S(1)}, bf16[32,512]{1,0:T(8,128)(2,1)S(1)}, u32[]{:S(2)}, u32[]{:S(2)}) collective-permute-start(bf16[32,512]{1,0:T(8,128)(2,1)S(1)} %fusion.8), channel_id=1, source_target_pairs={{0,128},{128,256},{256,384},{384,0},{1,129},{129,257},{257,385},{3... | collective-permute-start | bytes 98312 | tf_op jit(solution)/shard_map/ppermute | solution.py:145
  160.0 14.0 %all-to-all-start.4 = ((bf16[16,32,512]{2,1,0:T(8,128)(2,1)}), bf16[16,32,512]{2,1,0:T(8,128)(2,1)S(1)}, u32[]{:S(2)}, u32[]{:S(2)}) async-start(bf16[16,32,512]{2,1,0:T(8,128)(2,1)} %broadcast_in_dim.387), calls=%async_computation.4 | async-start | bytes 1048576 | tf_op jit(solution)/shard_map/all_to_all | solution.py:57
  163.5 15.9 %collective-permute-start.8 = (bf16[64,4096]{1,0:T(8,128)(2,1)S(1)}, bf16[64,4096]{1,0:T(8,128)(2,1)S(1)}, u32[]{:S(2)}, u32[]{:S(2)}) collective-permute-start(bf16[64,4096]{1,0:T(8,128)(2,1)S(1)} %bitcast.146), channel_id=1, source_target_pairs={{0,128},{128,256},{256,384},{1,129},{129,257},{257,385},{2,130},{1... | collective-permute-start | bytes 1572872 | tf_op jit(solution)/shard_map/ppermute | solution.py:137
  166.7 12.8 %collective-permute-start.7 = (bf16[128,640]{1,0:T(8,128)(2,1)}, bf16[128,640]{1,0:T(8,128)(2,1)}, u32[]{:S(2)}, u32[]{:S(2)}) collective-permute-start(bf16[128,640]{1,0:T(8,128)(2,1)} %pad_maximum_fusion.4), channel_id=1, source_target_pairs={{0,128},{128,256},{256,384},{384,0},{1,129},{129,257},{257,385},{3... | collective-permute-start | bytes 491528 | tf_op jit(solution)/shard_map/ppermute | solution.py:148
  233.2 16.0 %all-to-all-start.6 = ((bf16[8,32,512]{2,1,0:T(8,128)(2,1)}), bf16[8,32,512]{2,1,0:T(8,128)(2,1)S(1)}, u32[]{:S(2)}, u32[]{:S(2)}) async-start(bf16[8,32,512]{2,1,0:T(8,128)(2,1)} %bitcast.46), calls=%async_computation.6 | async-start | bytes 524288 | tf_op jit(solution)/shard_map/all_to_all | solution.py:90
  238.8 26.5 %copy-start.53 = (s32[8]{0:T(128)S(1)}, s32[8]{0:T(128)}, u32[]{:S(2)}) copy-start(s32[8]{0:T(128)} %get-tuple-element.64) | copy-start | bytes 100
  238.8 26.7 %copy-start.51 = (s32[8]{0:T(128)S(1)}, s32[8]{0:T(128)}, u32[]{:S(2)}) copy-start(s32[8]{0:T(128)} %copy-done.50) | copy-start | bytes 100
  251.0 14.1 %all-to-all-start.7 = ((bf16[8,3,8,640]{3,2,1,0:T(8,128)(2,1)}), bf16[8,3,8,640]{3,2,1,0:T(8,128)(2,1)S(1)}, u32[]{:S(2)}, u32[]{:S(2)}) async-start(bf16[8,3,8,640]{3,2,1,0:T(8,128)(2,1)} %pad_maximum_fusion.2), calls=%async_computation.7 | async-start | bytes 491520 | tf_op jit(solution)/shard_map/all_to_all | solution.py:158
  (46 other events, 389.9 us)

commit v4 on v3

--- a/solution.py
+++ b/solution.py
@@ -1,6 +1,8 @@
 import jax
 import jax.numpy as jnp
 from jax import lax
+from jax.experimental import pallas as pl
+from jax.experimental.pallas import tpu as pltpu
 from jax.sharding import Mesh, PartitionSpec as P
 
 BF = jnp.bfloat16
@@ -46,6 +48,52 @@
 
 def after(x, *others):
     return lax.optimization_barrier((x, *others))
+
+
+def project_body(core_ref, g_ref, gain_ref, scorer_ref, w0, w1, w2, w3, out_ref, held, sems):
+    copies = [pltpu.make_async_copy(w, held.at[i], sems.at[i]) for i, w in enumerate((w0, w1, w2, w3))]
+    for copy in copies:
+        copy.start()
+    core = core_ref[0]
+    half = g_ref.shape[0] // 2
+    width, units = w0.shape
+    n = out_ref.shape[0]
+    ss = jnp.zeros((n, 1), F32)
+    dot = jnp.zeros((n, 1), F32)
+    x = []
+    for k in range(2):
+        first = pl.multiple_of((core if k == 0 else 1 - core) * half, half)
+        v = g_ref[pl.ds(first, half)].reshape(n, width).astype(F32)
+        ss = ss + jnp.sum(v * v, axis=1, keepdims=True)
+        dot = dot + jnp.sum(v * scorer_ref[k : k + 1, :], axis=1, keepdims=True)
+        x.append((v * gain_ref[k : k + 1, :]).astype(BF))
+    at = lax.broadcasted_iota(jnp.int32, (n, 128), 1)
+    block = jnp.zeros((n, 128), F32)
+    for i, col in enumerate(parts3(ss) + parts3(dot)):
+        block = jnp.where(at == i, col.astype(F32), block)
+    out_ref[:, 2 * units :] = block.astype(BF)
+    for j in range(2):
+        copies[2 * j].wait()
+        total = jnp.dot(x[0], held[2 * j], preferred_element_type=F32)
+        copies[2 * j + 1].wait()
+        total = total + jnp.dot(x[1], held[2 * j + 1], preferred_element_type=F32)
+        out_ref[:, j * units : (j + 1) * units] = total.astype(BF)
+
+
+def project(g, gains, scorers, wg, wu, core):
+    n = g.shape[0] // 2 * g.shape[1]
+    width, units = wg[0].shape
+    vmem = pl.BlockSpec(memory_space=pltpu.VMEM)
+    anywhere = pl.BlockSpec(memory_space=pl.ANY)
+    return pl.pallas_call(
+        project_body,
+        out_shape=jax.ShapeDtypeStruct((n, 2 * units + 128), BF),
+        in_specs=[pl.BlockSpec(memory_space=pltpu.SMEM), vmem, vmem, vmem] + [anywhere] * 4,
+        out_specs=vmem,
+        scratch_shapes=[pltpu.VMEM((4, width, units), BF), pltpu.SemaphoreType.DMA((4,))],
+        compiler_params=pltpu.CompilerParams(vmem_limit_bytes=40 * 2**20),
+        cost_estimate=pl.CostEstimate(flops=8 * n * width * units, bytes_accessed=8 * width * units, transcendentals=0),
+    )(jnp.reshape(core, (1,)).astype(jnp.int32), g, gains, scorers, wg[0], wg[1], wu[0], wu[1])
 
 
 def tick(v, gains, scorers, wg, wu, wd, late, z, core):
@@ -56,21 +104,9 @@
     chunk = everyone // n_q
     g = lax.all_to_all(
         jnp.broadcast_to(v[None], (2 * n_z, rows, width)), PLANE, 0, 0, tiled=True
-    ).reshape(2, everyone, width)
-    ss = 0.0
-    dot = 0.0
-    gate = 0.0
-    up = 0.0
-    for k in range(2):
-        vk = lax.dynamic_index_in_dim(g, core ^ k, 0, keepdims=False).astype(F32)
-        ss = ss + jnp.sum(vk * vk, axis=1)
-        dot = dot + jnp.sum(vk * scorers[k], axis=1)
-        x = (vk * gains[k]).astype(BF)
-        gate = gate + jnp.dot(x, wg[k], preferred_element_type=F32)
-        up = up + jnp.dot(x, wu[k], preferred_element_type=F32)
-    extra = lanes(parts3(ss) + parts3(dot), everyone)
-    part = jnp.concatenate([gate.astype(BF), up.astype(BF), extra], axis=1)
-    units = gate.shape[1]
+    )
+    part = project(g, gains, scorers, wg, wu, core)
+    units = wg[0].shape[1]
     part, *late = after(part, *late)
     part = lax.all_to_all(part.reshape(n_q, chunk, -1), "q", 0, 0, tiled=True)
     total = jnp.sum(part.astype(F32), axis=0)
@@ -107,13 +143,17 @@
     e1 = lists[0, 0, 0]
     e2 = lists[1, 0, 0]
     e2_next = lax.ppermute(e2, "segment", [(i, (i - 1) % n_seg) for i in range(n_seg)])
-    v1 = jnp.take(pending, jnp.maximum(e1, 0), axis=0)
-    safe = jnp.maximum(e2_next, 0)
-    b2 = jnp.where(s == n_seg - 1, jnp.take(arriving, safe, axis=0), jnp.take(pending, safe, axis=0))
+    at = jnp.arange(n_rows, dtype=jnp.int32)[None, :]
+    wrap = s == n_seg - 1
+    v1 = pick((e1[:, None] == at).astype(BF), pending)
+    hit2 = e2_next[:, None] == at
+    b2 = jnp.dot((hit2 & wrap).astype(BF), arriving, preferred_element_type=F32)
+    b2 = (b2 + jnp.dot((hit2 & ~wrap).astype(BF), pending, preferred_element_type=F32)).astype(BF)
     both = jnp.concatenate([v1, b2], axis=0).reshape(2 * cap, n_dp, cut).transpose(1, 0, 2)
     codes = lanes([jnp.concatenate([e1, e2_next]).astype(BF)], 2 * cap)
     both = jnp.concatenate([both, jnp.broadcast_to(codes[None], (n_dp, 2 * cap, 128))], axis=2)
-    both, wg = after(both, cross(w_gate[0]))
+    both, w_g = after(both, w_gate[0])
+    wg = cross(w_g)
     got = lax.all_to_all(both, DP, 0, 0, tiled=True)
     slots1 = got[:, :cap].reshape(n_dp * cap, -1)
     slots2 = got[:, cap:].reshape(n_dp * cap, -1)
@@ -129,7 +169,8 @@
     v1c = pick(comp1, slots1[:, :cut])
     b2c = pick(comp2, slots2[:, :cut])
 
-    v1c, wu = after(v1c, cross(w_up[0]))
+    v1c, wg = after(v1c, wg)
+    wu = cross(after(w_up[0], got)[0])
     wg = (wg, sibling(wg))
     wu = (wu, sibling(wu))
     wd = (w_down[0], sibling(w_down[0]))
@@ -137,7 +178,7 @@
     base = lax.ppermute(pending, "segment", ahead[:-1])
 
     def slices(row):
-        return [lax.dynamic_slice_in_dim(row[0], (2 * q + (core ^ k)) * cut, cut, 0) for k in range(2)]
+        return jnp.stack([lax.dynamic_slice_in_dim(row[0], (2 * q + (core ^ k)) * cut, cut, 0) for k in range(2)])
 
     gains, scorers = slices(gain), slices(scorer)
     up1, _ = tick(v1c, gains, scorers, wg, wu, wd, [], z, core)

time: 270 us -> 260 us (0.963)
  starting transfers between devices: 78.8 us -> 66.9 us
  waiting for transfers between devices: 62.2 us -> 73.9 us
  matrix products: 19.3 us -> 11.9 us
  Pallas kernels: 0 us -> 6.55 us
  other arithmetic: 14.5 us -> 8.55 us
    all_to_all x1, starting transfers between devices: 12.5 us -> 4.47 us  [local(): got = lax.all_to_all(both, DP, 0, 0, tiled=True)]
    pallas_call x0 -> x2, Pallas kernels: none -> 6.55 us  [project(): pl.pallas_call(project_body, out_shape=jax.ShapeDtypeStruct((n, 2 * units...]
    dot_general x8 -> x2, matrix products: 5.95 us -> 1.53 us  [the longest x1 1.28 us: local(): jnp.dot((hit2 & ~wrap).astype(BF), pending, preferred_element_type=F32)]
    ppermute x1, waiting for transfers between devices: 0.92 us -> 5.22 us  [local(): lax.ppermute(e2, 'segment', [(i, (i - 1) % n_seg) for i in range(n_seg)])]
    all_to_all x2, waiting for transfers between devices: 10 us -> 13.1 us  [tick(): lax.all_to_all(jnp.broadcast_to(v[None], (2 * n_z, rows, width)), PLANE,...]
    dot_general x8 -> x9, matrix products: 7.87 us -> 4.85 us  [pick(): return jnp.dot(onehot, x, preferred_element_type=F32).astype(BF)]
    gather x3 -> x0, local copies, waits for them, and re-layouts: 2.93 us -> none  [the longest x1 1.76 us: local(): v1 = jnp.take(pending, jnp.maximum(e1, 0), axis=0)]
  transfers between devices with their start and end apart: 16 -> 16, of which waited for: 9 -> 9; matrix products, arithmetic and copies ran while one was open for 8% -> 4% of each run, Pallas kernels for 0% -> 1%
where the time goes in v4:
time: 260 us; the launch traced here: 258 us
  blocking collectives  82 us (32%)
  waiting for transfers between devices  73.9 us (28%)
  starting transfers between devices  66.9 us (26%)
  matrix products  11.9 us (5%)
  other arithmetic  8.55 us (3%)
  local copies, waits for them, and re-layouts  7.52 us (3%)
  Pallas kernels  6.55 us (3%)
    all_gather x2, blocking collectives, tick(): lax.all_gather(hidden, DP, axis=0, tiled=True).reshape(n_q, 2, chunk, -1)  59.9 us
    all_to_all x1, blocking collectives, tick(): part = lax.all_to_all(part.reshape(n_q, chunk, -1), 'q', 0, 0, tiled=True)  22 us
    all_to_all x2, starting transfers between devices, tick(): lax.all_to_all(jnp.broadcast_to(v[None], (2 * n_z, rows, width)), PLANE,...  19.1 us
    all_to_all x2, waiting for transfers between devices, tick(): lax.all_to_all(out.astype(BF).reshape(n_z, rows, width), 'z', 0, 0, tiled...  18.7 us
    all_to_all x1, waiting for transfers between devices, tick(): part = lax.all_to_all(part.reshape(n_q, chunk, -1), 'q', 0, 0, tiled=True)  14.9 us
    all_to_all x2, starting transfers between devices, tick(): lax.all_to_all(out.astype(BF).reshape(n_z, rows, width), 'z', 0, 0, tiled...  14.5 us
    all_to_all x2, waiting for transfers between devices, tick(): lax.all_to_all(jnp.broadcast_to(v[None], (2 * n_z, rows, width)), PLANE,...  13.1 us
    all_to_all x1, waiting for transfers between devices, local(): back = lax.all_to_all(back, DP, 0, 0, tiled=True)  10.1 us
  transfers between devices with their start and end apart: 16, of which 9 were waited for; matrix products, arithmetic and copies ran while one was open for 4% of the time, Pallas kernels for 1%

profile of v4, /device:TPU:6, one launch (start us, length us, event | category | flops | bytes accessed | tf_op | source)
XLA Modules:
  0.0 258.5 jit_solution(16008504080827369223)
XLA Ops:
  1.4 2.7 %collective-permute-start = (s32[8]{0:T(128)S(1)}, s32[8]{0:T(128)S(1)}, u32[]{:S(2)}, u32[]{:S(2)}) collective-permute-start(s32[8]{0:T(128)S(1)} %get-tuple-element.47), channel_id=1, source_target_pairs={{0,384},{128,0},{256,128},{384,256},{1,385},{129,1},{257,129},{385... | collective-permute-start | bytes 104 | tf_op jit(solution)/shard_map/ppermute | solution.py:145
  5.4 5.2 %collective-permute-done = s32[8]{0:T(128)S(1)} collective-permute-done((s32[8]{0:T(128)S(1)}, s32[8]{0:T(128)S(1)}, u32[]{:S(2)}, u32[]{:S(2)}) %collective-permute-start) | collective-permute-done | bytes 64 | tf_op jit(solution)/shard_map/ppermute | solution.py:145
  13.1 4.5 %all-to-all-start = ((bf16[8,16,640]{2,1,0:T(8,128)(2,1)}), bf16[8,16,640]{2,1,0:T(8,128)(2,1)S(1)}, u32[]{:S(2)}, u32[]{:S(2)}) async-start(bf16[8,16,640]{2,1,0:T(8,128)(2,1)} %pad_maximum_fusion.1), calls=%async_computation | async-start | bytes 327680 | tf_op jit(solution)/shard_map/all_to_all | solution.py:157
  19.4 7.6 %all-to-all-done = bf16[8,16,640]{2,1,0:T(8,128)(2,1)S(1)} async-done(((bf16[8,16,640]{2,1,0:T(8,128)(2,1)}), bf16[8,16,640]{2,1,0:T(8,128)(2,1)S(1)}, u32[]{:S(2)}, u32[]{:S(2)}) %all-to-all-start) | async-done | bytes 163872 | tf_op jit(solution)/shard_map/all_to_all | solution.py:157
  30.1 15.6 %all-to-all-start.1 = ((bf16[16,32,512]{2,1,0:T(8,128)(2,1)}), bf16[16,32,512]{2,1,0:T(8,128)(2,1)S(1)}, u32[]{:S(2)}, u32[]{:S(2)}) async-start(bf16[16,32,512]{2,1,0:T(8,128)(2,1)} %broadcast_in_dim.209), calls=%async_computation.1 | async-start | bytes 1048576 | tf_op jit(solution)/shard_map/all_to_all | solution.py:105
  47.6 2.4 collective-permute-start.4
  50.8 8.4 %all-to-all-done.1.g_ref = bf16[16,32,512]{2,1,0:T(8,128)(2,1)S(1)} async-done(((bf16[16,32,512]{2,1,0:T(8,128)(2,1)}), bf16[16,32,512]{2,1,0:T(8,128)(2,1)S(1)}, u32[]{:S(2)}, u32[]{:S(2)}) %all-to-all-start.1) | async-done | bytes 524320 | tf_op jit(solution)/shard_map/all_to_all | solution.py:105
  59.2 3.8 %shard_map.95 = bf16[256,1920]{1,0:T(8,128)(2,1)} custom-call(s32[1]{0:T(128)} %bitcast.6.core_ref, bf16[16,32,512]{2,1,0:T(8,128)(2,1)S(1)} %all-to-all-done.1.g_ref, f32[2,512]{1,0:T(2,128)S(1)} %pad_maximum_fusion.8.gain_ref, f32[2,512]{1,0:T(2,128)S(1)} %pad_maximum_fusion.9.scorer_ref, bf16[512,896]{1,0:T(8,128)(2,1)S(1)} %collective-permute-done.1.w0, ...), custom_call_target="tpu_custom_call" | custom-call | flops 939524096 | bytes 3670016 | tf_op jit(solution)/shard_map/pallas_call | solution.py:88
  63.0 5.3 %all-to-all-start.2 = ((bf16[4,64,1920]{2,1,0:T(8,128)(2,1)}), bf16[4,64,1920]{2,1,0:T(8,128)(2,1)}, u32[]{:S(2)}, u32[]{:S(2)}) async-start(bf16[4,64,1920]{2,1,0:T(8,128)(2,1)} %bitcast.8), calls=%async_computation.2 | async-start | bytes 1966080 | tf_op jit(solution)/shard_map/all_to_all | solution.py:111
  71.0 14.9 %all-to-all-done.2 = bf16[4,64,1920]{2,1,0:T(8,128)(2,1)} async-done(((bf16[4,64,1920]{2,1,0:T(8,128)(2,1)}), bf16[4,64,1920]{2,1,0:T(8,128)(2,1)}, u32[]{:S(2)}, u32[]{:S(2)}) %all-to-all-start.2) | async-done | bytes 983072 | tf_op jit(solution)/shard_map/all_to_all | solution.py:111
  88.1 33.3 %all_gather.6 = bf16[512,960]{1,0:T(8,128)(2,1)S(1)} all-gather(bf16[64,960]{1,0:T(8,128)(2,1)S(1)} %pad_maximum_fusion.4), channel_id=1, replica_groups=mesh['segment'=4,'q'=4,'h'=2,'z'=8,'core'=2] {'q','h'}, dimensions={0}, use_global_device_ids=true | all-gather | bytes 1105920 | tf_op jit(solution)/shard_map/all_gather | solution.py:118
  125.7 7.8 %all-to-all-start.3 = ((bf16[8,32,512]{2,1,0:T(8,128)(2,1)}), bf16[8,32,512]{2,1,0:T(8,128)(2,1)S(1)}, u32[]{:S(2)}, u32[]{:S(2)}) async-start(bf16[8,32,512]{2,1,0:T(8,128)(2,1)} %bitcast.18), calls=%async_computation.3 | async-start | bytes 524288 | tf_op jit(solution)/shard_map/all_to_all | solution.py:126
  134.6 9.3 %all-to-all-done.3 = bf16[8,32,512]{2,1,0:T(8,128)(2,1)S(1)} async-done(((bf16[8,32,512]{2,1,0:T(8,128)(2,1)}), bf16[8,32,512]{2,1,0:T(8,128)(2,1)S(1)}, u32[]{:S(2)}, u32[]{:S(2)}) %all-to-all-start.3) | async-done | bytes 262176 | tf_op jit(solution)/shard_map/all_to_all | solution.py:126
  146.1 4.2 %collective-permute-done.6 = bf16[32,512]{1,0:T(8,128)(2,1)S(1)} collective-permute-done((bf16[32,512]{1,0:T(8,128)(2,1)S(1)}, bf16[32,512]{1,0:T(8,128)(2,1)S(1)}, u32[]{:S(2)}, u32[]{:S(2)}) %collective-permute-start.6) | collective-permute-done | bytes 32800 | tf_op jit(solution)/shard_map/ppermute | solution.py:186
  151.2 3.6 %all-to-all-start.4 = ((bf16[16,32,512]{2,1,0:T(8,128)(2,1)}), bf16[16,32,512]{2,1,0:T(8,128)(2,1)S(1)}, u32[]{:S(2)}, u32[]{:S(2)}) async-start(bf16[16,32,512]{2,1,0:T(8,128)(2,1)} %broadcast_in_dim.220), calls=%async_computation.4 | async-start | bytes 1048576 | tf_op jit(solution)/shard_map/all_to_all | solution.py:105
  156.4 4.1 %collective-permute-start.7 = (bf16[128,640]{1,0:T(8,128)(2,1)S(1)}, bf16[128,640]{1,0:T(8,128)(2,1)}, u32[]{:S(2)}, u32[]{:S(2)}) collective-permute-start(bf16[128,640]{1,0:T(8,128)(2,1)S(1)} %pad_maximum_fusion.2), channel_id=1, source_target_pairs={{0,128},{128,256},{256,384},{384,0},{1,129},{129,257},{257,385},{3... | collective-permute-start | bytes 491528 | tf_op jit(solution)/shard_map/ppermute | solution.py:189
  160.5 4.7 %all-to-all-done.4.g_ref = bf16[16,32,512]{2,1,0:T(8,128)(2,1)S(1)} async-done(((bf16[16,32,512]{2,1,0:T(8,128)(2,1)}), bf16[16,32,512]{2,1,0:T(8,128)(2,1)S(1)}, u32[]{:S(2)}, u32[]{:S(2)}) %all-to-all-start.4) | async-done | bytes 524320 | tf_op jit(solution)/shard_map/all_to_all | solution.py:105
  165.2 2.8 %shard_map.96 = bf16[256,1920]{1,0:T(8,128)(2,1)S(1)} custom-call(s32[1]{0:T(128)} %bitcast.6.core_ref, bf16[16,32,512]{2,1,0:T(8,128)(2,1)S(1)} %all-to-all-done.4.g_ref, f32[2,512]{1,0:T(2,128)S(1)} %pad_maximum_fusion.8.gain_ref, f32[2,512]{1,0:T(2,128)S(1)} %pad_maximum_fusion.9.scorer_ref, bf16[512,896]{1,0:T(8,128)(2,1)S(1)} %collective-permute-done.1.w0, ...), custom_call_target="tpu_custom_call" | custom-call | flops 939524096 | bytes 3670016 | tf_op jit(solution)/shard_map/pallas_call | solution.py:88
  168.0 22.0 %all_to_all.40 = bf16[4,64,1920]{2,1,0:T(8,128)(2,1)S(1)} all-to-all(bf16[4,64,1920]{2,1,0:T(8,128)(2,1)S(1)} %bitcast.94), channel_id=1, replica_groups=mesh['segment'=4,'q'=4,'h'=2,'z'=8,'core'=2] {'q'}, dimensions={0} | all-to-all | bytes 1966080 | tf_op jit(solution)/shard_map/all_to_all | solution.py:111
  190.9 26.7 %all_gather.7 = bf16[512,960]{1,0:T(8,128)(2,1)S(1)} all-gather(bf16[64,960]{1,0:T(8,128)(2,1)S(1)} %pad_maximum_fusion.5), channel_id=1, replica_groups=mesh['segment'=4,'q'=4,'h'=2,'z'=8,'core'=2] {'q','h'}, dimensions={0}, use_global_device_ids=true | all-gather | bytes 1105920 | tf_op jit(solution)/shard_map/all_gather | solution.py:118
  221.6 6.8 %all-to-all-start.6 = ((bf16[8,32,512]{2,1,0:T(8,128)(2,1)}), bf16[8,32,512]{2,1,0:T(8,128)(2,1)S(1)}, u32[]{:S(2)}, u32[]{:S(2)}) async-start(bf16[8,32,512]{2,1,0:T(8,128)(2,1)} %bitcast.33), calls=%async_computation.6 | async-start | bytes 524288 | tf_op jit(solution)/shard_map/all_to_all | solution.py:126
  229.5 9.3 %all-to-all-done.6 = bf16[8,32,512]{2,1,0:T(8,128)(2,1)S(1)} async-done(((bf16[8,32,512]{2,1,0:T(8,128)(2,1)}), bf16[8,32,512]{2,1,0:T(8,128)(2,1)S(1)}, u32[]{:S(2)}, u32[]{:S(2)}) %all-to-all-start.6) | async-done | bytes 262176 | tf_op jit(solution)/shard_map/all_to_all | solution.py:126
  240.6 3.5 %all-to-all-start.7 = ((bf16[8,3,8,640]{3,2,1,0:T(8,128)(2,1)}), bf16[8,3,8,640]{3,2,1,0:T(8,128)(2,1)S(1)}, u32[]{:S(2)}, u32[]{:S(2)}) async-start(bf16[8,3,8,640]{3,2,1,0:T(8,128)(2,1)} %pad_maximum_fusion), calls=%async_computation.7 | async-start | bytes 491520 | tf_op jit(solution)/shard_map/all_to_all | solution.py:199
  244.2 10.1 %all-to-all-done.7 = bf16[8,3,8,640]{3,2,1,0:T(8,128)(2,1)S(1)} async-done(((bf16[8,3,8,640]{3,2,1,0:T(8,128)(2,1)}), bf16[8,3,8,640]{3,2,1,0:T(8,128)(2,1)S(1)}, u32[]{:S(2)}, u32[]{:S(2)}) %all-to-all-start.7) | async-done | bytes 245792 | tf_op jit(solution)/shard_map/all_to_all | solution.py:199
  (124 shorter events, 38.7 us)
Async XLA Ops:
  0.6 11.3 %copy-start.4 = (bf16[64,4096]{1,0:T(8,128)(2,1)S(1)}, bf16[64,4096]{1,0:T(8,128)(2,1)}, u32[]{:S(2)}) copy-start(bf16[64,4096]{1,0:T(8,128)(2,1)} %param.9) | copy-start | bytes 1572868
  1.4 4.0 %copy-start.9 = (s32[8]{0:T(128)}, s32[8]{0:T(128)S(1)}, u32[]{:S(2)}) copy-start(s32[8]{0:T(128)S(1)} %get-tuple-element.47) | copy-start | bytes 100
  1.4 9.3 %collective-permute-start = (s32[8]{0:T(128)S(1)}, s32[8]{0:T(128)S(1)}, u32[]{:S(2)}, u32[]{:S(2)}) collective-permute-start(s32[8]{0:T(128)S(1)} %get-tuple-element.47), channel_id=1, source_target_pairs={{0,384},{128,0},{256,128},{384,256},{1,385},{129,1},{257,129},{385... | collective-permute-start | bytes 104 | tf_op jit(solution)/shard_map/ppermute | solution.py:145
  13.1 13.9 %all-to-all-start = ((bf16[8,16,640]{2,1,0:T(8,128)(2,1)}), bf16[8,16,640]{2,1,0:T(8,128)(2,1)S(1)}, u32[]{:S(2)}, u32[]{:S(2)}) async-start(bf16[8,16,640]{2,1,0:T(8,128)(2,1)} %pad_maximum_fusion.1), calls=%async_computation | async-start | bytes 327680 | tf_op jit(solution)/shard_map/all_to_all | solution.py:157
  17.5 11.7 %collective-permute-start.1 = (bf16[512,896]{1,0:T(8,128)(2,1)}, bf16[512,896]{1,0:T(8,128)(2,1)S(1)}, u32[]{:S(2)}, u32[]{:S(2)}) collective-permute-start(bf16[512,896]{1,0:T(8,128)(2,1)} %bitcast.4), channel_id=1, source_target_pairs={{0,0},{17,17},{1,16},{16,1},{2,2},{19,19},{3,18},{18,3},{4,4},{21,... | collective-permute-start | bytes 2752520 | tf_op jit(solution)/shard_map/ppermute | solution.py:42
  27.0 20.6 %collective-permute-start.3 = (bf16[512,896]{1,0:T(8,128)(2,1)}, bf16[512,896]{1,0:T(8,128)(2,1)S(1)}, u32[]{:S(2)}, u32[]{:S(2)}) collective-permute-start(bf16[512,896]{1,0:T(8,128)(2,1)} %bitcast.116), channel_id=1, source_target_pairs={{0,0},{17,17},{1,16},{16,1},{2,2},{19,19},{3,18},{18,3},{4,4},{21,... | collective-permute-start | bytes 2752520 | tf_op jit(solution)/shard_map/ppermute | solution.py:42
  30.1 29.1 %all-to-all-start.1 = ((bf16[16,32,512]{2,1,0:T(8,128)(2,1)}), bf16[16,32,512]{2,1,0:T(8,128)(2,1)S(1)}, u32[]{:S(2)}, u32[]{:S(2)}) async-start(bf16[16,32,512]{2,1,0:T(8,128)(2,1)} %broadcast_in_dim.209), calls=%async_computation.1 | async-start | bytes 1048576 | tf_op jit(solution)/shard_map/all_to_all | solution.py:105
  45.6 5.1 %collective-permute-start.2 = (bf16[512,896]{1,0:T(8,128)(2,1)S(1)}, bf16[512,896]{1,0:T(8,128)(2,1)S(1)}, u32[]{:S(2)}, u32[]{:S(2)}) collective-permute-start(bf16[512,896]{1,0:T(8,128)(2,1)S(1)} %collective-permute-done.1.w0), channel_id=1, source_target_pairs={{0,1},{1,0},{2,3},{3,2},{4,5},{5,4},{6,7},{7,6},{8,9},{9,8},{10,11... | collective-permute-start | bytes 2752520 | tf_op jit(solution)/shard_map/ppermute | solution.py:46
  47.6 11.6 %collective-permute-start.4 = (bf16[512,896]{1,0:T(8,128)(2,1)S(1)}, bf16[512,896]{1,0:T(8,128)(2,1)}, u32[]{:S(2)}, u32[]{:S(2)}) collective-permute-start(bf16[512,896]{1,0:T(8,128)(2,1)S(1)} %collective-permute-done.3.w2), channel_id=1, source_target_pairs={{0,1},{1,0},{2,3},{3,2},{4,5},{5,4},{6,7},{7,6},{8,9},{9,8},{10,11... | collective-permute-start | bytes 2752520 | tf_op jit(solution)/shard_map/ppermute | solution.py:46
  63.0 23.0 %all-to-all-start.2 = ((bf16[4,64,1920]{2,1,0:T(8,128)(2,1)}), bf16[4,64,1920]{2,1,0:T(8,128)(2,1)}, u32[]{:S(2)}, u32[]{:S(2)}) async-start(bf16[4,64,1920]{2,1,0:T(8,128)(2,1)} %bitcast.8), calls=%async_computation.2 | async-start | bytes 1966080 | tf_op jit(solution)/shard_map/all_to_all | solution.py:111
  68.3 55.1 %collective-permute-start.5 = (bf16[896,512]{1,0:T(8,128)(2,1)}, bf16[896,512]{1,0:T(8,128)(2,1)}, u32[]{:S(2)}, u32[]{:S(2)}) collective-permute-start(bf16[896,512]{1,0:T(8,128)(2,1)} %bitcast.100), channel_id=1, source_target_pairs={{0,1},{1,0},{2,3},{3,2},{4,5},{5,4},{6,7},{7,6},{8,9},{9,8},{10,11... | collective-permute-start | bytes 2752520 | tf_op jit(solution)/shard_map/ppermute | solution.py:46
  125.7 18.2 %all-to-all-start.3 = ((bf16[8,32,512]{2,1,0:T(8,128)(2,1)}), bf16[8,32,512]{2,1,0:T(8,128)(2,1)S(1)}, u32[]{:S(2)}, u32[]{:S(2)}) async-start(bf16[8,32,512]{2,1,0:T(8,128)(2,1)} %bitcast.18), calls=%async_computation.3 | async-start | bytes 524288 | tf_op jit(solution)/shard_map/all_to_all | solution.py:126
  144.2 6.2 %collective-permute-start.6 = (bf16[32,512]{1,0:T(8,128)(2,1)S(1)}, bf16[32,512]{1,0:T(8,128)(2,1)S(1)}, u32[]{:S(2)}, u32[]{:S(2)}) collective-permute-start(bf16[32,512]{1,0:T(8,128)(2,1)S(1)} %fusion.5), channel_id=1, source_target_pairs={{0,128},{128,256},{256,384},{384,0},{1,129},{129,257},{257,385},{3... | collective-permute-start | bytes 98312 | tf_op jit(solution)/shard_map/ppermute | solution.py:186
  150.3 5.8 %copy-start.6 = (bf16[32,512]{1,0:T(8,128)(2,1)}, bf16[32,512]{1,0:T(8,128)(2,1)S(1)}, u32[]{:S(2)}) copy-start(bf16[32,512]{1,0:T(8,128)(2,1)S(1)} %collective-permute-done.6) | copy-start | bytes 98308
  151.2 14.0 %all-to-all-start.4 = ((bf16[16,32,512]{2,1,0:T(8,128)(2,1)}), bf16[16,32,512]{2,1,0:T(8,128)(2,1)S(1)}, u32[]{:S(2)}, u32[]{:S(2)}) async-start(bf16[16,32,512]{2,1,0:T(8,128)(2,1)} %broadcast_in_dim.220), calls=%async_computation.4 | async-start | bytes 1048576 | tf_op jit(solution)/shard_map/all_to_all | solution.py:105
  154.8 13.2 %collective-permute-start.8 = (bf16[64,4096]{1,0:T(8,128)(2,1)}, bf16[64,4096]{1,0:T(8,128)(2,1)}, u32[]{:S(2)}, u32[]{:S(2)}) collective-permute-start(bf16[64,4096]{1,0:T(8,128)(2,1)} %bitcast.95), channel_id=1, source_target_pairs={{0,128},{128,256},{256,384},{1,129},{129,257},{257,385},{2,130},{1... | collective-permute-start | bytes 1572872 | tf_op jit(solution)/shard_map/ppermute | solution.py:178
  156.4 11.5 %collective-permute-start.7 = (bf16[128,640]{1,0:T(8,128)(2,1)S(1)}, bf16[128,640]{1,0:T(8,128)(2,1)}, u32[]{:S(2)}, u32[]{:S(2)}) collective-permute-start(bf16[128,640]{1,0:T(8,128)(2,1)S(1)} %pad_maximum_fusion.2), channel_id=1, source_target_pairs={{0,128},{128,256},{256,384},{384,0},{1,129},{129,257},{257,385},{3... | collective-permute-start | bytes 491528 | tf_op jit(solution)/shard_map/ppermute | solution.py:189
  221.6 17.3 %copy-start.7 = (bf16[32,512]{1,0:T(8,128)(2,1)S(1)}, bf16[32,512]{1,0:T(8,128)(2,1)}, u32[]{:S(2)}) copy-start(bf16[32,512]{1,0:T(8,128)(2,1)} %copy-done.6) | copy-start | bytes 98308
  221.6 17.3 %all-to-all-start.6 = ((bf16[8,32,512]{2,1,0:T(8,128)(2,1)}), bf16[8,32,512]{2,1,0:T(8,128)(2,1)S(1)}, u32[]{:S(2)}, u32[]{:S(2)}) async-start(bf16[8,32,512]{2,1,0:T(8,128)(2,1)} %bitcast.33), calls=%async_computation.6 | async-start | bytes 524288 | tf_op jit(solution)/shard_map/all_to_all | solution.py:126
  228.4 15.9 %copy-start.8 = (s32[2,1,1,8]{3,2,1,0:T(1,128)S(1)}, s32[2,1,1,8]{3,2,1,0:T(1,128)}, u32[]{:S(2)}) copy-start(s32[2,1,1,8]{3,2,1,0:T(1,128)} %param.15) | copy-start | bytes 196
  228.4 26.3 %copy-start.10 = (s32[8]{0:T(128)S(1)}, s32[8]{0:T(128)}, u32[]{:S(2)}) copy-start(s32[8]{0:T(128)} %copy-done.9) | copy-start | bytes 100
  240.6 14.7 %copy-start = (bf16[1,64,4096]{2,1,0:T(8,128)(2,1)S(1)}, bf16[1,64,4096]{2,1,0:T(8,128)(2,1)}, u32[]{:S(2)}) copy-start(bf16[1,64,4096]{2,1,0:T(8,128)(2,1)} %param.8) | copy-start | bytes 1572868
  240.6 13.8 %all-to-all-start.7 = ((bf16[8,3,8,640]{3,2,1,0:T(8,128)(2,1)}), bf16[8,3,8,640]{3,2,1,0:T(8,128)(2,1)S(1)}, u32[]{:S(2)}, u32[]{:S(2)}) async-start(bf16[8,3,8,640]{3,2,1,0:T(8,128)(2,1)} %pad_maximum_fusion), calls=%async_computation.7 | async-start | bytes 491520 | tf_op jit(solution)/shard_map/all_to_all | solution.py:199
  254.8 1.8 copy-start.5
  (3 other events, 3.7 us)

commit v5 on v4

--- a/solution.py
+++ b/solution.py
@@ -1,3 +1,5 @@
+import functools
+
 import jax
 import jax.numpy as jnp
 from jax import lax
@@ -96,6 +98,73 @@
     )(jnp.reshape(core, (1,)).astype(jnp.int32), g, gains, scorers, wg[0], wg[1], wu[0], wu[1])
 
 
+def finish_body(features, part_ref, out_ref):
+    chunk, lanes_out = out_ref.shape
+    units = lanes_out - 64
+
+    def summed(lo, n):
+        total = part_ref[0, :, lo : lo + n].astype(F32)
+        for i in range(1, part_ref.shape[0]):
+            total = total + part_ref[i, :, lo : lo + n].astype(F32)
+        return total
+
+    ext = summed(2 * units, 128)
+    inv = lax.rsqrt((ext[:, 0:1] + ext[:, 1:2] + ext[:, 2:3]) / features + 1e-05)
+    weight = jax.nn.sigmoid(ext[:, 3:4] + ext[:, 4:5] + ext[:, 5:6])
+    gate = summed(0, units) * inv
+    out_ref[:, :units] = (jax.nn.silu(gate) * (summed(units, units) * inv)).astype(BF)
+    at = lax.broadcasted_iota(jnp.int32, (chunk, 64), 1)
+    block = jnp.zeros((chunk, 64), F32)
+    for i, col in enumerate(parts3(weight)):
+        block = jnp.where(at == i, col.astype(F32), block)
+    out_ref[:, units:] = block.astype(BF)
+
+
+def finish(part, units, features):
+    vmem = pl.BlockSpec(memory_space=pltpu.VMEM)
+    return pl.pallas_call(
+        functools.partial(finish_body, features),
+        out_shape=jax.ShapeDtypeStruct((part.shape[1], units + 64), BF),
+        in_specs=[vmem],
+        out_specs=vmem,
+        compiler_params=pltpu.CompilerParams(vmem_limit_bytes=32 * 2**20),
+        cost_estimate=pl.CostEstimate(flops=10 * part.size, bytes_accessed=2 * part.size, transcendentals=part.size // 8),
+    )(part)
+
+
+def lower_body(core_ref, hidden_ref, w0, w1, out_ref, held, sems):
+    copies = [pltpu.make_async_copy(w, held.at[i], sems.at[i]) for i, w in enumerate((w0, w1))]
+    for copy in copies:
+        copy.start()
+    core = core_ref[0]
+    units = w0.shape[0]
+    n = out_ref.shape[0]
+    total = None
+    for k in range(2):
+        side = core if k == 0 else 1 - core
+        x = hidden_ref[:, pl.ds(side, 1), :, :units].reshape(n, units)
+        copies[k].wait()
+        product = jnp.dot(x, held[k], preferred_element_type=F32)
+        total = product if total is None else total + product
+    out_ref[...] = total.astype(BF)
+
+
+def lower(hidden, wd, core):
+    n = hidden.shape[0] * hidden.shape[2]
+    units, width = wd[0].shape
+    vmem = pl.BlockSpec(memory_space=pltpu.VMEM)
+    anywhere = pl.BlockSpec(memory_space=pl.ANY)
+    return pl.pallas_call(
+        lower_body,
+        out_shape=jax.ShapeDtypeStruct((n, width), BF),
+        in_specs=[pl.BlockSpec(memory_space=pltpu.SMEM), vmem, anywhere, anywhere],
+        out_specs=vmem,
+        scratch_shapes=[pltpu.VMEM((2, units, width), BF), pltpu.SemaphoreType.DMA((2,))],
+        compiler_params=pltpu.CompilerParams(vmem_limit_bytes=32 * 2**20),
+        cost_estimate=pl.CostEstimate(flops=4 * n * width * units, bytes_accessed=4 * width * units, transcendentals=0),
+    )(jnp.reshape(core, (1,)).astype(jnp.int32), hidden, wd[0], wd[1])
+
+
 def tick(v, gains, scorers, wg, wu, wd, late, z, core):
     rows, width = v.shape
     n_z = lax.axis_size("z")
@@ -109,21 +178,13 @@
     units = wg[0].shape[1]
     part, *late = after(part, *late)
     part = lax.all_to_all(part.reshape(n_q, chunk, -1), "q", 0, 0, tiled=True)
-    total = jnp.sum(part.astype(F32), axis=0)
-    ext = total[:, 2 * units :]
-    inv = lax.rsqrt((ext[:, 0] + ext[:, 1] + ext[:, 2]) / (8 * width) + 1e-05)[:, None]
-    weight = jax.nn.sigmoid(ext[:, 3] + ext[:, 4] + ext[:, 5])
-    hidden = (jax.nn.silu(total[:, :units] * inv) * (total[:, units : 2 * units] * inv)).astype(BF)
-    hidden = jnp.concatenate([hidden, lanes(parts3(weight), chunk)[:, :64]], axis=1)
+    hidden = finish(part, units, 8 * width)
     hidden = lax.all_gather(hidden, DP, axis=0, tiled=True).reshape(n_q, 2, chunk, -1)
     own = lax.dynamic_slice(hidden[:, 0, :, units:], (z * rows // chunk, z * rows % chunk, 0), (1, rows, 64))
     own = own[0].astype(F32)
     weight = own[:, 0] + own[:, 1] + own[:, 2]
-    out = 0.0
-    for k in range(2):
-        hk = lax.dynamic_index_in_dim(hidden[..., :units], core ^ k, 1, keepdims=False)
-        out = out + jnp.dot(hk.reshape(everyone, units), wd[k], preferred_element_type=F32)
-    out = lax.all_to_all(out.astype(BF).reshape(n_z, rows, width), "z", 0, 0, tiled=True)
+    out = lower(hidden, wd, core)
+    out = lax.all_to_all(out.reshape(n_z, rows, width), "z", 0, 0, tiled=True)
     block_out = jnp.sum(out.astype(F32), axis=0).astype(BF).astype(F32)
     return (v.astype(F32) + weight[:, None] * block_out).astype(BF), late
 

time: 260 us -> 255 us (0.981)
  matrix products: 11.9 us -> 5.42 us
  Pallas kernels: 6.55 us -> 12.7 us
    pallas_call x0 -> x4, Pallas kernels: none -> 6.14 us  [the longest x2 5.64 us: lower(): pl.pallas_call(lower_body, out_shape=jax.ShapeDtypeStruct((n, width), BF)...]
    dot_general x4 -> x0, matrix products: 5.5 us -> none  [tick(): jnp.dot(hk.reshape(everyone, units), wd[k], preferred_element_type=F32)]
  transfers between devices with their start and end apart: 16 -> 16, of which waited for: 9 -> 9; matrix products, arithmetic and copies ran while one was open for 4% -> 2% of each run, Pallas kernels for 1% -> 1%
where the time goes in v5:
time: 255 us; the launch traced here: 253 us
  blocking collectives  82.2 us (32%)
  waiting for transfers between devices  75.6 us (30%)
  starting transfers between devices  65 us (25%)
  Pallas kernels  12.7 us (5%)
  other arithmetic  6.05 us (2%)
  matrix products  5.42 us (2%)
  local copies, waits for them, and re-layouts  5.29 us (2%)
    all_gather x2, blocking collectives, tick(): lax.all_gather(hidden, DP, axis=0, tiled=True).reshape(n_q, 2, chunk, -1)  60 us
    all_to_all x1, blocking collectives, tick(): part = lax.all_to_all(part.reshape(n_q, chunk, -1), 'q', 0, 0, tiled=True)  22.2 us
    all_to_all x2, waiting for transfers between devices, tick(): out = lax.all_to_all(out.reshape(n_z, rows, width), 'z', 0, 0, tiled=True)  19.5 us
    all_to_all x2, starting transfers between devices, tick(): lax.all_to_all(jnp.broadcast_to(v[None], (2 * n_z, rows, width)), PLANE,...  19 us
    all_to_all x1, waiting for transfers between devices, tick(): part = lax.all_to_all(part.reshape(n_q, chunk, -1), 'q', 0, 0, tiled=True)  14.8 us
    all_to_all x2, starting transfers between devices, tick(): out = lax.all_to_all(out.reshape(n_z, rows, width), 'z', 0, 0, tiled=True)  13.7 us
    all_to_all x2, waiting for transfers between devices, tick(): lax.all_to_all(jnp.broadcast_to(v[None], (2 * n_z, rows, width)), PLANE,...  13.1 us
    all_to_all x1, waiting for transfers between devices, local(): back = lax.all_to_all(back, DP, 0, 0, tiled=True)  10.1 us
  transfers between devices with their start and end apart: 16, of which 9 were waited for; matrix products, arithmetic and copies ran while one was open for 2% of the time, Pallas kernels for 1%

profile of v5, /device:TPU:6, one launch (start us, length us, event | category | flops | bytes accessed | tf_op | source)
XLA Modules:
  0.0 253.4 jit_solution(17282570737577369038)
XLA Ops:
  5.5 5.2 %collective-permute-done = s32[8]{0:T(128)S(1)} collective-permute-done((s32[8]{0:T(128)S(1)}, s32[8]{0:T(128)S(1)}, u32[]{:S(2)}, u32[]{:S(2)}) %collective-permute-start) | collective-permute-done | bytes 64 | tf_op jit(solution)/shard_map/ppermute | solution.py:206
  12.0 4.5 %all-to-all-start = ((bf16[8,16,640]{2,1,0:T(8,128)(2,1)}), bf16[8,16,640]{2,1,0:T(8,128)(2,1)S(1)}, u32[]{:S(2)}, u32[]{:S(2)}) async-start(bf16[8,16,640]{2,1,0:T(8,128)(2,1)} %pad_maximum_fusion.1), calls=%async_computation | async-start | bytes 327680 | tf_op jit(solution)/shard_map/all_to_all | solution.py:218
  17.2 8.7 %all-to-all-done = bf16[8,16,640]{2,1,0:T(8,128)(2,1)S(1)} async-done(((bf16[8,16,640]{2,1,0:T(8,128)(2,1)}), bf16[8,16,640]{2,1,0:T(8,128)(2,1)S(1)}, u32[]{:S(2)}, u32[]{:S(2)}) %all-to-all-start) | async-done | bytes 163872 | tf_op jit(solution)/shard_map/all_to_all | solution.py:218
  29.0 15.3 %all-to-all-start.1 = ((bf16[16,32,512]{2,1,0:T(8,128)(2,1)}), bf16[16,32,512]{2,1,0:T(8,128)(2,1)S(1)}, u32[]{:S(2)}, u32[]{:S(2)}) async-start(bf16[16,32,512]{2,1,0:T(8,128)(2,1)} %broadcast_in_dim.74), calls=%async_computation.1 | async-start | bytes 1048576 | tf_op jit(solution)/shard_map/all_to_all | solution.py:174
  49.5 8.4 %all-to-all-done.1.g_ref = bf16[16,32,512]{2,1,0:T(8,128)(2,1)S(1)} async-done(((bf16[16,32,512]{2,1,0:T(8,128)(2,1)}), bf16[16,32,512]{2,1,0:T(8,128)(2,1)S(1)}, u32[]{:S(2)}, u32[]{:S(2)}) %all-to-all-start.1) | async-done | bytes 524320 | tf_op jit(solution)/shard_map/all_to_all | solution.py:174
  58.0 3.7 %shard_map.95 = bf16[256,1920]{1,0:T(8,128)(2,1)} custom-call(s32[1]{0:T(128)} %bitcast.6.core_ref, bf16[16,32,512]{2,1,0:T(8,128)(2,1)S(1)} %all-to-all-done.1.g_ref, f32[2,512]{1,0:T(2,128)S(1)} %pad_maximum_fusion.6.gain_ref, f32[2,512]{1,0:T(2,128)S(1)} %pad_maximum_fusion.7.scorer_ref, bf16[512,896]{1,0:T(8,128)(2,1)S(1)} %collective-permute-done.1.w0, ...), custom_call_target="tpu_custom_call" | custom-call | flops 939524096 | bytes 3670016 | tf_op jit(solution)/shard_map/pallas_call | solution.py:90
  61.7 5.5 %all-to-all-start.2 = ((bf16[4,64,1920]{2,1,0:T(8,128)(2,1)}), bf16[4,64,1920]{2,1,0:T(8,128)(2,1)S(1)}, u32[]{:S(2)}, u32[]{:S(2)}) async-start(bf16[4,64,1920]{2,1,0:T(8,128)(2,1)} %bitcast.8), calls=%async_computation.2 | async-start | bytes 1966080 | tf_op jit(solution)/shard_map/all_to_all | solution.py:180
  69.9 14.8 %all-to-all-done.2.part_ref = bf16[4,64,1920]{2,1,0:T(8,128)(2,1)S(1)} async-done(((bf16[4,64,1920]{2,1,0:T(8,128)(2,1)}), bf16[4,64,1920]{2,1,0:T(8,128)(2,1)S(1)}, u32[]{:S(2)}, u32[]{:S(2)}) %all-to-all-start.2) | async-done | bytes 983072 | tf_op jit(solution)/shard_map/all_to_all | solution.py:180
  85.0 33.3 %all_gather.6 = bf16[512,960]{1,0:T(8,128)(2,1)S(1)} all-gather(bf16[64,960]{1,0:T(8,128)(2,1)S(1)} %shard_map.96), channel_id=1, replica_groups=mesh['segment'=4,'q'=4,'h'=2,'z'=8,'core'=2] {'q','h'}, dimensions={0}, use_global_device_ids=true | all-gather | bytes 1105920 | tf_op jit(solution)/shard_map/all_gather | solution.py:182
  118.4 2.8 %shard_map.97 = bf16[256,512]{1,0:T(8,128)(2,1)} custom-call(s32[1]{0:T(128)} %bitcast.6.core_ref, bf16[4,2,64,960]{3,2,1,0:T(8,128)(2,1)S(1)} %bitcast.65, bf16[896,512]{1,0:T(8,128)(2,1)S(1)} %bitcast.71, bf16[896,512]{1,0:T(8,128)(2,1)} %collective-permute-done.5.w1), custom_call_target="tpu_custom_call" | custom-call | flops 469762048 | bytes 1835008 | tf_op jit(solution)/shard_map/pallas_call | solution.py:157
  121.2 7.7 %all-to-all-start.3 = ((bf16[8,32,512]{2,1,0:T(8,128)(2,1)}), bf16[8,32,512]{2,1,0:T(8,128)(2,1)S(1)}, u32[]{:S(2)}, u32[]{:S(2)}) async-start(bf16[8,32,512]{2,1,0:T(8,128)(2,1)} %bitcast.13), calls=%async_computation.3 | async-start | bytes 524288 | tf_op jit(solution)/shard_map/all_to_all | solution.py:187
  129.3 10.1 %all-to-all-done.3 = bf16[8,32,512]{2,1,0:T(8,128)(2,1)S(1)} async-done(((bf16[8,32,512]{2,1,0:T(8,128)(2,1)}), bf16[8,32,512]{2,1,0:T(8,128)(2,1)S(1)}, u32[]{:S(2)}, u32[]{:S(2)}) %all-to-all-start.3) | async-done | bytes 262176 | tf_op jit(solution)/shard_map/all_to_all | solution.py:187
  141.6 4.2 %collective-permute-done.6 = bf16[32,512]{1,0:T(8,128)(2,1)S(1)} collective-permute-done((bf16[32,512]{1,0:T(8,128)(2,1)S(1)}, bf16[32,512]{1,0:T(8,128)(2,1)S(1)}, u32[]{:S(2)}, u32[]{:S(2)}) %collective-permute-start.6) | collective-permute-done | bytes 32800 | tf_op jit(solution)/shard_map/ppermute | solution.py:247
  146.6 3.7 %all-to-all-start.4 = ((bf16[16,32,512]{2,1,0:T(8,128)(2,1)}), bf16[16,32,512]{2,1,0:T(8,128)(2,1)S(1)}, u32[]{:S(2)}, u32[]{:S(2)}) async-start(bf16[16,32,512]{2,1,0:T(8,128)(2,1)} %broadcast_in_dim.76), calls=%async_computation.4 | async-start | bytes 1048576 | tf_op jit(solution)/shard_map/all_to_all | solution.py:174
  152.0 4.0 %collective-permute-start.7 = (bf16[128,640]{1,0:T(8,128)(2,1)S(1)}, bf16[128,640]{1,0:T(8,128)(2,1)}, u32[]{:S(2)}, u32[]{:S(2)}) collective-permute-start(bf16[128,640]{1,0:T(8,128)(2,1)S(1)} %pad_maximum_fusion.2), channel_id=1, source_target_pairs={{0,128},{128,256},{256,384},{384,0},{1,129},{129,257},{257,385},{3... | collective-permute-start | bytes 491528 | tf_op jit(solution)/shard_map/ppermute | solution.py:250
  156.0 4.7 %all-to-all-done.4.g_ref = bf16[16,32,512]{2,1,0:T(8,128)(2,1)S(1)} async-done(((bf16[16,32,512]{2,1,0:T(8,128)(2,1)}), bf16[16,32,512]{2,1,0:T(8,128)(2,1)S(1)}, u32[]{:S(2)}, u32[]{:S(2)}) %all-to-all-start.4) | async-done | bytes 524320 | tf_op jit(solution)/shard_map/all_to_all | solution.py:174
  161.9 2.8 %shard_map.98 = bf16[256,1920]{1,0:T(8,128)(2,1)S(1)} custom-call(s32[1]{0:T(128)} %bitcast.6.core_ref, bf16[16,32,512]{2,1,0:T(8,128)(2,1)S(1)} %all-to-all-done.4.g_ref, f32[2,512]{1,0:T(2,128)S(1)} %pad_maximum_fusion.6.gain_ref, f32[2,512]{1,0:T(2,128)S(1)} %pad_maximum_fusion.7.scorer_ref, bf16[512,896]{1,0:T(8,128)(2,1)S(1)} %collective-permute-done.1.w0, ...), custom_call_target="tpu_custom_call" | custom-call | flops 939524096 | bytes 3670016 | tf_op jit(solution)/shard_map/pallas_call | solution.py:90
  164.7 22.2 %all_to_all.40.part_ref = bf16[4,64,1920]{2,1,0:T(8,128)(2,1)S(1)} all-to-all(bf16[4,64,1920]{2,1,0:T(8,128)(2,1)S(1)} %bitcast.69), channel_id=1, replica_groups=mesh['segment'=4,'q'=4,'h'=2,'z'=8,'core'=2] {'q'}, dimensions={0} | all-to-all | bytes 1966080 | tf_op jit(solution)/shard_map/all_to_all | solution.py:180
  187.2 26.6 %all_gather.7 = bf16[512,960]{1,0:T(8,128)(2,1)S(1)} all-gather(bf16[64,960]{1,0:T(8,128)(2,1)S(1)} %shard_map.99), channel_id=1, replica_groups=mesh['segment'=4,'q'=4,'h'=2,'z'=8,'core'=2] {'q','h'}, dimensions={0}, use_global_device_ids=true | all-gather | bytes 1105920 | tf_op jit(solution)/shard_map/all_gather | solution.py:182
  213.8 2.8 %shard_map.100 = bf16[256,512]{1,0:T(8,128)(2,1)} custom-call(s32[1]{0:T(128)} %bitcast.6.core_ref, bf16[4,2,64,960]{3,2,1,0:T(8,128)(2,1)S(1)} %bitcast.67, bf16[896,512]{1,0:T(8,128)(2,1)S(1)} %bitcast.72, bf16[896,512]{1,0:T(8,128)(2,1)} %collective-permute-done.5.w1), custom_call_target="tpu_custom_call" | custom-call | flops 469762048 | bytes 1835008 | tf_op jit(solution)/shard_map/pallas_call | solution.py:157
  216.7 6.0 %all-to-all-start.6 = ((bf16[8,32,512]{2,1,0:T(8,128)(2,1)}), bf16[8,32,512]{2,1,0:T(8,128)(2,1)S(1)}, u32[]{:S(2)}, u32[]{:S(2)}) async-start(bf16[8,32,512]{2,1,0:T(8,128)(2,1)} %bitcast.23), calls=%async_computation.6 | async-start | bytes 524288 | tf_op jit(solution)/shard_map/all_to_all | solution.py:187
  223.7 9.4 %all-to-all-done.6 = bf16[8,32,512]{2,1,0:T(8,128)(2,1)S(1)} async-done(((bf16[8,32,512]{2,1,0:T(8,128)(2,1)}), bf16[8,32,512]{2,1,0:T(8,128)(2,1)S(1)}, u32[]{:S(2)}, u32[]{:S(2)}) %all-to-all-start.6) | async-done | bytes 262176 | tf_op jit(solution)/shard_map/all_to_all | solution.py:187
  234.9 3.5 %all-to-all-start.7 = ((bf16[8,3,8,640]{3,2,1,0:T(8,128)(2,1)}), bf16[8,3,8,640]{3,2,1,0:T(8,128)(2,1)S(1)}, u32[]{:S(2)}, u32[]{:S(2)}) async-start(bf16[8,3,8,640]{3,2,1,0:T(8,128)(2,1)} %pad_maximum_fusion), calls=%async_computation.7 | async-start | bytes 491520 | tf_op jit(solution)/shard_map/all_to_all | solution.py:260
  238.5 10.1 %all-to-all-done.7 = bf16[8,3,8,640]{3,2,1,0:T(8,128)(2,1)S(1)} async-done(((bf16[8,3,8,640]{3,2,1,0:T(8,128)(2,1)}), bf16[8,3,8,640]{3,2,1,0:T(8,128)(2,1)S(1)}, u32[]{:S(2)}, u32[]{:S(2)}) %all-to-all-start.7) | async-done | bytes 245792 | tf_op jit(solution)/shard_map/all_to_all | solution.py:260
  (102 shorter events, 32.0 us)
Async XLA Ops:
  0.6 10.0 %copy-start.5 = (bf16[1,64,4096]{2,1,0:T(8,128)(2,1)S(1)}, bf16[1,64,4096]{2,1,0:T(8,128)(2,1)}, u32[]{:S(2)}) copy-start(bf16[1,64,4096]{2,1,0:T(8,128)(2,1)} %param.8) | copy-start | bytes 1572868
  1.4 9.3 %collective-permute-start = (s32[8]{0:T(128)S(1)}, s32[8]{0:T(128)S(1)}, u32[]{:S(2)}, u32[]{:S(2)}) collective-permute-start(s32[8]{0:T(128)S(1)} %get-tuple-element.31), channel_id=1, source_target_pairs={{0,384},{128,0},{256,128},{384,256},{1,385},{129,1},{257,129},{385... | collective-permute-start | bytes 104 | tf_op jit(solution)/shard_map/ppermute | solution.py:206
  4.1 6.8 %copy-start.7 = (bf16[64,4096]{1,0:T(8,128)(2,1)S(1)}, bf16[64,4096]{1,0:T(8,128)(2,1)}, u32[]{:S(2)}) copy-start(bf16[64,4096]{1,0:T(8,128)(2,1)} %param.9) | copy-start | bytes 1572868
  10.9 5.6 %copy-start.12 = (bf16[1,512,896]{2,1,0:T(8,128)(2,1)S(1)}, bf16[1,512,896]{2,1,0:T(8,128)(2,1)}, u32[]{:S(2)}) copy-start(bf16[1,512,896]{2,1,0:T(8,128)(2,1)} %param.12) | copy-start | bytes 2752516
  12.0 13.9 %all-to-all-start = ((bf16[8,16,640]{2,1,0:T(8,128)(2,1)}), bf16[8,16,640]{2,1,0:T(8,128)(2,1)S(1)}, u32[]{:S(2)}, u32[]{:S(2)}) async-start(bf16[8,16,640]{2,1,0:T(8,128)(2,1)} %pad_maximum_fusion.1), calls=%async_computation | async-start | bytes 327680 | tf_op jit(solution)/shard_map/all_to_all | solution.py:218
  16.5 11.7 %collective-permute-start.1 = (bf16[512,896]{1,0:T(8,128)(2,1)S(1)}, bf16[512,896]{1,0:T(8,128)(2,1)S(1)}, u32[]{:S(2)}, u32[]{:S(2)}) collective-permute-start(bf16[512,896]{1,0:T(8,128)(2,1)S(1)} %bitcast.79), channel_id=1, source_target_pairs={{0,0},{17,17},{1,16},{16,1},{2,2},{19,19},{3,18},{18,3},{4,4},{21,... | collective-permute-start | bytes 2752520 | tf_op jit(solution)/shard_map/ppermute | solution.py:44
  26.0 20.4 %collective-permute-start.3 = (bf16[512,896]{1,0:T(8,128)(2,1)}, bf16[512,896]{1,0:T(8,128)(2,1)S(1)}, u32[]{:S(2)}, u32[]{:S(2)}) collective-permute-start(bf16[512,896]{1,0:T(8,128)(2,1)} %bitcast.80), channel_id=1, source_target_pairs={{0,0},{17,17},{1,16},{16,1},{2,2},{19,19},{3,18},{18,3},{4,4},{21,... | collective-permute-start | bytes 2752520 | tf_op jit(solution)/shard_map/ppermute | solution.py:44
  29.0 28.9 %all-to-all-start.1 = ((bf16[16,32,512]{2,1,0:T(8,128)(2,1)}), bf16[16,32,512]{2,1,0:T(8,128)(2,1)S(1)}, u32[]{:S(2)}, u32[]{:S(2)}) async-start(bf16[16,32,512]{2,1,0:T(8,128)(2,1)} %broadcast_in_dim.74), calls=%async_computation.1 | async-start | bytes 1048576 | tf_op jit(solution)/shard_map/all_to_all | solution.py:174
  44.4 5.1 %collective-permute-start.2 = (bf16[512,896]{1,0:T(8,128)(2,1)S(1)}, bf16[512,896]{1,0:T(8,128)(2,1)S(1)}, u32[]{:S(2)}, u32[]{:S(2)}) collective-permute-start(bf16[512,896]{1,0:T(8,128)(2,1)S(1)} %collective-permute-done.1.w0), channel_id=1, source_target_pairs={{0,1},{1,0},{2,3},{3,2},{4,5},{5,4},{6,7},{7,6},{8,9},{9,8},{10,11... | collective-permute-start | bytes 2752520 | tf_op jit(solution)/shard_map/ppermute | solution.py:48
  46.3 15.4 %copy-start.1 = (bf16[512,896]{1,0:T(8,128)(2,1)}, bf16[512,896]{1,0:T(8,128)(2,1)S(1)}, u32[]{:S(2)}) copy-start(bf16[512,896]{1,0:T(8,128)(2,1)S(1)} %collective-permute-done.3.w2) | copy-start | bytes 2752516
  46.3 11.6 %collective-permute-start.4 = (bf16[512,896]{1,0:T(8,128)(2,1)S(1)}, bf16[512,896]{1,0:T(8,128)(2,1)}, u32[]{:S(2)}, u32[]{:S(2)}) collective-permute-start(bf16[512,896]{1,0:T(8,128)(2,1)S(1)} %collective-permute-done.3.w2), channel_id=1, source_target_pairs={{0,1},{1,0},{2,3},{3,2},{4,5},{5,4},{6,7},{7,6},{8,9},{9,8},{10,11... | collective-permute-start | bytes 2752520 | tf_op jit(solution)/shard_map/ppermute | solution.py:48
  49.5 12.2 %copy-start.3 = (bf16[512,896]{1,0:T(8,128)(2,1)}, bf16[512,896]{1,0:T(8,128)(2,1)S(1)}, u32[]{:S(2)}) copy-start(bf16[512,896]{1,0:T(8,128)(2,1)S(1)} %collective-permute-done.2.w1) | copy-start | bytes 2752516
  61.7 23.0 %all-to-all-start.2 = ((bf16[4,64,1920]{2,1,0:T(8,128)(2,1)}), bf16[4,64,1920]{2,1,0:T(8,128)(2,1)S(1)}, u32[]{:S(2)}, u32[]{:S(2)}) async-start(bf16[4,64,1920]{2,1,0:T(8,128)(2,1)} %bitcast.8), calls=%async_computation.2 | async-start | bytes 1966080 | tf_op jit(solution)/shard_map/all_to_all | solution.py:180
  67.2 51.1 %collective-permute-start.5 = (bf16[896,512]{1,0:T(8,128)(2,1)S(1)}, bf16[896,512]{1,0:T(8,128)(2,1)}, u32[]{:S(2)}, u32[]{:S(2)}) collective-permute-start(bf16[896,512]{1,0:T(8,128)(2,1)S(1)} %bitcast.70), channel_id=1, source_target_pairs={{0,1},{1,0},{2,3},{3,2},{4,5},{5,4},{6,7},{7,6},{8,9},{9,8},{10,11... | collective-permute-start | bytes 2752520 | tf_op jit(solution)/shard_map/ppermute | solution.py:48
  121.2 18.2 %all-to-all-start.3 = ((bf16[8,32,512]{2,1,0:T(8,128)(2,1)}), bf16[8,32,512]{2,1,0:T(8,128)(2,1)S(1)}, u32[]{:S(2)}, u32[]{:S(2)}) async-start(bf16[8,32,512]{2,1,0:T(8,128)(2,1)} %bitcast.13), calls=%async_computation.3 | async-start | bytes 524288 | tf_op jit(solution)/shard_map/all_to_all | solution.py:187
  139.6 6.1 %collective-permute-start.6 = (bf16[32,512]{1,0:T(8,128)(2,1)S(1)}, bf16[32,512]{1,0:T(8,128)(2,1)S(1)}, u32[]{:S(2)}, u32[]{:S(2)}) collective-permute-start(bf16[32,512]{1,0:T(8,128)(2,1)S(1)} %fusion.3), channel_id=1, source_target_pairs={{0,128},{128,256},{256,384},{384,0},{1,129},{129,257},{257,385},{3... | collective-permute-start | bytes 98312 | tf_op jit(solution)/shard_map/ppermute | solution.py:247
  146.6 14.1 %copy-start.2 = (bf16[512,896]{1,0:T(8,128)(2,1)S(1)}, bf16[512,896]{1,0:T(8,128)(2,1)}, u32[]{:S(2)}) copy-start(bf16[512,896]{1,0:T(8,128)(2,1)} %copy-done.1) | copy-start | bytes 2752516
  146.6 14.1 %all-to-all-start.4 = ((bf16[16,32,512]{2,1,0:T(8,128)(2,1)}), bf16[16,32,512]{2,1,0:T(8,128)(2,1)S(1)}, u32[]{:S(2)}, u32[]{:S(2)}) async-start(bf16[16,32,512]{2,1,0:T(8,128)(2,1)} %broadcast_in_dim.76), calls=%async_computation.4 | async-start | bytes 1048576 | tf_op jit(solution)/shard_map/all_to_all | solution.py:174
  150.3 14.4 %collective-permute-start.8 = (bf16[64,4096]{1,0:T(8,128)(2,1)}, bf16[64,4096]{1,0:T(8,128)(2,1)}, u32[]{:S(2)}, u32[]{:S(2)}) collective-permute-start(bf16[64,4096]{1,0:T(8,128)(2,1)} %bitcast.73), channel_id=1, source_target_pairs={{0,128},{128,256},{256,384},{1,129},{129,257},{257,385},{2,130},{1... | collective-permute-start | bytes 1572872 | tf_op jit(solution)/shard_map/ppermute | solution.py:239
  152.0 12.7 %collective-permute-start.7 = (bf16[128,640]{1,0:T(8,128)(2,1)S(1)}, bf16[128,640]{1,0:T(8,128)(2,1)}, u32[]{:S(2)}, u32[]{:S(2)}) collective-permute-start(bf16[128,640]{1,0:T(8,128)(2,1)S(1)} %pad_maximum_fusion.2), channel_id=1, source_target_pairs={{0,128},{128,256},{256,384},{384,0},{1,129},{129,257},{257,385},{3... | collective-permute-start | bytes 491528 | tf_op jit(solution)/shard_map/ppermute | solution.py:250
  216.7 16.4 %all-to-all-start.6 = ((bf16[8,32,512]{2,1,0:T(8,128)(2,1)}), bf16[8,32,512]{2,1,0:T(8,128)(2,1)S(1)}, u32[]{:S(2)}, u32[]{:S(2)}) async-start(bf16[8,32,512]{2,1,0:T(8,128)(2,1)} %bitcast.23), calls=%async_computation.6 | async-start | bytes 524288 | tf_op jit(solution)/shard_map/all_to_all | solution.py:187
  223.7 9.4 %copy-start.10 = (bf16[32,512]{1,0:T(8,128)(2,1)S(1)}, bf16[32,512]{1,0:T(8,128)(2,1)}, u32[]{:S(2)}) copy-start(bf16[32,512]{1,0:T(8,128)(2,1)} %copy-done.9) | copy-start | bytes 98308
  234.9 13.8 %all-to-all-start.7 = ((bf16[8,3,8,640]{3,2,1,0:T(8,128)(2,1)}), bf16[8,3,8,640]{3,2,1,0:T(8,128)(2,1)S(1)}, u32[]{:S(2)}, u32[]{:S(2)}) async-start(bf16[8,3,8,640]{3,2,1,0:T(8,128)(2,1)} %pad_maximum_fusion), calls=%async_computation.7 | async-start | bytes 491520 | tf_op jit(solution)/shard_map/all_to_all | solution.py:260
  238.4 10.7 %copy-start.6 = (bf16[1,64,4096]{2,1,0:T(8,128)(2,1)S(1)}, bf16[1,64,4096]{2,1,0:T(8,128)(2,1)}, u32[]{:S(2)}) copy-start(bf16[1,64,4096]{2,1,0:T(8,128)(2,1)} %param.8) | copy-start | bytes 1572868
  (5 other events, 12.3 us)

commit v6 on v5

--- a/solution.py
+++ b/solution.py
@@ -230,7 +230,6 @@
     v1c = pick(comp1, slots1[:, :cut])
     b2c = pick(comp2, slots2[:, :cut])
 
-    v1c, wg = after(v1c, wg)
     wu = cross(after(w_up[0], got)[0])
     wg = (wg, sibling(wg))
     wu = (wu, sibling(wu))

time: 255 us -> 251 us (0.984)
  waiting for transfers between devices: 75.6 us -> 83.9 us
  starting transfers between devices: 65 us -> 58.8 us
  blocking collectives: 82.2 us -> 76.2 us
    all_gather x2, blocking collectives: 60 us -> 53 us  [tick(): lax.all_gather(hidden, DP, axis=0, tiled=True).reshape(n_q, 2, chunk, -1)]
    all_to_all x1, waiting for transfers between devices: 14.8 us -> 20.1 us  [tick(): part = lax.all_to_all(part.reshape(n_q, chunk, -1), 'q', 0, 0, tiled=True)]
    all_to_all x2, starting transfers between devices: 19 us -> 14.2 us  [tick(): lax.all_to_all(jnp.broadcast_to(v[None], (2 * n_z, rows, width)), PLANE,...]
    all_to_all x2, waiting for transfers between devices: 13.1 us -> 16.5 us  [tick(): lax.all_to_all(jnp.broadcast_to(v[None], (2 * n_z, rows, width)), PLANE,...]
where the time goes in v6:
time: 251 us; the launch traced here: 250 us
  waiting for transfers between devices  83.9 us (33%)
  blocking collectives  76.2 us (30%)
  starting transfers between devices  58.8 us (23%)
  Pallas kernels  12.7 us (5%)
  other arithmetic  6.05 us (2%)
  matrix products  5.42 us (2%)
  local copies, waits for them, and re-layouts  5.29 us (2%)
    all_gather x2, blocking collectives, tick(): lax.all_gather(hidden, DP, axis=0, tiled=True).reshape(n_q, 2, chunk, -1)  53 us
    all_to_all x1, blocking collectives, tick(): part = lax.all_to_all(part.reshape(n_q, chunk, -1), 'q', 0, 0, tiled=True)  23.2 us
    all_to_all x1, waiting for transfers between devices, tick(): part = lax.all_to_all(part.reshape(n_q, chunk, -1), 'q', 0, 0, tiled=True)  20.1 us
    all_to_all x2, waiting for transfers between devices, tick(): out = lax.all_to_all(out.reshape(n_z, rows, width), 'z', 0, 0, tiled=True)  19.5 us
    all_to_all x2, waiting for transfers between devices, tick(): lax.all_to_all(jnp.broadcast_to(v[None], (2 * n_z, rows, width)), PLANE,...  16.5 us
    all_to_all x2, starting transfers between devices, tick(): lax.all_to_all(jnp.broadcast_to(v[None], (2 * n_z, rows, width)), PLANE,...  14.2 us
    all_to_all x2, starting transfers between devices, tick(): out = lax.all_to_all(out.reshape(n_z, rows, width), 'z', 0, 0, tiled=True)  12.3 us
    all_to_all x1, waiting for transfers between devices, local(): back = lax.all_to_all(back, DP, 0, 0, tiled=True)  10.1 us
  transfers between devices with their start and end apart: 16, of which 9 were waited for; matrix products, arithmetic and copies ran while one was open for 2% of the time, Pallas kernels for 1%

profile of v6, /device:TPU:6, one launch (start us, length us, event | category | flops | bytes accessed | tf_op | source)
XLA Modules:
  0.0 249.6 jit_solution(7883115081586148089)
XLA Ops:
  5.5 5.2 %collective-permute-done = s32[8]{0:T(128)S(1)} collective-permute-done((s32[8]{0:T(128)S(1)}, s32[8]{0:T(128)S(1)}, u32[]{:S(2)}, u32[]{:S(2)}) %collective-permute-start) | collective-permute-done | bytes 64 | tf_op jit(solution)/shard_map/ppermute | solution.py:206
  12.0 4.5 %all-to-all-start = ((bf16[8,16,640]{2,1,0:T(8,128)(2,1)}), bf16[8,16,640]{2,1,0:T(8,128)(2,1)S(1)}, u32[]{:S(2)}, u32[]{:S(2)}) async-start(bf16[8,16,640]{2,1,0:T(8,128)(2,1)} %pad_maximum_fusion.1), calls=%async_computation | async-start | bytes 327680 | tf_op jit(solution)/shard_map/all_to_all | solution.py:218
  17.2 8.7 %all-to-all-done = bf16[8,16,640]{2,1,0:T(8,128)(2,1)S(1)} async-done(((bf16[8,16,640]{2,1,0:T(8,128)(2,1)}), bf16[8,16,640]{2,1,0:T(8,128)(2,1)S(1)}, u32[]{:S(2)}, u32[]{:S(2)}) %all-to-all-start) | async-done | bytes 163872 | tf_op jit(solution)/shard_map/all_to_all | solution.py:218
  29.0 10.5 %all-to-all-start.1 = ((bf16[16,32,512]{2,1,0:T(8,128)(2,1)}), bf16[16,32,512]{2,1,0:T(8,128)(2,1)S(1)}, u32[]{:S(2)}, u32[]{:S(2)}) async-start(bf16[16,32,512]{2,1,0:T(8,128)(2,1)} %broadcast_in_dim.74), calls=%async_computation.1 | async-start | bytes 1048576 | tf_op jit(solution)/shard_map/all_to_all | solution.py:174
  44.7 11.8 %all-to-all-done.1.g_ref = bf16[16,32,512]{2,1,0:T(8,128)(2,1)S(1)} async-done(((bf16[16,32,512]{2,1,0:T(8,128)(2,1)}), bf16[16,32,512]{2,1,0:T(8,128)(2,1)S(1)}, u32[]{:S(2)}, u32[]{:S(2)}) %all-to-all-start.1) | async-done | bytes 524320 | tf_op jit(solution)/shard_map/all_to_all | solution.py:174
  56.5 3.7 %shard_map.95 = bf16[256,1920]{1,0:T(8,128)(2,1)} custom-call(s32[1]{0:T(128)} %bitcast.6.core_ref, bf16[16,32,512]{2,1,0:T(8,128)(2,1)S(1)} %all-to-all-done.1.g_ref, f32[2,512]{1,0:T(2,128)S(1)} %pad_maximum_fusion.6.gain_ref, f32[2,512]{1,0:T(2,128)S(1)} %pad_maximum_fusion.7.scorer_ref, bf16[512,896]{1,0:T(8,128)(2,1)S(1)} %collective-permute-done.1.w0, ...), custom_call_target="tpu_custom_call" | custom-call | flops 939524096 | bytes 3670016 | tf_op jit(solution)/shard_map/pallas_call | solution.py:90
  60.3 5.5 %all-to-all-start.2 = ((bf16[4,64,1920]{2,1,0:T(8,128)(2,1)}), bf16[4,64,1920]{2,1,0:T(8,128)(2,1)S(1)}, u32[]{:S(2)}, u32[]{:S(2)}) async-start(bf16[4,64,1920]{2,1,0:T(8,128)(2,1)} %bitcast.8), calls=%async_computation.2 | async-start | bytes 1966080 | tf_op jit(solution)/shard_map/all_to_all | solution.py:180
  68.5 20.1 %all-to-all-done.2.part_ref = bf16[4,64,1920]{2,1,0:T(8,128)(2,1)S(1)} async-done(((bf16[4,64,1920]{2,1,0:T(8,128)(2,1)}), bf16[4,64,1920]{2,1,0:T(8,128)(2,1)S(1)}, u32[]{:S(2)}, u32[]{:S(2)}) %all-to-all-start.2) | async-done | bytes 983072 | tf_op jit(solution)/shard_map/all_to_all | solution.py:180
  88.8 26.9 %all_gather.6 = bf16[512,960]{1,0:T(8,128)(2,1)S(1)} all-gather(bf16[64,960]{1,0:T(8,128)(2,1)S(1)} %shard_map.96), channel_id=1, replica_groups=mesh['segment'=4,'q'=4,'h'=2,'z'=8,'core'=2] {'q','h'}, dimensions={0}, use_global_device_ids=true | all-gather | bytes 1105920 | tf_op jit(solution)/shard_map/all_gather | solution.py:182
  115.8 2.8 %shard_map.97 = bf16[256,512]{1,0:T(8,128)(2,1)} custom-call(s32[1]{0:T(128)} %bitcast.6.core_ref, bf16[4,2,64,960]{3,2,1,0:T(8,128)(2,1)S(1)} %bitcast.65, bf16[896,512]{1,0:T(8,128)(2,1)S(1)} %bitcast.71, bf16[896,512]{1,0:T(8,128)(2,1)} %collective-permute-done.5.w1), custom_call_target="tpu_custom_call" | custom-call | flops 469762048 | bytes 1835008 | tf_op jit(solution)/shard_map/pallas_call | solution.py:157
  118.6 6.0 %all-to-all-start.3 = ((bf16[8,32,512]{2,1,0:T(8,128)(2,1)}), bf16[8,32,512]{2,1,0:T(8,128)(2,1)S(1)}, u32[]{:S(2)}, u32[]{:S(2)}) async-start(bf16[8,32,512]{2,1,0:T(8,128)(2,1)} %bitcast.13), calls=%async_computation.3 | async-start | bytes 524288 | tf_op jit(solution)/shard_map/all_to_all | solution.py:187
  125.0 10.1 %all-to-all-done.3 = bf16[8,32,512]{2,1,0:T(8,128)(2,1)S(1)} async-done(((bf16[8,32,512]{2,1,0:T(8,128)(2,1)}), bf16[8,32,512]{2,1,0:T(8,128)(2,1)S(1)}, u32[]{:S(2)}, u32[]{:S(2)}) %all-to-all-start.3) | async-done | bytes 262176 | tf_op jit(solution)/shard_map/all_to_all | solution.py:187
  137.3 3.9 %collective-permute-done.6 = bf16[32,512]{1,0:T(8,128)(2,1)S(1)} collective-permute-done((bf16[32,512]{1,0:T(8,128)(2,1)S(1)}, bf16[32,512]{1,0:T(8,128)(2,1)S(1)}, u32[]{:S(2)}, u32[]{:S(2)}) %collective-permute-start.6) | collective-permute-done | bytes 32800 | tf_op jit(solution)/shard_map/ppermute | solution.py:246
  142.0 3.7 %all-to-all-start.4 = ((bf16[16,32,512]{2,1,0:T(8,128)(2,1)}), bf16[16,32,512]{2,1,0:T(8,128)(2,1)S(1)}, u32[]{:S(2)}, u32[]{:S(2)}) async-start(bf16[16,32,512]{2,1,0:T(8,128)(2,1)} %broadcast_in_dim.76), calls=%async_computation.4 | async-start | bytes 1048576 | tf_op jit(solution)/shard_map/all_to_all | solution.py:174
  147.4 4.1 %collective-permute-start.7 = (bf16[128,640]{1,0:T(8,128)(2,1)S(1)}, bf16[128,640]{1,0:T(8,128)(2,1)}, u32[]{:S(2)}, u32[]{:S(2)}) collective-permute-start(bf16[128,640]{1,0:T(8,128)(2,1)S(1)} %pad_maximum_fusion.2), channel_id=1, source_target_pairs={{0,128},{128,256},{256,384},{384,0},{1,129},{129,257},{257,385},{3... | collective-permute-start | bytes 491528 | tf_op jit(solution)/shard_map/ppermute | solution.py:249
  151.5 4.7 %all-to-all-done.4.g_ref = bf16[16,32,512]{2,1,0:T(8,128)(2,1)S(1)} async-done(((bf16[16,32,512]{2,1,0:T(8,128)(2,1)}), bf16[16,32,512]{2,1,0:T(8,128)(2,1)S(1)}, u32[]{:S(2)}, u32[]{:S(2)}) %all-to-all-start.4) | async-done | bytes 524320 | tf_op jit(solution)/shard_map/all_to_all | solution.py:174
  157.3 2.8 %shard_map.98 = bf16[256,1920]{1,0:T(8,128)(2,1)S(1)} custom-call(s32[1]{0:T(128)} %bitcast.6.core_ref, bf16[16,32,512]{2,1,0:T(8,128)(2,1)S(1)} %all-to-all-done.4.g_ref, f32[2,512]{1,0:T(2,128)S(1)} %pad_maximum_fusion.6.gain_ref, f32[2,512]{1,0:T(2,128)S(1)} %pad_maximum_fusion.7.scorer_ref, bf16[512,896]{1,0:T(8,128)(2,1)S(1)} %collective-permute-done.1.w0, ...), custom_call_target="tpu_custom_call" | custom-call | flops 939524096 | bytes 3670016 | tf_op jit(solution)/shard_map/pallas_call | solution.py:90
  160.1 23.2 %all_to_all.40.part_ref = bf16[4,64,1920]{2,1,0:T(8,128)(2,1)S(1)} all-to-all(bf16[4,64,1920]{2,1,0:T(8,128)(2,1)S(1)} %bitcast.69), channel_id=1, replica_groups=mesh['segment'=4,'q'=4,'h'=2,'z'=8,'core'=2] {'q'}, dimensions={0} | all-to-all | bytes 1966080 | tf_op jit(solution)/shard_map/all_to_all | solution.py:180
  183.6 26.1 %all_gather.7 = bf16[512,960]{1,0:T(8,128)(2,1)S(1)} all-gather(bf16[64,960]{1,0:T(8,128)(2,1)S(1)} %shard_map.99), channel_id=1, replica_groups=mesh['segment'=4,'q'=4,'h'=2,'z'=8,'core'=2] {'q','h'}, dimensions={0}, use_global_device_ids=true | all-gather | bytes 1105920 | tf_op jit(solution)/shard_map/all_gather | solution.py:182
  209.7 2.8 %shard_map.100 = bf16[256,512]{1,0:T(8,128)(2,1)} custom-call(s32[1]{0:T(128)} %bitcast.6.core_ref, bf16[4,2,64,960]{3,2,1,0:T(8,128)(2,1)S(1)} %bitcast.67, bf16[896,512]{1,0:T(8,128)(2,1)S(1)} %bitcast.72, bf16[896,512]{1,0:T(8,128)(2,1)} %collective-permute-done.5.w1), custom_call_target="tpu_custom_call" | custom-call | flops 469762048 | bytes 1835008 | tf_op jit(solution)/shard_map/pallas_call | solution.py:157
  212.5 6.3 %all-to-all-start.6 = ((bf16[8,32,512]{2,1,0:T(8,128)(2,1)}), bf16[8,32,512]{2,1,0:T(8,128)(2,1)S(1)}, u32[]{:S(2)}, u32[]{:S(2)}) async-start(bf16[8,32,512]{2,1,0:T(8,128)(2,1)} %bitcast.23), calls=%async_computation.6 | async-start | bytes 524288 | tf_op jit(solution)/shard_map/all_to_all | solution.py:187
  219.9 9.4 %all-to-all-done.6 = bf16[8,32,512]{2,1,0:T(8,128)(2,1)S(1)} async-done(((bf16[8,32,512]{2,1,0:T(8,128)(2,1)}), bf16[8,32,512]{2,1,0:T(8,128)(2,1)S(1)}, u32[]{:S(2)}, u32[]{:S(2)}) %all-to-all-start.6) | async-done | bytes 262176 | tf_op jit(solution)/shard_map/all_to_all | solution.py:187
  231.1 3.5 %all-to-all-start.7 = ((bf16[8,3,8,640]{3,2,1,0:T(8,128)(2,1)}), bf16[8,3,8,640]{3,2,1,0:T(8,128)(2,1)S(1)}, u32[]{:S(2)}, u32[]{:S(2)}) async-start(bf16[8,3,8,640]{3,2,1,0:T(8,128)(2,1)} %pad_maximum_fusion), calls=%async_computation.7 | async-start | bytes 491520 | tf_op jit(solution)/shard_map/all_to_all | solution.py:259
  234.7 10.1 %all-to-all-done.7 = bf16[8,3,8,640]{3,2,1,0:T(8,128)(2,1)S(1)} async-done(((bf16[8,3,8,640]{3,2,1,0:T(8,128)(2,1)}), bf16[8,3,8,640]{3,2,1,0:T(8,128)(2,1)S(1)}, u32[]{:S(2)}, u32[]{:S(2)}) %all-to-all-start.7) | async-done | bytes 245792 | tf_op jit(solution)/shard_map/all_to_all | solution.py:259
  (102 shorter events, 32.0 us)
Async XLA Ops:
  0.6 10.0 %copy-start.5 = (bf16[1,64,4096]{2,1,0:T(8,128)(2,1)S(1)}, bf16[1,64,4096]{2,1,0:T(8,128)(2,1)}, u32[]{:S(2)}) copy-start(bf16[1,64,4096]{2,1,0:T(8,128)(2,1)} %param.8) | copy-start | bytes 1572868
  1.4 9.3 %collective-permute-start = (s32[8]{0:T(128)S(1)}, s32[8]{0:T(128)S(1)}, u32[]{:S(2)}, u32[]{:S(2)}) collective-permute-start(s32[8]{0:T(128)S(1)} %get-tuple-element.27), channel_id=1, source_target_pairs={{0,384},{128,0},{256,128},{384,256},{1,385},{129,1},{257,129},{385... | collective-permute-start | bytes 104 | tf_op jit(solution)/shard_map/ppermute | solution.py:206
  4.1 6.8 %copy-start.7 = (bf16[64,4096]{1,0:T(8,128)(2,1)S(1)}, bf16[64,4096]{1,0:T(8,128)(2,1)}, u32[]{:S(2)}) copy-start(bf16[64,4096]{1,0:T(8,128)(2,1)} %param.9) | copy-start | bytes 1572868
  10.9 5.6 %copy-start.12 = (bf16[1,512,896]{2,1,0:T(8,128)(2,1)S(1)}, bf16[1,512,896]{2,1,0:T(8,128)(2,1)}, u32[]{:S(2)}) copy-start(bf16[1,512,896]{2,1,0:T(8,128)(2,1)} %param.12) | copy-start | bytes 2752516
  12.0 13.9 %all-to-all-start = ((bf16[8,16,640]{2,1,0:T(8,128)(2,1)}), bf16[8,16,640]{2,1,0:T(8,128)(2,1)S(1)}, u32[]{:S(2)}, u32[]{:S(2)}) async-start(bf16[8,16,640]{2,1,0:T(8,128)(2,1)} %pad_maximum_fusion.1), calls=%async_computation | async-start | bytes 327680 | tf_op jit(solution)/shard_map/all_to_all | solution.py:218
  16.5 23.1 %collective-permute-start.1 = (bf16[512,896]{1,0:T(8,128)(2,1)S(1)}, bf16[512,896]{1,0:T(8,128)(2,1)S(1)}, u32[]{:S(2)}, u32[]{:S(2)}) collective-permute-start(bf16[512,896]{1,0:T(8,128)(2,1)S(1)} %bitcast.79), channel_id=1, source_target_pairs={{0,0},{17,17},{1,16},{16,1},{2,2},{19,19},{3,18},{18,3},{4,4},{21,... | collective-permute-start | bytes 2752520 | tf_op jit(solution)/shard_map/ppermute | solution.py:44
  26.0 15.9 %collective-permute-start.3 = (bf16[512,896]{1,0:T(8,128)(2,1)}, bf16[512,896]{1,0:T(8,128)(2,1)S(1)}, u32[]{:S(2)}, u32[]{:S(2)}) collective-permute-start(bf16[512,896]{1,0:T(8,128)(2,1)} %bitcast.80), channel_id=1, source_target_pairs={{0,0},{17,17},{1,16},{16,1},{2,2},{19,19},{3,18},{18,3},{4,4},{21,... | collective-permute-start | bytes 2752520 | tf_op jit(solution)/shard_map/ppermute | solution.py:44
  29.0 27.5 %all-to-all-start.1 = ((bf16[16,32,512]{2,1,0:T(8,128)(2,1)}), bf16[16,32,512]{2,1,0:T(8,128)(2,1)S(1)}, u32[]{:S(2)}, u32[]{:S(2)}) async-start(bf16[16,32,512]{2,1,0:T(8,128)(2,1)} %broadcast_in_dim.74), calls=%async_computation.1 | async-start | bytes 1048576 | tf_op jit(solution)/shard_map/all_to_all | solution.py:174
  39.6 16.9 %collective-permute-start.2 = (bf16[512,896]{1,0:T(8,128)(2,1)S(1)}, bf16[512,896]{1,0:T(8,128)(2,1)S(1)}, u32[]{:S(2)}, u32[]{:S(2)}) collective-permute-start(bf16[512,896]{1,0:T(8,128)(2,1)S(1)} %collective-permute-done.1.w0), channel_id=1, source_target_pairs={{0,1},{1,0},{2,3},{3,2},{4,5},{5,4},{6,7},{7,6},{8,9},{9,8},{10,11... | collective-permute-start | bytes 2752520 | tf_op jit(solution)/shard_map/ppermute | solution.py:48
  41.9 18.4 %copy-start.1 = (bf16[512,896]{1,0:T(8,128)(2,1)}, bf16[512,896]{1,0:T(8,128)(2,1)S(1)}, u32[]{:S(2)}) copy-start(bf16[512,896]{1,0:T(8,128)(2,1)S(1)} %collective-permute-done.3.w2) | copy-start | bytes 2752516
  41.9 14.6 %collective-permute-start.4 = (bf16[512,896]{1,0:T(8,128)(2,1)S(1)}, bf16[512,896]{1,0:T(8,128)(2,1)}, u32[]{:S(2)}, u32[]{:S(2)}) collective-permute-start(bf16[512,896]{1,0:T(8,128)(2,1)S(1)} %collective-permute-done.3.w2), channel_id=1, source_target_pairs={{0,1},{1,0},{2,3},{3,2},{4,5},{5,4},{6,7},{7,6},{8,9},{9,8},{10,11... | collective-permute-start | bytes 2752520 | tf_op jit(solution)/shard_map/ppermute | solution.py:48
  60.3 5.5 %copy-start = (bf16[1,896,512]{2,1,0:T(8,128)(2,1)S(1)}, bf16[1,896,512]{2,1,0:T(8,128)(2,1)}, u32[]{:S(2)}) copy-start(bf16[1,896,512]{2,1,0:T(8,128)(2,1)} %param.14) | copy-start | bytes 2752516
  60.3 28.3 %all-to-all-start.2 = ((bf16[4,64,1920]{2,1,0:T(8,128)(2,1)}), bf16[4,64,1920]{2,1,0:T(8,128)(2,1)S(1)}, u32[]{:S(2)}, u32[]{:S(2)}) async-start(bf16[4,64,1920]{2,1,0:T(8,128)(2,1)} %bitcast.8), calls=%async_computation.2 | async-start | bytes 1966080 | tf_op jit(solution)/shard_map/all_to_all | solution.py:180
  65.8 49.9 %collective-permute-start.5 = (bf16[896,512]{1,0:T(8,128)(2,1)S(1)}, bf16[896,512]{1,0:T(8,128)(2,1)}, u32[]{:S(2)}, u32[]{:S(2)}) collective-permute-start(bf16[896,512]{1,0:T(8,128)(2,1)S(1)} %bitcast.70), channel_id=1, source_target_pairs={{0,1},{1,0},{2,3},{3,2},{4,5},{5,4},{6,7},{7,6},{8,9},{9,8},{10,11... | collective-permute-start | bytes 2752520 | tf_op jit(solution)/shard_map/ppermute | solution.py:48
  118.6 16.5 %all-to-all-start.3 = ((bf16[8,32,512]{2,1,0:T(8,128)(2,1)}), bf16[8,32,512]{2,1,0:T(8,128)(2,1)S(1)}, u32[]{:S(2)}, u32[]{:S(2)}) async-start(bf16[8,32,512]{2,1,0:T(8,128)(2,1)} %bitcast.13), calls=%async_computation.3 | async-start | bytes 524288 | tf_op jit(solution)/shard_map/all_to_all | solution.py:187
  135.4 5.8 %collective-permute-start.6 = (bf16[32,512]{1,0:T(8,128)(2,1)S(1)}, bf16[32,512]{1,0:T(8,128)(2,1)S(1)}, u32[]{:S(2)}, u32[]{:S(2)}) collective-permute-start(bf16[32,512]{1,0:T(8,128)(2,1)S(1)} %fusion.3), channel_id=1, source_target_pairs={{0,128},{128,256},{256,384},{384,0},{1,129},{129,257},{257,385},{3... | collective-permute-start | bytes 98312 | tf_op jit(solution)/shard_map/ppermute | solution.py:246
  142.0 14.1 %copy-start.2 = (bf16[512,896]{1,0:T(8,128)(2,1)S(1)}, bf16[512,896]{1,0:T(8,128)(2,1)}, u32[]{:S(2)}) copy-start(bf16[512,896]{1,0:T(8,128)(2,1)} %copy-done.1) | copy-start | bytes 2752516
  142.0 14.1 %all-to-all-start.4 = ((bf16[16,32,512]{2,1,0:T(8,128)(2,1)}), bf16[16,32,512]{2,1,0:T(8,128)(2,1)S(1)}, u32[]{:S(2)}, u32[]{:S(2)}) async-start(bf16[16,32,512]{2,1,0:T(8,128)(2,1)} %broadcast_in_dim.76), calls=%async_computation.4 | async-start | bytes 1048576 | tf_op jit(solution)/shard_map/all_to_all | solution.py:174
  145.7 14.4 %collective-permute-start.8 = (bf16[64,4096]{1,0:T(8,128)(2,1)}, bf16[64,4096]{1,0:T(8,128)(2,1)}, u32[]{:S(2)}, u32[]{:S(2)}) collective-permute-start(bf16[64,4096]{1,0:T(8,128)(2,1)} %bitcast.73), channel_id=1, source_target_pairs={{0,128},{128,256},{256,384},{1,129},{129,257},{257,385},{2,130},{1... | collective-permute-start | bytes 1572872 | tf_op jit(solution)/shard_map/ppermute | solution.py:238
  147.4 12.7 %collective-permute-start.7 = (bf16[128,640]{1,0:T(8,128)(2,1)S(1)}, bf16[128,640]{1,0:T(8,128)(2,1)}, u32[]{:S(2)}, u32[]{:S(2)}) collective-permute-start(bf16[128,640]{1,0:T(8,128)(2,1)S(1)} %pad_maximum_fusion.2), channel_id=1, source_target_pairs={{0,128},{128,256},{256,384},{384,0},{1,129},{129,257},{257,385},{3... | collective-permute-start | bytes 491528 | tf_op jit(solution)/shard_map/ppermute | solution.py:249
  212.5 16.8 %all-to-all-start.6 = ((bf16[8,32,512]{2,1,0:T(8,128)(2,1)}), bf16[8,32,512]{2,1,0:T(8,128)(2,1)S(1)}, u32[]{:S(2)}, u32[]{:S(2)}) async-start(bf16[8,32,512]{2,1,0:T(8,128)(2,1)} %bitcast.23), calls=%async_computation.6 | async-start | bytes 524288 | tf_op jit(solution)/shard_map/all_to_all | solution.py:187
  219.9 9.4 %copy-start.10 = (bf16[32,512]{1,0:T(8,128)(2,1)S(1)}, bf16[32,512]{1,0:T(8,128)(2,1)}, u32[]{:S(2)}) copy-start(bf16[32,512]{1,0:T(8,128)(2,1)} %copy-done.9) | copy-start | bytes 98308
  231.1 13.8 %all-to-all-start.7 = ((bf16[8,3,8,640]{3,2,1,0:T(8,128)(2,1)}), bf16[8,3,8,640]{3,2,1,0:T(8,128)(2,1)S(1)}, u32[]{:S(2)}, u32[]{:S(2)}) async-start(bf16[8,3,8,640]{3,2,1,0:T(8,128)(2,1)} %pad_maximum_fusion), calls=%async_computation.7 | async-start | bytes 491520 | tf_op jit(solution)/shard_map/all_to_all | solution.py:259
  234.6 10.7 %copy-start.6 = (bf16[1,64,4096]{2,1,0:T(8,128)(2,1)S(1)}, bf16[1,64,4096]{2,1,0:T(8,128)(2,1)}, u32[]{:S(2)}) copy-start(bf16[1,64,4096]{2,1,0:T(8,128)(2,1)} %param.8) | copy-start | bytes 1572868
  (5 other events, 10.5 us)

commit v7 on v6

--- a/solution.py
+++ b/solution.py
@@ -52,20 +52,20 @@
     return lax.optimization_barrier((x, *others))
 
 
-def project_body(core_ref, g_ref, gain_ref, scorer_ref, w0, w1, w2, w3, out_ref, held, sems):
+def project_body(side_dim, core_ref, g_ref, gain_ref, scorer_ref, w0, w1, w2, w3, out_ref, held, sems):
     copies = [pltpu.make_async_copy(w, held.at[i], sems.at[i]) for i, w in enumerate((w0, w1, w2, w3))]
     for copy in copies:
         copy.start()
     core = core_ref[0]
-    half = g_ref.shape[0] // 2
     width, units = w0.shape
     n = out_ref.shape[0]
     ss = jnp.zeros((n, 1), F32)
     dot = jnp.zeros((n, 1), F32)
     x = []
     for k in range(2):
-        first = pl.multiple_of((core if k == 0 else 1 - core) * half, half)
-        v = g_ref[pl.ds(first, half)].reshape(n, width).astype(F32)
+        side = pl.ds(core if k == 0 else 1 - core, 1)
+        v = g_ref[side] if side_dim == 0 else g_ref[:, side]
+        v = v.reshape(n, width).astype(F32)
         ss = ss + jnp.sum(v * v, axis=1, keepdims=True)
         dot = dot + jnp.sum(v * scorer_ref[k : k + 1, :], axis=1, keepdims=True)
         x.append((v * gain_ref[k : k + 1, :]).astype(BF))
@@ -82,13 +82,13 @@
         out_ref[:, j * units : (j + 1) * units] = total.astype(BF)
 
 
-def project(g, gains, scorers, wg, wu, core):
-    n = g.shape[0] // 2 * g.shape[1]
+def project(g, side_dim, gains, scorers, wg, wu, core):
+    n = g.shape[0] * g.shape[1] // 2 * g.shape[2]
     width, units = wg[0].shape
     vmem = pl.BlockSpec(memory_space=pltpu.VMEM)
     anywhere = pl.BlockSpec(memory_space=pl.ANY)
     return pl.pallas_call(
-        project_body,
+        functools.partial(project_body, side_dim),
         out_shape=jax.ShapeDtypeStruct((n, 2 * units + 128), BF),
         in_specs=[pl.BlockSpec(memory_space=pltpu.SMEM), vmem, vmem, vmem] + [anywhere] * 4,
         out_specs=vmem,
@@ -165,16 +165,19 @@
     )(jnp.reshape(core, (1,)).astype(jnp.int32), hidden, wd[0], wd[1])
 
 
-def tick(v, gains, scorers, wg, wu, wd, late, z, core):
+def tick(v, both, gains, scorers, wg, wu, wd, late, z, core):
     rows, width = v.shape
     n_z = lax.axis_size("z")
     n_q = lax.axis_size("q")
     everyone = n_z * rows
     chunk = everyone // n_q
-    g = lax.all_to_all(
-        jnp.broadcast_to(v[None], (2 * n_z, rows, width)), PLANE, 0, 0, tiled=True
-    )
-    part = project(g, gains, scorers, wg, wu, core)
+    if both is None:
+        g = lax.all_to_all(jnp.broadcast_to(v[None], (2 * n_z, rows, width)), PLANE, 0, 0, tiled=True)
+        g, side_dim = g.reshape(2, n_z, rows, width), 0
+    else:
+        g = lax.all_to_all(jnp.broadcast_to(both[None], (n_z,) + both.shape), "z", 0, 0, tiled=True)
+        side_dim = 1
+    part = project(g, side_dim, gains, scorers, wg, wu, core)
     units = wg[0].shape[1]
     part, *late = after(part, *late)
     part = lax.all_to_all(part.reshape(n_q, chunk, -1), "q", 0, 0, tiled=True)
@@ -210,14 +213,18 @@
     hit2 = e2_next[:, None] == at
     b2 = jnp.dot((hit2 & wrap).astype(BF), arriving, preferred_element_type=F32)
     b2 = (b2 + jnp.dot((hit2 & ~wrap).astype(BF), pending, preferred_element_type=F32)).astype(BF)
-    both = jnp.concatenate([v1, b2], axis=0).reshape(2 * cap, n_dp, cut).transpose(1, 0, 2)
-    codes = lanes([jnp.concatenate([e1, e2_next]).astype(BF)], 2 * cap)
-    both = jnp.concatenate([both, jnp.broadcast_to(codes[None], (n_dp, 2 * cap, 128))], axis=2)
-    both, w_g = after(both, w_gate[0])
+    pairs = v1.reshape(cap, n_dp // 2, 1, 2, cut).transpose(1, 2, 3, 0, 4)
+    pairs = jnp.broadcast_to(pairs, (n_dp // 2, 2, 2, cap, cut)).reshape(n_dp, 2 * cap, cut)
+    both = jnp.concatenate([pairs, b2.reshape(cap, n_dp, cut).transpose(1, 0, 2)], axis=1)
+    codes = lanes([jnp.concatenate([e1, e1, e2_next]).astype(BF)], 3 * cap)
+    both = jnp.concatenate([both, jnp.broadcast_to(codes[None], (n_dp, 3 * cap, 128))], axis=2)
+    both, w_g, w_u = after(both, w_gate[0], w_up[0])
     wg = cross(w_g)
+    wu = cross(w_u)
     got = lax.all_to_all(both, DP, 0, 0, tiled=True)
     slots1 = got[:, :cap].reshape(n_dp * cap, -1)
-    slots2 = got[:, cap:].reshape(n_dp * cap, -1)
+    far1 = got[:, cap : 2 * cap].reshape(n_dp * cap, -1)
+    slots2 = got[:, 2 * cap :].reshape(n_dp * cap, -1)
     c1 = slots1[:, cut].astype(jnp.int32)
     c2 = slots2[:, cut].astype(jnp.int32)
     block = jnp.arange(n_dp * cap, dtype=jnp.int32) // cap
@@ -227,10 +234,10 @@
     same = (same & (s < n_seg - 1)).astype(BF)
     hit = pick(pick(comp2, same), comp1.T)
     has = jnp.sum(hit.astype(F32), axis=1)[:, None] > 0
-    v1c = pick(comp1, slots1[:, :cut])
+    pair1 = jnp.stack([pick(comp1, slots1[:, :cut]), pick(comp1, far1[:, :cut])])
+    v1c = jnp.where(lax.axis_index("h") == 0, pair1[0], pair1[1])
     b2c = pick(comp2, slots2[:, :cut])
 
-    wu = cross(after(w_up[0], got)[0])
     wg = (wg, sibling(wg))
     wu = (wu, sibling(wu))
     wd = (w_down[0], sibling(w_down[0]))
@@ -241,7 +248,7 @@
         return jnp.stack([lax.dynamic_slice_in_dim(row[0], (2 * q + (core ^ k)) * cut, cut, 0) for k in range(2)])
 
     gains, scorers = slices(gain), slices(scorer)
-    up1, _ = tick(v1c, gains, scorers, wg, wu, wd, [], z, core)
+    up1, _ = tick(v1c, pair1, gains, scorers, wg, wu, wd, [], z, core)
     v2n = jnp.where(has, pick(hit, up1), b2c)
     v2c = lax.ppermute(v2n, "segment", ahead)
     up1_slots = jnp.concatenate([pick(comp1.T, up1), slots1[:, cut:]], axis=1)
@@ -251,7 +258,7 @@
         "segment",
         ahead,
     )
-    up2, (before, base) = tick(v2c, gains, scorers, wg, wu, wd, [before, base], z, core)
+    up2, (before, base) = tick(v2c, None, gains, scorers, wg, wu, wd, [before, base], z, core)
     own_comp2 = before[n_dp * cap :, :compact]
     before = before[: n_dp * cap]
     up2_slots = jnp.concatenate([pick(own_comp2, up2), slots1[:, cut:]], axis=1)

time: 251 us -> 250 us (level)
  waiting for transfers between devices: 83.9 us -> 79.2 us
  starting transfers between devices: 58.8 us -> 61.4 us
    all_to_all x2 -> x1, waiting for transfers between devices: 16.5 us -> 4.12 us  [tick(): lax.all_to_all(jnp.broadcast_to(v[None], (2 * n_z, rows, width)), PLANE,...]
    all_to_all x2 -> x1, starting transfers between devices: 14.2 us -> 3.71 us  [tick(): lax.all_to_all(jnp.broadcast_to(v[None], (2 * n_z, rows, width)), PLANE,...]
    all_to_all x0 -> x1, starting transfers between devices: none -> 10.3 us  [tick(): lax.all_to_all(jnp.broadcast_to(both[None], (n_z,) + both.shape), 'z', 0,...]
    all_to_all x0 -> x1, waiting for transfers between devices: none -> 7.83 us  [tick(): lax.all_to_all(jnp.broadcast_to(both[None], (n_z,) + both.shape), 'z', 0,...]
    dot_general x9 -> x10, matrix products: 4.94 us -> 5.02 us  [pick(): return jnp.dot(onehot, x, preferred_element_type=F32).astype(BF)]
where the time goes in v7:
time: 250 us; the launch traced here: 249 us
  waiting for transfers between devices  79.2 us (32%)
  blocking collectives  76.7 us (31%)
  starting transfers between devices  61.4 us (25%)
  Pallas kernels  12.7 us (5%)
  other arithmetic  6.16 us (2%)
  local copies, waits for them, and re-layouts  5.9 us (2%)
  matrix products  5.51 us (2%)
    all_gather x2, blocking collectives, tick(): lax.all_gather(hidden, DP, axis=0, tiled=True).reshape(n_q, 2, chunk, -1)  53.4 us
    all_to_all x1, blocking collectives, tick(): part = lax.all_to_all(part.reshape(n_q, chunk, -1), 'q', 0, 0, tiled=True)  23.3 us
    all_to_all x1, waiting for transfers between devices, tick(): part = lax.all_to_all(part.reshape(n_q, chunk, -1), 'q', 0, 0, tiled=True)  21.1 us
    all_to_all x2, waiting for transfers between devices, tick(): out = lax.all_to_all(out.reshape(n_z, rows, width), 'z', 0, 0, tiled=True)  19.5 us
    all_to_all x2, starting transfers between devices, tick(): out = lax.all_to_all(out.reshape(n_z, rows, width), 'z', 0, 0, tiled=True)  13.5 us
    all_to_all x1, starting transfers between devices, tick(): lax.all_to_all(jnp.broadcast_to(both[None], (n_z,) + both.shape), 'z', 0,...  10.3 us
    all_to_all x1, waiting for transfers between devices, local(): back = lax.all_to_all(back, DP, 0, 0, tiled=True)  10.1 us
    all_to_all x1, waiting for transfers between devices, local(): got = lax.all_to_all(both, DP, 0, 0, tiled=True)  8.21 us
  transfers between devices with their start and end apart: 16, of which 9 were waited for; matrix products, arithmetic and copies ran while one was open for 2% of the time, Pallas kernels for 1%

profile of v7, /device:TPU:6, one launch (start us, length us, event | category | flops | bytes accessed | tf_op | source)
XLA Modules:
  0.0 248.7 jit_solution(10976634270518866899)
XLA Ops:
  5.5 5.2 %collective-permute-done = s32[8]{0:T(128)S(1)} collective-permute-done((s32[8]{0:T(128)S(1)}, s32[8]{0:T(128)S(1)}, u32[]{:S(2)}, u32[]{:S(2)}) %collective-permute-start) | collective-permute-done | bytes 64 | tf_op jit(solution)/shard_map/ppermute | solution.py:209
  12.1 4.5 %all-to-all-start = ((bf16[8,24,640]{2,1,0:T(8,128)(2,1)}), bf16[8,24,640]{2,1,0:T(8,128)(2,1)S(1)}, u32[]{:S(2)}, u32[]{:S(2)}) async-start(bf16[8,24,640]{2,1,0:T(8,128)(2,1)} %pad_maximum_fusion), calls=%async_computation | async-start | bytes 491520 | tf_op jit(solution)/shard_map/all_to_all | solution.py:224
  19.1 8.2 %all-to-all-done = bf16[8,24,640]{2,1,0:T(8,128)(2,1)S(1)} async-done(((bf16[8,24,640]{2,1,0:T(8,128)(2,1)}), bf16[8,24,640]{2,1,0:T(8,128)(2,1)S(1)}, u32[]{:S(2)}, u32[]{:S(2)}) %all-to-all-start) | async-done | bytes 245792 | tf_op jit(solution)/shard_map/all_to_all | solution.py:224
  28.7 10.3 %all-to-all-start.1 = ((bf16[8,2,32,512]{3,2,1,0:T(8,128)(2,1)}), bf16[8,2,32,512]{3,2,1,0:T(8,128)(2,1)S(1)}, u32[]{:S(2)}, u32[]{:S(2)}) async-start(bf16[8,2,32,512]{3,2,1,0:T(8,128)(2,1)} %broadcast_in_dim.80), calls=%async_computation.1 | async-start | bytes 1048576 | tf_op jit(solution)/shard_map/all_to_all | solution.py:178
  41.0 3.9 %collective-permute-start.4 = (bf16[512,896]{1,0:T(8,128)(2,1)S(1)}, bf16[512,896]{1,0:T(8,128)(2,1)}, u32[]{:S(2)}, u32[]{:S(2)}) collective-permute-start(bf16[512,896]{1,0:T(8,128)(2,1)S(1)} %collective-permute-done.3.w2), channel_id=1, source_target_pairs={{0,1},{1,0},{2,3},{3,2},{4,5},{5,4},{6,7},{7,6},{8,9},{9,8},{10,11... | collective-permute-start | bytes 2752520 | tf_op jit(solution)/shard_map/ppermute | solution.py:48
  45.6 7.8 %all-to-all-done.1.g_ref = bf16[8,2,32,512]{3,2,1,0:T(8,128)(2,1)S(1)} async-done(((bf16[8,2,32,512]{3,2,1,0:T(8,128)(2,1)}), bf16[8,2,32,512]{3,2,1,0:T(8,128)(2,1)S(1)}, u32[]{:S(2)}, u32[]{:S(2)}) %all-to-all-start.1) | async-done | bytes 524320 | tf_op jit(solution)/shard_map/all_to_all | solution.py:178
  53.5 3.7 %shard_map.95 = bf16[256,1920]{1,0:T(8,128)(2,1)} custom-call(s32[1]{0:T(128)} %bitcast.13.core_ref, bf16[8,2,32,512]{3,2,1,0:T(8,128)(2,1)S(1)} %all-to-all-done.1.g_ref, f32[2,512]{1,0:T(2,128)S(1)} %pad_maximum_fusion.6.gain_ref, f32[2,512]{1,0:T(2,128)S(1)} %pad_maximum_fusion.7.scorer_ref, bf16[512,896]{1,0:T(8,128)(2,1)S(1)} %collective-permute-done.1.w0, ...), custom_call_target="tpu_custom_call" | custom-call | flops 939524096 | bytes 3670016 | tf_op jit(solution)/shard_map/pallas_call | solution.py:90
  57.3 4.3 %all-to-all-start.2 = ((bf16[4,64,1920]{2,1,0:T(8,128)(2,1)}), bf16[4,64,1920]{2,1,0:T(8,128)(2,1)S(1)}, u32[]{:S(2)}, u32[]{:S(2)}) async-start(bf16[4,64,1920]{2,1,0:T(8,128)(2,1)} %bitcast.16), calls=%async_computation.2 | async-start | bytes 1966080 | tf_op jit(solution)/shard_map/all_to_all | solution.py:183
  64.2 21.1 %all-to-all-done.2.part_ref = bf16[4,64,1920]{2,1,0:T(8,128)(2,1)S(1)} async-done(((bf16[4,64,1920]{2,1,0:T(8,128)(2,1)}), bf16[4,64,1920]{2,1,0:T(8,128)(2,1)S(1)}, u32[]{:S(2)}, u32[]{:S(2)}) %all-to-all-start.2) | async-done | bytes 983072 | tf_op jit(solution)/shard_map/all_to_all | solution.py:183
  85.6 26.7 %all_gather.6 = bf16[512,960]{1,0:T(8,128)(2,1)S(1)} all-gather(bf16[64,960]{1,0:T(8,128)(2,1)S(1)} %shard_map.96), channel_id=1, replica_groups=mesh['segment'=4,'q'=4,'h'=2,'z'=8,'core'=2] {'q','h'}, dimensions={0}, use_global_device_ids=true | all-gather | bytes 1105920 | tf_op jit(solution)/shard_map/all_gather | solution.py:185
  112.4 2.8 %shard_map.97 = bf16[256,512]{1,0:T(8,128)(2,1)} custom-call(s32[1]{0:T(128)} %bitcast.13.core_ref, bf16[4,2,64,960]{3,2,1,0:T(8,128)(2,1)S(1)} %bitcast.74, bf16[896,512]{1,0:T(8,128)(2,1)S(1)} %bitcast.80, bf16[896,512]{1,0:T(8,128)(2,1)} %collective-permute-done.5.w1), custom_call_target="tpu_custom_call" | custom-call | flops 469762048 | bytes 1835008 | tf_op jit(solution)/shard_map/pallas_call | solution.py:157
  115.2 7.6 %all-to-all-start.3 = ((bf16[8,32,512]{2,1,0:T(8,128)(2,1)}), bf16[8,32,512]{2,1,0:T(8,128)(2,1)S(1)}, u32[]{:S(2)}, u32[]{:S(2)}) async-start(bf16[8,32,512]{2,1,0:T(8,128)(2,1)} %bitcast.21), calls=%async_computation.3 | async-start | bytes 524288 | tf_op jit(solution)/shard_map/all_to_all | solution.py:190
  123.1 10.1 %all-to-all-done.3 = bf16[8,32,512]{2,1,0:T(8,128)(2,1)S(1)} async-done(((bf16[8,32,512]{2,1,0:T(8,128)(2,1)}), bf16[8,32,512]{2,1,0:T(8,128)(2,1)S(1)}, u32[]{:S(2)}, u32[]{:S(2)}) %all-to-all-start.3) | async-done | bytes 262176 | tf_op jit(solution)/shard_map/all_to_all | solution.py:190
  136.2 3.2 %collective-permute-done.6 = bf16[32,512]{1,0:T(8,128)(2,1)S(1)} collective-permute-done((bf16[32,512]{1,0:T(8,128)(2,1)S(1)}, bf16[32,512]{1,0:T(8,128)(2,1)S(1)}, u32[]{:S(2)}, u32[]{:S(2)}) %collective-permute-start.6) | collective-permute-done | bytes 32800 | tf_op jit(solution)/shard_map/ppermute | solution.py:253
  140.8 3.7 %all-to-all-start.4 = ((bf16[16,32,512]{2,1,0:T(8,128)(2,1)}), bf16[16,32,512]{2,1,0:T(8,128)(2,1)S(1)}, u32[]{:S(2)}, u32[]{:S(2)}) async-start(bf16[16,32,512]{2,1,0:T(8,128)(2,1)} %broadcast_in_dim.132), calls=%async_computation.4 | async-start | bytes 1048576 | tf_op jit(solution)/shard_map/all_to_all | solution.py:175
  146.2 4.6 %collective-permute-start.7 = (bf16[128,640]{1,0:T(8,128)(2,1)S(1)}, bf16[128,640]{1,0:T(8,128)(2,1)}, u32[]{:S(2)}, u32[]{:S(2)}) collective-permute-start(bf16[128,640]{1,0:T(8,128)(2,1)S(1)} %pad_maximum_fusion.2), channel_id=1, source_target_pairs={{0,128},{128,256},{256,384},{384,0},{1,129},{129,257},{257,385},{3... | collective-permute-start | bytes 491528 | tf_op jit(solution)/shard_map/ppermute | solution.py:256
  150.8 4.1 %all-to-all-done.4 = bf16[16,32,512]{2,1,0:T(8,128)(2,1)S(1)} async-done(((bf16[16,32,512]{2,1,0:T(8,128)(2,1)}), bf16[16,32,512]{2,1,0:T(8,128)(2,1)S(1)}, u32[]{:S(2)}, u32[]{:S(2)}) %all-to-all-start.4) | async-done | bytes 524320 | tf_op jit(solution)/shard_map/all_to_all | solution.py:175
  158.9 23.3 %all_to_all.40.part_ref = bf16[4,64,1920]{2,1,0:T(8,128)(2,1)S(1)} all-to-all(bf16[4,64,1920]{2,1,0:T(8,128)(2,1)S(1)} %bitcast.78), channel_id=1, replica_groups=mesh['segment'=4,'q'=4,'h'=2,'z'=8,'core'=2] {'q'}, dimensions={0} | all-to-all | bytes 1966080 | tf_op jit(solution)/shard_map/all_to_all | solution.py:183
  182.5 26.7 %all_gather.7 = bf16[512,960]{1,0:T(8,128)(2,1)S(1)} all-gather(bf16[64,960]{1,0:T(8,128)(2,1)S(1)} %shard_map.99), channel_id=1, replica_groups=mesh['segment'=4,'q'=4,'h'=2,'z'=8,'core'=2] {'q','h'}, dimensions={0}, use_global_device_ids=true | all-gather | bytes 1105920 | tf_op jit(solution)/shard_map/all_gather | solution.py:185
  209.1 2.8 %shard_map.100 = bf16[256,512]{1,0:T(8,128)(2,1)} custom-call(s32[1]{0:T(128)} %bitcast.13.core_ref, bf16[4,2,64,960]{3,2,1,0:T(8,128)(2,1)S(1)} %bitcast.76, bf16[896,512]{1,0:T(8,128)(2,1)S(1)} %bitcast.81, bf16[896,512]{1,0:T(8,128)(2,1)} %collective-permute-done.5.w1), custom_call_target="tpu_custom_call" | custom-call | flops 469762048 | bytes 1835008 | tf_op jit(solution)/shard_map/pallas_call | solution.py:157
  212.0 6.0 %all-to-all-start.6 = ((bf16[8,32,512]{2,1,0:T(8,128)(2,1)}), bf16[8,32,512]{2,1,0:T(8,128)(2,1)S(1)}, u32[]{:S(2)}, u32[]{:S(2)}) async-start(bf16[8,32,512]{2,1,0:T(8,128)(2,1)} %bitcast.32), calls=%async_computation.6 | async-start | bytes 524288 | tf_op jit(solution)/shard_map/all_to_all | solution.py:190
  219.1 9.4 %all-to-all-done.6 = bf16[8,32,512]{2,1,0:T(8,128)(2,1)S(1)} async-done(((bf16[8,32,512]{2,1,0:T(8,128)(2,1)}), bf16[8,32,512]{2,1,0:T(8,128)(2,1)S(1)}, u32[]{:S(2)}, u32[]{:S(2)}) %all-to-all-start.6) | async-done | bytes 262176 | tf_op jit(solution)/shard_map/all_to_all | solution.py:190
  230.2 3.5 %all-to-all-start.7 = ((bf16[8,3,8,640]{3,2,1,0:T(8,128)(2,1)}), bf16[8,3,8,640]{3,2,1,0:T(8,128)(2,1)S(1)}, u32[]{:S(2)}, u32[]{:S(2)}) async-start(bf16[8,3,8,640]{3,2,1,0:T(8,128)(2,1)} %pad_maximum_fusion.1), calls=%async_computation.7 | async-start | bytes 491520 | tf_op jit(solution)/shard_map/all_to_all | solution.py:266
  233.8 10.1 %all-to-all-done.7 = bf16[8,3,8,640]{3,2,1,0:T(8,128)(2,1)S(1)} async-done(((bf16[8,3,8,640]{3,2,1,0:T(8,128)(2,1)}), bf16[8,3,8,640]{3,2,1,0:T(8,128)(2,1)S(1)}, u32[]{:S(2)}, u32[]{:S(2)}) %all-to-all-start.7) | async-done | bytes 245792 | tf_op jit(solution)/shard_map/all_to_all | solution.py:266
  (104 shorter events, 33.9 us)
Async XLA Ops:
  0.6 10.2 %copy-start.5 = (bf16[1,64,4096]{2,1,0:T(8,128)(2,1)S(1)}, bf16[1,64,4096]{2,1,0:T(8,128)(2,1)}, u32[]{:S(2)}) copy-start(bf16[1,64,4096]{2,1,0:T(8,128)(2,1)} %param.8) | copy-start | bytes 1572868
  1.4 9.3 %collective-permute-start = (s32[8]{0:T(128)S(1)}, s32[8]{0:T(128)S(1)}, u32[]{:S(2)}, u32[]{:S(2)}) collective-permute-start(s32[8]{0:T(128)S(1)} %get-tuple-element.28), channel_id=1, source_target_pairs={{0,384},{128,0},{256,128},{384,256},{1,385},{129,1},{257,129},{385... | collective-permute-start | bytes 104 | tf_op jit(solution)/shard_map/ppermute | solution.py:209
  4.1 6.9 %copy-start.7 = (bf16[64,4096]{1,0:T(8,128)(2,1)S(1)}, bf16[64,4096]{1,0:T(8,128)(2,1)}, u32[]{:S(2)}) copy-start(bf16[64,4096]{1,0:T(8,128)(2,1)} %param.9) | copy-start | bytes 1572868
  11.0 5.5 %copy-start.12 = (bf16[1,512,896]{2,1,0:T(8,128)(2,1)S(1)}, bf16[1,512,896]{2,1,0:T(8,128)(2,1)}, u32[]{:S(2)}) copy-start(bf16[1,512,896]{2,1,0:T(8,128)(2,1)} %param.12) | copy-start | bytes 2752516
  12.1 15.3 %all-to-all-start = ((bf16[8,24,640]{2,1,0:T(8,128)(2,1)}), bf16[8,24,640]{2,1,0:T(8,128)(2,1)S(1)}, u32[]{:S(2)}, u32[]{:S(2)}) async-start(bf16[8,24,640]{2,1,0:T(8,128)(2,1)} %pad_maximum_fusion), calls=%async_computation | async-start | bytes 491520 | tf_op jit(solution)/shard_map/all_to_all | solution.py:224
  16.5 22.5 %collective-permute-start.1 = (bf16[512,896]{1,0:T(8,128)(2,1)S(1)}, bf16[512,896]{1,0:T(8,128)(2,1)S(1)}, u32[]{:S(2)}, u32[]{:S(2)}) collective-permute-start(bf16[512,896]{1,0:T(8,128)(2,1)S(1)} %bitcast.92), channel_id=1, source_target_pairs={{0,0},{17,17},{1,16},{16,1},{2,2},{19,19},{3,18},{18,3},{4,4},{21,... | collective-permute-start | bytes 2752520 | tf_op jit(solution)/shard_map/ppermute | solution.py:44
  17.3 23.7 %collective-permute-start.3 = (bf16[512,896]{1,0:T(8,128)(2,1)}, bf16[512,896]{1,0:T(8,128)(2,1)S(1)}, u32[]{:S(2)}, u32[]{:S(2)}) collective-permute-start(bf16[512,896]{1,0:T(8,128)(2,1)} %bitcast.93), channel_id=1, source_target_pairs={{0,0},{17,17},{1,16},{16,1},{2,2},{19,19},{3,18},{18,3},{4,4},{21,... | collective-permute-start | bytes 2752520 | tf_op jit(solution)/shard_map/ppermute | solution.py:44
  28.7 24.8 %all-to-all-start.1 = ((bf16[8,2,32,512]{3,2,1,0:T(8,128)(2,1)}), bf16[8,2,32,512]{3,2,1,0:T(8,128)(2,1)S(1)}, u32[]{:S(2)}, u32[]{:S(2)}) async-start(bf16[8,2,32,512]{3,2,1,0:T(8,128)(2,1)} %broadcast_in_dim.80), calls=%async_computation.1 | async-start | bytes 1048576 | tf_op jit(solution)/shard_map/all_to_all | solution.py:178
  39.0 14.5 %collective-permute-start.2 = (bf16[512,896]{1,0:T(8,128)(2,1)S(1)}, bf16[512,896]{1,0:T(8,128)(2,1)S(1)}, u32[]{:S(2)}, u32[]{:S(2)}) collective-permute-start(bf16[512,896]{1,0:T(8,128)(2,1)S(1)} %collective-permute-done.1.w0), channel_id=1, source_target_pairs={{0,1},{1,0},{2,3},{3,2},{4,5},{5,4},{6,7},{7,6},{8,9},{9,8},{10,11... | collective-permute-start | bytes 2752520 | tf_op jit(solution)/shard_map/ppermute | solution.py:48
  41.0 16.3 %copy-start.1 = (bf16[512,896]{1,0:T(8,128)(2,1)}, bf16[512,896]{1,0:T(8,128)(2,1)S(1)}, u32[]{:S(2)}) copy-start(bf16[512,896]{1,0:T(8,128)(2,1)S(1)} %collective-permute-done.3.w2) | copy-start | bytes 2752516
  41.0 12.5 %collective-permute-start.4 = (bf16[512,896]{1,0:T(8,128)(2,1)S(1)}, bf16[512,896]{1,0:T(8,128)(2,1)}, u32[]{:S(2)}, u32[]{:S(2)}) collective-permute-start(bf16[512,896]{1,0:T(8,128)(2,1)S(1)} %collective-permute-done.3.w2), channel_id=1, source_target_pairs={{0,1},{1,0},{2,3},{3,2},{4,5},{5,4},{6,7},{7,6},{8,9},{9,8},{10,11... | collective-permute-start | bytes 2752520 | tf_op jit(solution)/shard_map/ppermute | solution.py:48
  57.3 4.3 %copy-start = (bf16[1,896,512]{2,1,0:T(8,128)(2,1)S(1)}, bf16[1,896,512]{2,1,0:T(8,128)(2,1)}, u32[]{:S(2)}) copy-start(bf16[1,896,512]{2,1,0:T(8,128)(2,1)} %param.14) | copy-start | bytes 2752516
  57.3 28.1 %all-to-all-start.2 = ((bf16[4,64,1920]{2,1,0:T(8,128)(2,1)}), bf16[4,64,1920]{2,1,0:T(8,128)(2,1)S(1)}, u32[]{:S(2)}, u32[]{:S(2)}) async-start(bf16[4,64,1920]{2,1,0:T(8,128)(2,1)} %bitcast.16), calls=%async_computation.2 | async-start | bytes 1966080 | tf_op jit(solution)/shard_map/all_to_all | solution.py:183
  61.6 50.8 %collective-permute-start.5 = (bf16[896,512]{1,0:T(8,128)(2,1)S(1)}, bf16[896,512]{1,0:T(8,128)(2,1)}, u32[]{:S(2)}, u32[]{:S(2)}) collective-permute-start(bf16[896,512]{1,0:T(8,128)(2,1)S(1)} %bitcast.79), channel_id=1, source_target_pairs={{0,1},{1,0},{2,3},{3,2},{4,5},{5,4},{6,7},{7,6},{8,9},{9,8},{10,11... | collective-permute-start | bytes 2752520 | tf_op jit(solution)/shard_map/ppermute | solution.py:48
  115.2 18.0 %all-to-all-start.3 = ((bf16[8,32,512]{2,1,0:T(8,128)(2,1)}), bf16[8,32,512]{2,1,0:T(8,128)(2,1)S(1)}, u32[]{:S(2)}, u32[]{:S(2)}) async-start(bf16[8,32,512]{2,1,0:T(8,128)(2,1)} %bitcast.21), calls=%async_computation.3 | async-start | bytes 524288 | tf_op jit(solution)/shard_map/all_to_all | solution.py:190
  133.6 5.8 %collective-permute-start.6 = (bf16[32,512]{1,0:T(8,128)(2,1)S(1)}, bf16[32,512]{1,0:T(8,128)(2,1)S(1)}, u32[]{:S(2)}, u32[]{:S(2)}) collective-permute-start(bf16[32,512]{1,0:T(8,128)(2,1)S(1)} %fusion.3), channel_id=1, source_target_pairs={{0,128},{128,256},{256,384},{384,0},{1,129},{129,257},{257,385},{3... | collective-permute-start | bytes 98312 | tf_op jit(solution)/shard_map/ppermute | solution.py:253
  140.8 14.1 %copy-start.2 = (bf16[512,896]{1,0:T(8,128)(2,1)S(1)}, bf16[512,896]{1,0:T(8,128)(2,1)}, u32[]{:S(2)}) copy-start(bf16[512,896]{1,0:T(8,128)(2,1)} %copy-done.1) | copy-start | bytes 2752516
  140.8 14.1 %all-to-all-start.4 = ((bf16[16,32,512]{2,1,0:T(8,128)(2,1)}), bf16[16,32,512]{2,1,0:T(8,128)(2,1)S(1)}, u32[]{:S(2)}, u32[]{:S(2)}) async-start(bf16[16,32,512]{2,1,0:T(8,128)(2,1)} %broadcast_in_dim.132), calls=%async_computation.4 | async-start | bytes 1048576 | tf_op jit(solution)/shard_map/all_to_all | solution.py:175
  144.5 14.4 %collective-permute-start.8 = (bf16[64,4096]{1,0:T(8,128)(2,1)}, bf16[64,4096]{1,0:T(8,128)(2,1)}, u32[]{:S(2)}, u32[]{:S(2)}) collective-permute-start(bf16[64,4096]{1,0:T(8,128)(2,1)} %bitcast.83), channel_id=1, source_target_pairs={{0,128},{128,256},{256,384},{1,129},{129,257},{257,385},{2,130},{1... | collective-permute-start | bytes 1572872 | tf_op jit(solution)/shard_map/ppermute | solution.py:245
  146.2 12.7 %collective-permute-start.7 = (bf16[128,640]{1,0:T(8,128)(2,1)S(1)}, bf16[128,640]{1,0:T(8,128)(2,1)}, u32[]{:S(2)}, u32[]{:S(2)}) collective-permute-start(bf16[128,640]{1,0:T(8,128)(2,1)S(1)} %pad_maximum_fusion.2), channel_id=1, source_target_pairs={{0,128},{128,256},{256,384},{384,0},{1,129},{129,257},{257,385},{3... | collective-permute-start | bytes 491528 | tf_op jit(solution)/shard_map/ppermute | solution.py:256
  212.0 16.4 %all-to-all-start.6 = ((bf16[8,32,512]{2,1,0:T(8,128)(2,1)}), bf16[8,32,512]{2,1,0:T(8,128)(2,1)S(1)}, u32[]{:S(2)}, u32[]{:S(2)}) async-start(bf16[8,32,512]{2,1,0:T(8,128)(2,1)} %bitcast.32), calls=%async_computation.6 | async-start | bytes 524288 | tf_op jit(solution)/shard_map/all_to_all | solution.py:190
  219.0 9.4 %copy-start.10 = (bf16[32,512]{1,0:T(8,128)(2,1)S(1)}, bf16[32,512]{1,0:T(8,128)(2,1)}, u32[]{:S(2)}) copy-start(bf16[32,512]{1,0:T(8,128)(2,1)} %copy-done.9) | copy-start | bytes 98308
  230.2 13.8 %all-to-all-start.7 = ((bf16[8,3,8,640]{3,2,1,0:T(8,128)(2,1)}), bf16[8,3,8,640]{3,2,1,0:T(8,128)(2,1)S(1)}, u32[]{:S(2)}, u32[]{:S(2)}) async-start(bf16[8,3,8,640]{3,2,1,0:T(8,128)(2,1)} %pad_maximum_fusion.1), calls=%async_computation.7 | async-start | bytes 491520 | tf_op jit(solution)/shard_map/all_to_all | solution.py:266
  233.7 10.7 %copy-start.6 = (bf16[1,64,4096]{2,1,0:T(8,128)(2,1)S(1)}, bf16[1,64,4096]{2,1,0:T(8,128)(2,1)}, u32[]{:S(2)}) copy-start(bf16[1,64,4096]{2,1,0:T(8,128)(2,1)} %param.8) | copy-start | bytes 1572868
  (5 other events, 10.3 us)

commit v8 on v7

--- a/solution.py
+++ b/solution.py
@@ -243,6 +243,7 @@
     wd = (w_down[0], sibling(w_down[0]))
     ahead = [(i, (i + 1) % n_seg) for i in range(n_seg)]
     base = lax.ppermute(pending, "segment", ahead[:-1])
+    e1_before = lax.ppermute(e1, "segment", ahead)
 
     def slices(row):
         return jnp.stack([lax.dynamic_slice_in_dim(row[0], (2 * q + (core ^ k)) * cut, cut, 0) for k in range(2)])
@@ -251,21 +252,20 @@
     up1, _ = tick(v1c, pair1, gains, scorers, wg, wu, wd, [], z, core)
     v2n = jnp.where(has, pick(hit, up1), b2c)
     v2c = lax.ppermute(v2n, "segment", ahead)
-    up1_slots = jnp.concatenate([pick(comp1.T, up1), slots1[:, cut:]], axis=1)
+    up1_slots = pick(comp1.T, up1)
     comp2_slots = comp2.T
     before = lax.ppermute(
-        jnp.concatenate([up1_slots, jnp.concatenate([comp2_slots, jnp.zeros((n_dp * cap, cut + 128 - compact), BF)], axis=1)], axis=0),
+        jnp.concatenate([up1_slots, jnp.concatenate([comp2_slots, jnp.zeros((n_dp * cap, cut - compact), BF)], axis=1)], axis=0),
         "segment",
         ahead,
     )
-    up2, (before, base) = tick(v2c, None, gains, scorers, wg, wu, wd, [before, base], z, core)
+    up2, (before, base, e1_before) = tick(v2c, None, gains, scorers, wg, wu, wd, [before, base, e1_before], z, core)
     own_comp2 = before[n_dp * cap :, :compact]
     before = before[: n_dp * cap]
-    up2_slots = jnp.concatenate([pick(own_comp2, up2), slots1[:, cut:]], axis=1)
+    up2_slots = pick(own_comp2, up2)
     back = jnp.stack([x.reshape(n_dp, cap, -1) for x in (up1_slots, before, up2_slots)], axis=1)
     back = lax.all_to_all(back, DP, 0, 0, tiled=True)
-    e1_before = back[0, 1, :, cut].astype(jnp.int32)
-    rows = back[..., :cut].transpose(1, 2, 0, 3).reshape(3, cap, width)
+    rows = back.transpose(1, 2, 0, 3).reshape(3, cap, width)
 
     def put(into, at, new):
         onehot = jnp.arange(n_rows, dtype=jnp.int32)[:, None] == at[None, :]

time: 250 us -> 251 us (level)
  blocking collectives: 76.7 us -> 53.3 us
  waiting for transfers between devices: 79.2 us -> 96.1 us
  starting transfers between devices: 61.4 us -> 67.1 us
    all_to_all x1 -> x0, blocking collectives: 23.3 us -> none  [tick(): part = lax.all_to_all(part.reshape(n_q, chunk, -1), 'q', 0, 0, tiled=True)]
    all_to_all x1 -> x2, waiting for transfers between devices: 21.1 us -> 40.8 us  [tick(): part = lax.all_to_all(part.reshape(n_q, chunk, -1), 'q', 0, 0, tiled=True)]
    all_to_all x1 -> x2, starting transfers between devices: 4.3 us -> 8.13 us  [tick(): part = lax.all_to_all(part.reshape(n_q, chunk, -1), 'q', 0, 0, tiled=True)]
  transfers between devices with their start and end apart: 16 -> 18, of which waited for: 9 -> 10; matrix products, arithmetic and copies ran while one was open for 2% -> 2% of each run, Pallas kernels for 1% -> 2%
where the time goes in v8:
time: 251 us; the launch traced here: 248 us
  waiting for transfers between devices  96.1 us (38%)
  starting transfers between devices  67.1 us (27%)
  blocking collectives  53.3 us (21%)
  Pallas kernels  13.6 us (5%)
  other arithmetic  5.87 us (2%)
  local copies, waits for them, and re-layouts  5.81 us (2%)
  matrix products  5.49 us (2%)
    all_gather x2, blocking collectives, tick(): lax.all_gather(hidden, DP, axis=0, tiled=True).reshape(n_q, 2, chunk, -1)  53.3 us
    all_to_all x2, waiting for transfers between devices, tick(): part = lax.all_to_all(part.reshape(n_q, chunk, -1), 'q', 0, 0, tiled=True)  40.8 us
    all_to_all x2, waiting for transfers between devices, tick(): out = lax.all_to_all(out.reshape(n_z, rows, width), 'z', 0, 0, tiled=True)  19.4 us
    all_to_all x2, starting transfers between devices, tick(): out = lax.all_to_all(out.reshape(n_z, rows, width), 'z', 0, 0, tiled=True)  12.5 us
    all_to_all x1, starting transfers between devices, tick(): lax.all_to_all(jnp.broadcast_to(both[None], (n_z,) + both.shape), 'z', 0,...  10.3 us
    all_to_all x1, waiting for transfers between devices, local(): back = lax.all_to_all(back, DP, 0, 0, tiled=True)  9.6 us
    all_to_all x1, waiting for transfers between devices, local(): got = lax.all_to_all(both, DP, 0, 0, tiled=True)  8.21 us
    all_to_all x2, starting transfers between devices, tick(): part = lax.all_to_all(part.reshape(n_q, chunk, -1), 'q', 0, 0, tiled=True)  8.13 us
  transfers between devices with their start and end apart: 18, of which 10 were waited for; matrix products, arithmetic and copies ran while one was open for 2% of the time, Pallas kernels for 2%

profile of v8, /device:TPU:6, one launch (start us, length us, event | category | flops | bytes accessed | tf_op | source)
XLA Modules:
  0.0 248.4 jit_solution(5433286419187571540)
XLA Ops:
  5.5 5.2 %collective-permute-done = s32[8]{0:T(128)S(1)} collective-permute-done((s32[8]{0:T(128)S(1)}, s32[8]{0:T(128)S(1)}, u32[]{:S(2)}, u32[]{:S(2)}) %collective-permute-start) | collective-permute-done | bytes 64 | tf_op jit(solution)/shard_map/ppermute | solution.py:209
  12.1 4.5 %all-to-all-start = ((bf16[8,24,640]{2,1,0:T(8,128)(2,1)}), bf16[8,24,640]{2,1,0:T(8,128)(2,1)S(1)}, u32[]{:S(2)}, u32[]{:S(2)}) async-start(bf16[8,24,640]{2,1,0:T(8,128)(2,1)} %pad_maximum_fusion), calls=%async_computation | async-start | bytes 491520 | tf_op jit(solution)/shard_map/all_to_all | solution.py:224
  19.1 8.2 %all-to-all-done = bf16[8,24,640]{2,1,0:T(8,128)(2,1)S(1)} async-done(((bf16[8,24,640]{2,1,0:T(8,128)(2,1)}), bf16[8,24,640]{2,1,0:T(8,128)(2,1)S(1)}, u32[]{:S(2)}, u32[]{:S(2)}) %all-to-all-start) | async-done | bytes 245792 | tf_op jit(solution)/shard_map/all_to_all | solution.py:224
  28.7 10.3 %all-to-all-start.1 = ((bf16[8,2,32,512]{3,2,1,0:T(8,128)(2,1)}), bf16[8,2,32,512]{3,2,1,0:T(8,128)(2,1)S(1)}, u32[]{:S(2)}, u32[]{:S(2)}) async-start(bf16[8,2,32,512]{3,2,1,0:T(8,128)(2,1)} %broadcast_in_dim.80), calls=%async_computation.1 | async-start | bytes 1048576 | tf_op jit(solution)/shard_map/all_to_all | solution.py:178
  41.0 3.9 %collective-permute-start.4 = (bf16[512,896]{1,0:T(8,128)(2,1)S(1)}, bf16[512,896]{1,0:T(8,128)(2,1)}, u32[]{:S(2)}, u32[]{:S(2)}) collective-permute-start(bf16[512,896]{1,0:T(8,128)(2,1)S(1)} %collective-permute-done.3.w2), channel_id=1, source_target_pairs={{0,1},{1,0},{2,3},{3,2},{4,5},{5,4},{6,7},{7,6},{8,9},{9,8},{10,11... | collective-permute-start | bytes 2752520 | tf_op jit(solution)/shard_map/ppermute | solution.py:48
  45.6 7.8 %all-to-all-done.1.g_ref = bf16[8,2,32,512]{3,2,1,0:T(8,128)(2,1)S(1)} async-done(((bf16[8,2,32,512]{3,2,1,0:T(8,128)(2,1)}), bf16[8,2,32,512]{3,2,1,0:T(8,128)(2,1)S(1)}, u32[]{:S(2)}, u32[]{:S(2)}) %all-to-all-start.1) | async-done | bytes 524320 | tf_op jit(solution)/shard_map/all_to_all | solution.py:178
  53.5 3.7 %shard_map.95 = bf16[256,1920]{1,0:T(8,128)(2,1)} custom-call(s32[1]{0:T(128)} %bitcast.13.core_ref, bf16[8,2,32,512]{3,2,1,0:T(8,128)(2,1)S(1)} %all-to-all-done.1.g_ref, f32[2,512]{1,0:T(2,128)S(1)} %pad_maximum_fusion.4.gain_ref, f32[2,512]{1,0:T(2,128)S(1)} %pad_maximum_fusion.5.scorer_ref, bf16[512,896]{1,0:T(8,128)(2,1)S(1)} %collective-permute-done.1.w0, ...), custom_call_target="tpu_custom_call" | custom-call | flops 939524096 | bytes 3670016 | tf_op jit(solution)/shard_map/pallas_call | solution.py:90
  57.3 4.3 %all-to-all-start.2 = ((bf16[4,64,1920]{2,1,0:T(8,128)(2,1)}), bf16[4,64,1920]{2,1,0:T(8,128)(2,1)S(1)}, u32[]{:S(2)}, u32[]{:S(2)}) async-start(bf16[4,64,1920]{2,1,0:T(8,128)(2,1)} %bitcast.16), calls=%async_computation.2 | async-start | bytes 1966080 | tf_op jit(solution)/shard_map/all_to_all | solution.py:183
  64.1 21.3 %all-to-all-done.2.part_ref = bf16[4,64,1920]{2,1,0:T(8,128)(2,1)S(1)} async-done(((bf16[4,64,1920]{2,1,0:T(8,128)(2,1)}), bf16[4,64,1920]{2,1,0:T(8,128)(2,1)S(1)}, u32[]{:S(2)}, u32[]{:S(2)}) %all-to-all-start.2) | async-done | bytes 983072 | tf_op jit(solution)/shard_map/all_to_all | solution.py:183
  85.6 26.7 %all_gather.6 = bf16[512,960]{1,0:T(8,128)(2,1)S(1)} all-gather(bf16[64,960]{1,0:T(8,128)(2,1)S(1)} %shard_map.96), channel_id=1, replica_groups=mesh['segment'=4,'q'=4,'h'=2,'z'=8,'core'=2] {'q','h'}, dimensions={0}, use_global_device_ids=true | all-gather | bytes 1105920 | tf_op jit(solution)/shard_map/all_gather | solution.py:185
  112.4 2.8 %shard_map.97 = bf16[256,512]{1,0:T(8,128)(2,1)} custom-call(s32[1]{0:T(128)} %bitcast.13.core_ref, bf16[4,2,64,960]{3,2,1,0:T(8,128)(2,1)S(1)} %bitcast.72, bf16[896,512]{1,0:T(8,128)(2,1)S(1)} %bitcast.77, bf16[896,512]{1,0:T(8,128)(2,1)} %collective-permute-done.5.w1), custom_call_target="tpu_custom_call" | custom-call | flops 469762048 | bytes 1835008 | tf_op jit(solution)/shard_map/pallas_call | solution.py:157
  115.2 7.6 %all-to-all-start.3 = ((bf16[8,32,512]{2,1,0:T(8,128)(2,1)}), bf16[8,32,512]{2,1,0:T(8,128)(2,1)S(1)}, u32[]{:S(2)}, u32[]{:S(2)}) async-start(bf16[8,32,512]{2,1,0:T(8,128)(2,1)} %bitcast.21), calls=%async_computation.3 | async-start | bytes 524288 | tf_op jit(solution)/shard_map/all_to_all | solution.py:190
  123.1 10.1 %all-to-all-done.3 = bf16[8,32,512]{2,1,0:T(8,128)(2,1)S(1)} async-done(((bf16[8,32,512]{2,1,0:T(8,128)(2,1)}), bf16[8,32,512]{2,1,0:T(8,128)(2,1)S(1)}, u32[]{:S(2)}, u32[]{:S(2)}) %all-to-all-start.3) | async-done | bytes 262176 | tf_op jit(solution)/shard_map/all_to_all | solution.py:190
  136.3 3.2 %collective-permute-done.6 = bf16[32,512]{1,0:T(8,128)(2,1)S(1)} collective-permute-done((bf16[32,512]{1,0:T(8,128)(2,1)S(1)}, bf16[32,512]{1,0:T(8,128)(2,1)S(1)}, u32[]{:S(2)}, u32[]{:S(2)}) %collective-permute-start.6) | collective-permute-done | bytes 32800 | tf_op jit(solution)/shard_map/ppermute | solution.py:254
  140.4 3.6 %all-to-all-start.4 = ((bf16[16,32,512]{2,1,0:T(8,128)(2,1)}), bf16[16,32,512]{2,1,0:T(8,128)(2,1)S(1)}, u32[]{:S(2)}, u32[]{:S(2)}) async-start(bf16[16,32,512]{2,1,0:T(8,128)(2,1)} %broadcast_in_dim.132), calls=%async_computation.4 | async-start | bytes 1048576 | tf_op jit(solution)/shard_map/all_to_all | solution.py:175
  145.6 4.7 %collective-permute-start.7 = (bf16[128,512]{1,0:T(8,128)(2,1)S(1)}, bf16[128,512]{1,0:T(8,128)(2,1)}, u32[]{:S(2)}, u32[]{:S(2)}) collective-permute-start(bf16[128,512]{1,0:T(8,128)(2,1)S(1)} %pad_maximum_fusion.2), channel_id=1, source_target_pairs={{0,128},{128,256},{256,384},{384,0},{1,129},{129,257},{257,385},{3... | collective-permute-start | bytes 393224 | tf_op jit(solution)/shard_map/ppermute | solution.py:257
  155.5 3.7 %shard_map.98 = bf16[256,1920]{1,0:T(8,128)(2,1)} custom-call(s32[1]{0:T(128)} %bitcast.13.core_ref, bf16[2,8,32,512]{3,2,1,0:T(8,128)(2,1)S(1)} %bitcast.79, f32[2,512]{1,0:T(2,128)S(1)} %pad_maximum_fusion.4.gain_ref, f32[2,512]{1,0:T(2,128)S(1)} %pad_maximum_fusion.5.scorer_ref, bf16[512,896]{1,0:T(8,128)(2,1)S(1)} %collective-permute-done.1.w0, ...), custom_call_target="tpu_custom_call" | custom-call | flops 939524096 | bytes 3670016 | tf_op jit(solution)/shard_map/pallas_call | solution.py:90
  159.3 3.8 %all-to-all-start.5 = ((bf16[4,64,1920]{2,1,0:T(8,128)(2,1)}), bf16[4,64,1920]{2,1,0:T(8,128)(2,1)S(1)}, u32[]{:S(2)}, u32[]{:S(2)}) async-start(bf16[4,64,1920]{2,1,0:T(8,128)(2,1)} %bitcast.28), calls=%async_computation.5 | async-start | bytes 1966080 | tf_op jit(solution)/shard_map/all_to_all | solution.py:183
  163.8 19.5 %all-to-all-done.5.part_ref = bf16[4,64,1920]{2,1,0:T(8,128)(2,1)S(1)} async-done(((bf16[4,64,1920]{2,1,0:T(8,128)(2,1)}), bf16[4,64,1920]{2,1,0:T(8,128)(2,1)S(1)}, u32[]{:S(2)}, u32[]{:S(2)}) %all-to-all-start.5) | async-done | bytes 983072 | tf_op jit(solution)/shard_map/all_to_all | solution.py:183
  183.6 26.6 %all_gather.7 = bf16[512,960]{1,0:T(8,128)(2,1)S(1)} all-gather(bf16[64,960]{1,0:T(8,128)(2,1)S(1)} %shard_map.99), channel_id=1, replica_groups=mesh['segment'=4,'q'=4,'h'=2,'z'=8,'core'=2] {'q','h'}, dimensions={0}, use_global_device_ids=true | all-gather | bytes 1105920 | tf_op jit(solution)/shard_map/all_gather | solution.py:185
  213.0 5.0 %all-to-all-start.6 = ((bf16[8,32,512]{2,1,0:T(8,128)(2,1)}), bf16[8,32,512]{2,1,0:T(8,128)(2,1)S(1)}, u32[]{:S(2)}, u32[]{:S(2)}) async-start(bf16[8,32,512]{2,1,0:T(8,128)(2,1)} %bitcast.32), calls=%async_computation.6 | async-start | bytes 524288 | tf_op jit(solution)/shard_map/all_to_all | solution.py:190
  219.2 9.2 %all-to-all-done.6 = bf16[8,32,512]{2,1,0:T(8,128)(2,1)S(1)} async-done(((bf16[8,32,512]{2,1,0:T(8,128)(2,1)}), bf16[8,32,512]{2,1,0:T(8,128)(2,1)S(1)}, u32[]{:S(2)}, u32[]{:S(2)}) %all-to-all-start.6) | async-done | bytes 262176 | tf_op jit(solution)/shard_map/all_to_all | solution.py:190
  230.1 4.2 %all-to-all-start.7 = ((bf16[8,3,8,512]{3,2,1,0:T(8,128)(2,1)}), bf16[8,3,8,512]{3,2,1,0:T(8,128)(2,1)S(1)}, u32[]{:S(2)}, u32[]{:S(2)}) async-start(bf16[8,3,8,512]{3,2,1,0:T(8,128)(2,1)} %pad_maximum_fusion.1), calls=%async_computation.7 | async-start | bytes 393216 | tf_op jit(solution)/shard_map/all_to_all | solution.py:267
  234.5 9.6 %all-to-all-done.7 = bf16[8,3,8,512]{3,2,1,0:T(8,128)(2,1)S(1)} async-done(((bf16[8,3,8,512]{3,2,1,0:T(8,128)(2,1)}), bf16[8,3,8,512]{3,2,1,0:T(8,128)(2,1)S(1)}, u32[]{:S(2)}, u32[]{:S(2)}) %all-to-all-start.7) | async-done | bytes 196640 | tf_op jit(solution)/shard_map/all_to_all | solution.py:267
  (98 shorter events, 37.8 us)
Async XLA Ops:
  0.6 10.2 %copy-start.5 = (bf16[1,64,4096]{2,1,0:T(8,128)(2,1)S(1)}, bf16[1,64,4096]{2,1,0:T(8,128)(2,1)}, u32[]{:S(2)}) copy-start(bf16[1,64,4096]{2,1,0:T(8,128)(2,1)} %param.8) | copy-start | bytes 1572868
  1.4 9.3 %collective-permute-start = (s32[8]{0:T(128)S(1)}, s32[8]{0:T(128)S(1)}, u32[]{:S(2)}, u32[]{:S(2)}) collective-permute-start(s32[8]{0:T(128)S(1)} %get-tuple-element.28), channel_id=1, source_target_pairs={{0,384},{128,0},{256,128},{384,256},{1,385},{129,1},{257,129},{385... | collective-permute-start | bytes 104 | tf_op jit(solution)/shard_map/ppermute | solution.py:209
  4.1 6.9 %copy-start.7 = (bf16[64,4096]{1,0:T(8,128)(2,1)S(1)}, bf16[64,4096]{1,0:T(8,128)(2,1)}, u32[]{:S(2)}) copy-start(bf16[64,4096]{1,0:T(8,128)(2,1)} %param.9) | copy-start | bytes 1572868
  11.0 5.5 %copy-start.10 = (bf16[1,512,896]{2,1,0:T(8,128)(2,1)S(1)}, bf16[1,512,896]{2,1,0:T(8,128)(2,1)}, u32[]{:S(2)}) copy-start(bf16[1,512,896]{2,1,0:T(8,128)(2,1)} %param.12) | copy-start | bytes 2752516
  12.1 15.3 %all-to-all-start = ((bf16[8,24,640]{2,1,0:T(8,128)(2,1)}), bf16[8,24,640]{2,1,0:T(8,128)(2,1)S(1)}, u32[]{:S(2)}, u32[]{:S(2)}) async-start(bf16[8,24,640]{2,1,0:T(8,128)(2,1)} %pad_maximum_fusion), calls=%async_computation | async-start | bytes 491520 | tf_op jit(solution)/shard_map/all_to_all | solution.py:224
  16.5 22.5 %collective-permute-start.1 = (bf16[512,896]{1,0:T(8,128)(2,1)S(1)}, bf16[512,896]{1,0:T(8,128)(2,1)S(1)}, u32[]{:S(2)}, u32[]{:S(2)}) collective-permute-start(bf16[512,896]{1,0:T(8,128)(2,1)S(1)} %bitcast.91), channel_id=1, source_target_pairs={{0,0},{17,17},{1,16},{16,1},{2,2},{19,19},{3,18},{18,3},{4,4},{21,... | collective-permute-start | bytes 2752520 | tf_op jit(solution)/shard_map/ppermute | solution.py:44
  17.3 23.7 %collective-permute-start.3 = (bf16[512,896]{1,0:T(8,128)(2,1)}, bf16[512,896]{1,0:T(8,128)(2,1)S(1)}, u32[]{:S(2)}, u32[]{:S(2)}) collective-permute-start(bf16[512,896]{1,0:T(8,128)(2,1)} %bitcast.92), channel_id=1, source_target_pairs={{0,0},{17,17},{1,16},{16,1},{2,2},{19,19},{3,18},{18,3},{4,4},{21,... | collective-permute-start | bytes 2752520 | tf_op jit(solution)/shard_map/ppermute | solution.py:44
  28.7 24.8 %all-to-all-start.1 = ((bf16[8,2,32,512]{3,2,1,0:T(8,128)(2,1)}), bf16[8,2,32,512]{3,2,1,0:T(8,128)(2,1)S(1)}, u32[]{:S(2)}, u32[]{:S(2)}) async-start(bf16[8,2,32,512]{3,2,1,0:T(8,128)(2,1)} %broadcast_in_dim.80), calls=%async_computation.1 | async-start | bytes 1048576 | tf_op jit(solution)/shard_map/all_to_all | solution.py:178
  39.0 14.5 %collective-permute-start.2 = (bf16[512,896]{1,0:T(8,128)(2,1)S(1)}, bf16[512,896]{1,0:T(8,128)(2,1)S(1)}, u32[]{:S(2)}, u32[]{:S(2)}) collective-permute-start(bf16[512,896]{1,0:T(8,128)(2,1)S(1)} %collective-permute-done.1.w0), channel_id=1, source_target_pairs={{0,1},{1,0},{2,3},{3,2},{4,5},{5,4},{6,7},{7,6},{8,9},{9,8},{10,11... | collective-permute-start | bytes 2752520 | tf_op jit(solution)/shard_map/ppermute | solution.py:48
  41.0 16.3 %copy-start.1 = (bf16[512,896]{1,0:T(8,128)(2,1)}, bf16[512,896]{1,0:T(8,128)(2,1)S(1)}, u32[]{:S(2)}) copy-start(bf16[512,896]{1,0:T(8,128)(2,1)S(1)} %collective-permute-done.3.w2) | copy-start | bytes 2752516
  41.0 12.5 %collective-permute-start.4 = (bf16[512,896]{1,0:T(8,128)(2,1)S(1)}, bf16[512,896]{1,0:T(8,128)(2,1)}, u32[]{:S(2)}, u32[]{:S(2)}) collective-permute-start(bf16[512,896]{1,0:T(8,128)(2,1)S(1)} %collective-permute-done.3.w2), channel_id=1, source_target_pairs={{0,1},{1,0},{2,3},{3,2},{4,5},{5,4},{6,7},{7,6},{8,9},{9,8},{10,11... | collective-permute-start | bytes 2752520 | tf_op jit(solution)/shard_map/ppermute | solution.py:48
  57.3 28.1 %all-to-all-start.2 = ((bf16[4,64,1920]{2,1,0:T(8,128)(2,1)}), bf16[4,64,1920]{2,1,0:T(8,128)(2,1)S(1)}, u32[]{:S(2)}, u32[]{:S(2)}) async-start(bf16[4,64,1920]{2,1,0:T(8,128)(2,1)} %bitcast.16), calls=%async_computation.2 | async-start | bytes 1966080 | tf_op jit(solution)/shard_map/all_to_all | solution.py:183
  61.6 50.8 %collective-permute-start.5 = (bf16[896,512]{1,0:T(8,128)(2,1)S(1)}, bf16[896,512]{1,0:T(8,128)(2,1)}, u32[]{:S(2)}, u32[]{:S(2)}) collective-permute-start(bf16[896,512]{1,0:T(8,128)(2,1)S(1)} %bitcast.76), channel_id=1, source_target_pairs={{0,1},{1,0},{2,3},{3,2},{4,5},{5,4},{6,7},{7,6},{8,9},{9,8},{10,11... | collective-permute-start | bytes 2752520 | tf_op jit(solution)/shard_map/ppermute | solution.py:48
  115.2 18.0 %all-to-all-start.3 = ((bf16[8,32,512]{2,1,0:T(8,128)(2,1)}), bf16[8,32,512]{2,1,0:T(8,128)(2,1)S(1)}, u32[]{:S(2)}, u32[]{:S(2)}) async-start(bf16[8,32,512]{2,1,0:T(8,128)(2,1)} %bitcast.21), calls=%async_computation.3 | async-start | bytes 524288 | tf_op jit(solution)/shard_map/all_to_all | solution.py:190
  133.6 20.8 %copy-start.2 = (bf16[512,896]{1,0:T(8,128)(2,1)S(1)}, bf16[512,896]{1,0:T(8,128)(2,1)}, u32[]{:S(2)}) copy-start(bf16[512,896]{1,0:T(8,128)(2,1)} %copy-done.1) | copy-start | bytes 2752516
  133.6 5.9 %collective-permute-start.6 = (bf16[32,512]{1,0:T(8,128)(2,1)S(1)}, bf16[32,512]{1,0:T(8,128)(2,1)S(1)}, u32[]{:S(2)}, u32[]{:S(2)}) collective-permute-start(bf16[32,512]{1,0:T(8,128)(2,1)S(1)} %fusion.4), channel_id=1, source_target_pairs={{0,128},{128,256},{256,384},{384,0},{1,129},{129,257},{257,385},{3... | collective-permute-start | bytes 98312 | tf_op jit(solution)/shard_map/ppermute | solution.py:254
  140.4 14.0 %all-to-all-start.4 = ((bf16[16,32,512]{2,1,0:T(8,128)(2,1)}), bf16[16,32,512]{2,1,0:T(8,128)(2,1)S(1)}, u32[]{:S(2)}, u32[]{:S(2)}) async-start(bf16[16,32,512]{2,1,0:T(8,128)(2,1)} %broadcast_in_dim.132), calls=%async_computation.4 | async-start | bytes 1048576 | tf_op jit(solution)/shard_map/all_to_all | solution.py:175
  143.9 15.3 %collective-permute-start.8 = (bf16[64,4096]{1,0:T(8,128)(2,1)}, bf16[64,4096]{1,0:T(8,128)(2,1)}, u32[]{:S(2)}, u32[]{:S(2)}) collective-permute-start(bf16[64,4096]{1,0:T(8,128)(2,1)} %bitcast.80), channel_id=1, source_target_pairs={{0,128},{128,256},{256,384},{1,129},{129,257},{257,385},{2,130},{1... | collective-permute-start | bytes 1572872 | tf_op jit(solution)/shard_map/ppermute | solution.py:245
  145.6 13.7 %collective-permute-start.7 = (bf16[128,512]{1,0:T(8,128)(2,1)S(1)}, bf16[128,512]{1,0:T(8,128)(2,1)}, u32[]{:S(2)}, u32[]{:S(2)}) collective-permute-start(bf16[128,512]{1,0:T(8,128)(2,1)S(1)} %pad_maximum_fusion.2), channel_id=1, source_target_pairs={{0,128},{128,256},{256,384},{384,0},{1,129},{129,257},{257,385},{3... | collective-permute-start | bytes 393224 | tf_op jit(solution)/shard_map/ppermute | solution.py:257
  150.2 9.0 %collective-permute-start.9 = (s32[8]{0:T(128)S(1)}, s32[8]{0:T(128)S(1)}, u32[]{:S(2)}, u32[]{:S(2)}) collective-permute-start(s32[8]{0:T(128)S(1)} %get-tuple-element.26), channel_id=1, source_target_pairs={{0,128},{128,256},{256,384},{384,0},{1,129},{129,257},{257,385},{3... | collective-permute-start | bytes 104 | tf_op jit(solution)/shard_map/ppermute | solution.py:246
  159.3 24.0 %all-to-all-start.5 = ((bf16[4,64,1920]{2,1,0:T(8,128)(2,1)}), bf16[4,64,1920]{2,1,0:T(8,128)(2,1)S(1)}, u32[]{:S(2)}, u32[]{:S(2)}) async-start(bf16[4,64,1920]{2,1,0:T(8,128)(2,1)} %bitcast.28), calls=%async_computation.5 | async-start | bytes 1966080 | tf_op jit(solution)/shard_map/all_to_all | solution.py:183
  213.0 15.5 %all-to-all-start.6 = ((bf16[8,32,512]{2,1,0:T(8,128)(2,1)}), bf16[8,32,512]{2,1,0:T(8,128)(2,1)S(1)}, u32[]{:S(2)}, u32[]{:S(2)}) async-start(bf16[8,32,512]{2,1,0:T(8,128)(2,1)} %bitcast.32), calls=%async_computation.6 | async-start | bytes 524288 | tf_op jit(solution)/shard_map/all_to_all | solution.py:190
  229.4 14.7 %copy-start.6 = (bf16[1,64,4096]{2,1,0:T(8,128)(2,1)S(1)}, bf16[1,64,4096]{2,1,0:T(8,128)(2,1)}, u32[]{:S(2)}) copy-start(bf16[1,64,4096]{2,1,0:T(8,128)(2,1)} %param.8) | copy-start | bytes 1572868
  230.1 14.0 %all-to-all-start.7 = ((bf16[8,3,8,512]{3,2,1,0:T(8,128)(2,1)}), bf16[8,3,8,512]{3,2,1,0:T(8,128)(2,1)S(1)}, u32[]{:S(2)}, u32[]{:S(2)}) async-start(bf16[8,3,8,512]{3,2,1,0:T(8,128)(2,1)} %pad_maximum_fusion.1), calls=%async_computation.7 | async-start | bytes 393216 | tf_op jit(solution)/shard_map/all_to_all | solution.py:267
  (5 other events, 11.0 us)
